TPU v7x, 32 devices: a whole 2x2x4 slice. The times are simulated.
32 devices in a mesh: gx: 2 (over y), yz: 16 (over z, x, core).
Axes of the slice: x: 2, y: 2, z: 4, core: 2. Of those that a mesh axis runs over, the one named last changes fastest.
Arguments:
- old_pos: float32 [3, 8192], P(None, ('gx', 'yz')), may hold values from 0 to 1
- old_species: int32 [8192], P(('gx', 'yz')), may hold values from 0 to 4
- block_dest: int32 [64, 1], P(('gx', 'yz')), may hold values from 0 to 2; in each aligned block of 2 rows (0 to 1, 2 to 3, ...) no two rows name the same one
- block_count: int32 [64], P(('gx', 'yz')), may hold values from 1 to 128
- send_list: int32 [128, 64], P(('gx', 'yz')), may hold values from 0 to 383
- neighbours: int32 [4, 12288], P(None, ('gx', 'yz')), may hold values from 0 to 639
- embed: float32 [5, 128], replicated, may hold values from -6 to 6
- atom_ref: float32 [5], replicated, may hold values from -3 to -0.5
- w_up: float32 [2, 128, 128], replicated, may hold values from -0.5 to 0.5
- gammas: float32 [2, 8], replicated, may hold values from 0.3 to 3
- w_rad: float32 [2, 8, 384], replicated, may hold values from -2 to 2
- w_mix: float32 [2, 128, 128], replicated, may hold values from -0.5 to 0.5
- readout: float32 [2, 128], replicated, may hold values from -0.5 to 0.5
Outputs:
- forces: float32 [3, 12288], P(None, ('gx', 'yz'))
- energy: float32 [], replicated
Inputs may be any that keep to these rules, and one draw needn't show every extreme that they name: `block_dest`: 0 sends a block to the previous index along yz, 1 keeps it, 2 sends it to the next; among the 2 blocks of one brick at most 1 share a destination, and some destination has exactly 1. `send_list`: slots after migration; row f of a brick's four rows lists what it sends to face f of its neighbours (rows 0, 1 to the next and previous index along gx, rows 2, 3 to the next and previous along yz). `neighbours`: an entry below 384 is a slot of the brick; 384 + f * 64 + g is ghost g of face f.
All inputs are finite; a program needn't handle non-finite values.
Results may differ from a plain program's by a relative error of at most 0.0003.
Values sent between devices are 32-bit elements; how exact they have to be, the bound alone decides.
No kernel may reach another device: no remote copies, remote signals or barrier semaphores. Data moves between devices by JAX's collectives and lax.ppermute only.
A program may use at most 64 MiB of HBM per device.

v0:
```python
import math

import jax
import jax.numpy as jnp
from jax import lax
from jax.sharding import PartitionSpec as P

root_three = math.sqrt(3.0)
root_fifteen = math.sqrt(15.0)
root_five_half = 0.5 * math.sqrt(5.0)
root_fifteen_half = 0.5 * math.sqrt(15.0)
degree_of = (0, 1, 1, 1, 2, 2, 2, 2, 2)
highest = lax.Precision.HIGHEST


def from_behind(value, axis, by):
    size = lax.axis_size(axis)
    return lax.ppermute(value, axis, [(i, (i + by) % size) for i in range(size)])


def harmonics(unit_x, unit_y, unit_z):
    square = unit_x * unit_x + unit_y * unit_y + unit_z * unit_z
    return jnp.stack(
        [
            jnp.ones_like(unit_x),
            root_three * unit_x,
            root_three * unit_y,
            root_three * unit_z,
            root_fifteen * unit_x * unit_y,
            root_fifteen * unit_y * unit_z,
            root_five_half * (3.0 * unit_z * unit_z - square),
            root_fifteen * unit_x * unit_z,
            root_fifteen_half * (unit_x * unit_x - unit_y * unit_y),
        ],
        axis=1,
    )


def edge_terms(source_pos, target_pos, source_feat, gammas, w_rad):
    offset = source_pos - target_pos
    length_sq = jnp.sum(offset * offset, axis=0)
    basis = jnp.exp(-gammas[:, None] * length_sq[None, :])
    radial = jnp.einsum("qs,qf->sf", basis, w_rad, precision=highest)
    channels = source_feat.shape[1]
    radial = radial.reshape(-1, 3, channels)[:, jnp.asarray(degree_of, dtype=jnp.int32), :]
    scale = lax.rsqrt(1.0 + length_sq)
    unit = offset * scale[None, :]
    angular = harmonics(unit[0], unit[1], unit[2])
    return radial * angular[:, :, None] * source_feat[:, None, :]


def gather_messages(pos_ext, projected, neighbours, gammas, w_rad):
    slots = neighbours.shape[1]
    target_pos = pos_ext[:, :slots]

    def add_edges(column, total):
        source = neighbours[column]
        return total + edge_terms(pos_ext[:, source], target_pos, projected[source], gammas, w_rad)

    start = jnp.zeros((slots, 9, projected.shape[1]), pos_ext.dtype)
    return lax.fori_loop(0, neighbours.shape[0], add_edges, start)


def update(h_local, summed, live, w_mix, entries):
    averaged = summed / entries
    invariant = (
        averaged[:, 0, :]
        + jnp.sum(averaged[:, 1:4, :] * averaged[:, 1:4, :], axis=1)
        + jnp.sum(averaged[:, 4:, :] * averaged[:, 4:, :], axis=1)
    )
    mixed = jnp.dot(invariant, w_mix, precision=highest)
    return (h_local + jax.nn.silu(mixed)) * live[:, None]


def layer_forward(pos_ext, h_ext, neighbours, live, w_up, gammas, w_rad, w_mix):
    projected = jnp.dot(h_ext, w_up, precision=highest)
    summed = gather_messages(pos_ext, projected, neighbours, gammas, w_rad)
    return update(h_ext[: neighbours.shape[1]], summed, live, w_mix, neighbours.shape[0])


def layer_backward(
    pos_ext, h_ext, neighbours, live, w_up, gammas, w_rad, w_mix, cotangent, need_features
):
    slots = neighbours.shape[1]
    projected = jnp.dot(h_ext, w_up, precision=highest)
    summed = gather_messages(pos_ext, projected, neighbours, gammas, w_rad)

    def finish(h_local, total):
        return update(h_local, total, live, w_mix, neighbours.shape[0])

    _, pull = jax.vjp(finish, h_ext[:slots], summed)
    g_local, g_summed = pull(cotangent)
    target_pos = pos_ext[:, :slots]

    def terms(source_pos, there, source_feat):
        return edge_terms(source_pos, there, source_feat, gammas, w_rad)

    def edge_grads(column, carry):
        g_pos, g_proj = carry
        source = neighbours[column]
        _, pull_edge = jax.vjp(terms, pos_ext[:, source], target_pos, projected[source])
        g_source, g_target, g_feat = pull_edge(g_summed)
        g_pos = g_pos.at[:, source].add(g_source)
        g_pos = g_pos.at[:, :slots].add(g_target)
        if need_features:
            g_proj = g_proj.at[source].add(g_feat)
        return (g_pos, g_proj)

    carry = (jnp.zeros_like(pos_ext), jnp.zeros_like(projected))
    g_pos, g_proj = lax.fori_loop(0, neighbours.shape[0], edge_grads, carry)
    if need_features:
        g_h = jnp.dot(g_proj, w_up.T, precision=highest).at[:slots].add(g_local)
        return (g_pos, g_h)
    return (g_pos, g_local)


def species_onehot(species, width, dtype):
    return (species[:, None] == jnp.arange(width, dtype=jnp.int32)[None, :]).astype(dtype)


def embed_rows(species, live, embed):
    onehot = species_onehot(species, embed.shape[0], embed.dtype)
    return jnp.dot(onehot, embed, precision=highest) * live[:, None]


def base_energy(species, live, atom_ref):
    onehot = species_onehot(species, atom_ref.shape[0], atom_ref.dtype)
    return jnp.dot(onehot, atom_ref, precision=highest) * live


def pack_blocks(old_pos, old_species, dest, count):
    n_blocks = dest.shape[0]
    per_block = old_species.shape[0] // n_blocks
    capacity = n_blocks // 2
    order = jnp.arange(n_blocks, dtype=jnp.int32)
    earlier = (order[:, None] > order[None, :]).astype(jnp.int32)
    same_dest = (dest[:, None] == dest[None, :]).astype(jnp.int32)
    rank = jnp.sum(earlier * same_dest, axis=1)
    select = (
        (dest[None, None, :] == jnp.arange(3, dtype=jnp.int32)[:, None, None])
        & (rank[None, None, :] == jnp.arange(capacity, dtype=jnp.int32)[None, :, None])
    ).astype(jnp.int32)
    blocks_pos = old_pos.reshape(3, n_blocks, per_block)
    packed_pos = jnp.sum(
        select.astype(old_pos.dtype)[:, :, None, :, None] * blocks_pos[None, None, :, :, :], axis=3
    )
    packed_species = jnp.sum(
        select[:, :, :, None] * old_species.reshape(n_blocks, per_block)[None, None, :, :], axis=2
    )
    packed_count = jnp.sum(select * count[None, None, :], axis=2)
    return (packed_pos, packed_species, packed_count)


def ghost_send(members):
    arrived = []
    for shift_by in (1, -1):
        face = 0 if shift_by == 1 else 1
        rows = tuple((item[face] for item in members))
        arrived.append(from_behind(rows, "gx", shift_by))
    for shift_by in (1, -1):
        face = 2 if shift_by == 1 else 3
        rows = tuple((item[face] for item in members))
        arrived.append(from_behind(rows, "yz", shift_by))
    return tuple((jnp.stack([part[member] for part in arrived]) for member in range(len(members))))


def ghost_return(members):
    arrived = []
    for shift_by in (-1, 1):
        face = 0 if shift_by == -1 else 1
        rows = tuple((item[face] for item in members))
        arrived.append(from_behind(rows, "gx", shift_by))
    for shift_by in (-1, 1):
        face = 2 if shift_by == -1 else 3
        rows = tuple((item[face] for item in members))
        arrived.append(from_behind(rows, "yz", shift_by))
    return tuple((jnp.stack([part[member] for part in arrived]) for member in range(len(members))))


def shards(
    old_pos,
    old_species,
    block_dest,
    block_count,
    send_list,
    neighbours,
    embed,
    atom_ref,
    w_up,
    gammas,
    w_rad,
    w_mix,
    readout,
):
    packed_pos, packed_species, packed_count = pack_blocks(
        old_pos, old_species, block_dest[:, 0], block_count
    )
    moved = {}
    for shift_by in (1, -1):
        group = 2 if shift_by == 1 else 0
        moved[group] = from_behind(
            (packed_pos[group], packed_species[group], packed_count[group]), "yz", shift_by
        )
    arrived_pos = jnp.stack([moved[0][0], packed_pos[1], moved[2][0]])
    arrived_species = jnp.stack([moved[0][1], packed_species[1], moved[2][1]])
    arrived_count = jnp.stack([moved[0][2], packed_count[1], moved[2][2]])
    per_block = arrived_species.shape[-1]
    positions = arrived_pos.transpose(2, 0, 1, 3).reshape(3, -1)
    species = arrived_species.reshape(-1)
    live = (
        (jnp.arange(per_block, dtype=jnp.int32)[None, :] < arrived_count.reshape(-1)[:, None])
        .astype(jnp.float32)
        .reshape(-1)
    )
    slots = species.shape[0]
    ghosts_per = send_list.shape[1]
    flat_lists = send_list.reshape(-1)
    h_zero = embed_rows(species, live, embed)
    pos_rows = positions[:, send_list].transpose(1, 0, 2)
    got_ghost_pos, got_rows = ghost_send((pos_rows, h_zero[send_list]))
    ghost_zero = got_rows.reshape(-1, h_zero.shape[1])
    pos_ext = jnp.concatenate([positions, got_ghost_pos.transpose(1, 0, 2).reshape(3, -1)], axis=1)
    h_ext_zero = jnp.concatenate([h_zero, ghost_zero], axis=0)
    h_one = layer_forward(
        pos_ext, h_ext_zero, neighbours, live, w_up[0], gammas[0], w_rad[0], w_mix[0]
    )
    (got_one,) = ghost_send((h_one[send_list],))
    h_ext_one = jnp.concatenate([h_one, got_one.reshape(-1, h_one.shape[1])], axis=0)
    h_two = layer_forward(
        pos_ext, h_ext_one, neighbours, live, w_up[1], gammas[1], w_rad[1], w_mix[1]
    )
    atomic = jnp.dot(h_one, readout[0], precision=highest) + jnp.dot(
        h_two, readout[1], precision=highest
    )
    local_energy = jnp.sum(base_energy(species, live, atom_ref) + live * atomic)
    total, count = lax.psum((local_energy, jnp.sum(live)), ("gx", "yz"))
    energy = total / count
    g_two = live[:, None] * readout[1][None, :]
    g_pos_two, g_h_one = layer_backward(
        pos_ext, h_ext_one, neighbours, live, w_up[1], gammas[1], w_rad[1], w_mix[1], g_two, True
    )
    ghost_grad_h = g_h_one[slots:].reshape(4, ghosts_per, -1)
    ghost_grad_pos = g_pos_two[:, slots:].reshape(3, 4, ghosts_per).transpose(1, 0, 2)
    back_h, back_pos = ghost_return((ghost_grad_h, ghost_grad_pos))
    g_local_one = (
        (g_h_one[:slots] + live[:, None] * readout[0][None, :])
        .at[flat_lists]
        .add(back_h.reshape(-1, back_h.shape[2]))
    )
    g_positions = (
        g_pos_two[:, :slots].at[:, flat_lists].add(back_pos.transpose(1, 0, 2).reshape(3, -1))
    )
    g_pos_one, _ = layer_backward(
        pos_ext,
        h_ext_zero,
        neighbours,
        live,
        w_up[0],
        gammas[0],
        w_rad[0],
        w_mix[0],
        g_local_one,
        False,
    )
    (back_last,) = ghost_return(
        (g_pos_one[:, slots:].reshape(3, 4, ghosts_per).transpose(1, 0, 2),)
    )
    g_positions = (
        (g_positions + g_pos_one[:, :slots])
        .at[:, flat_lists]
        .add(back_last.transpose(1, 0, 2).reshape(3, -1))
    )
    forces = -g_positions
    return (forces, energy)


def solution(mesh):
    return jax.shard_map(
        shards,
        mesh=mesh,
        in_specs=(
            P(None, ("gx", "yz")),
            P(("gx", "yz")),
            P(("gx", "yz"), None),
            P(("gx", "yz")),
            P(("gx", "yz"), None),
            P(None, ("gx", "yz")),
            P(),
            P(),
            P(),
            P(),
            P(),
            P(),
            P(),
        ),
        out_specs=(P(None, ("gx", "yz")), P()),
        check_vma=False,
    )
```

profile of v0, /device:TPU:0, one launch (start us, length us, event | category | flops | bytes accessed | tf_op | source)
XLA Modules:
  0.0 385.2 jit_solution(2473130426955570154)
XLA Ops:
  3.0 5.4 %collective-permute-start.8 = (s32[1]{0:T(128)}, s32[1]{0:T(128)}, u32[]{:S(2)}, u32[]{:S(2)}) collective-permute-start(s32[1]{0:T(128)} %get-tuple-element.1908), channel_id=1, source_target_pairs={{0,15},{1,0},{2,1},{3,2},{4,3},{5,4},{6,5},{7,6},{8,7},{9,8},{10,9... | collective-permute-start | bytes 20 | tf_op jit(solution)/shard_map/ppermute | solution.py:18
  9.8 4.5 %collective-permute-start.6 = (s32[1,128]{1,0:T(1,128)S(1)}, s32[1,128]{1,0:T(1,128)S(1)}, u32[]{:S(2)}, u32[]{:S(2)}) collective-permute-start(s32[1,128]{1,0:T(1,128)S(1)} %get-tuple-element.1899), channel_id=1, source_target_pairs={{0,15},{1,0},{2,1},{3,2},{4,3},{5,4},{6,5},{7,6},{8,7},{9,8},{10,9... | collective-permute-start | bytes 1544 | tf_op jit(solution)/shard_map/ppermute | solution.py:18
  15.1 4.5 %collective-permute-start = (f32[1,3,128]{2,1,0:T(4,128)S(1)}, f32[1,3,128]{2,1,0:T(4,128)S(1)}, u32[]{:S(2)}, u32[]{:S(2)}) collective-permute-start(f32[1,3,128]{2,1,0:T(4,128)S(1)} %get-tuple-element.1896), channel_id=1, source_target_pairs={{0,15},{1,0},{2,1},{3,2},{4,3},{5,4},{6,5},{7,6},{8,7},{9,8},{10,9... | collective-permute-start | bytes 4616 | tf_op jit(solution)/shard_map/ppermute | solution.py:18
  34.2 4.5 %collective-permute-start.5 = (f32[3,64]{1,0:T(4,128)S(1)}, f32[3,64]{1,0:T(4,128)S(1)}, u32[]{:S(2)}, u32[]{:S(2)}) collective-permute-start(f32[3,64]{1,0:T(4,128)S(1)} %get-tuple-element.1885), channel_id=1, source_target_pairs={{0,15},{1,0},{2,1},{3,2},{4,3},{5,4},{6,5},{7,6},{8,7},{9,8},{10,9... | collective-permute-start | bytes 2312 | tf_op jit(solution)/shard_map/ppermute | solution.py:18
  40.3 4.4 %collective-permute-start.13 = (f32[64,128]{1,0:T(8,128)S(1)}, f32[64,128]{1,0:T(8,128)S(1)}, u32[]{:S(2)}, u32[]{:S(2)}) collective-permute-start(f32[64,128]{1,0:T(8,128)S(1)} %get-tuple-element.1881), channel_id=1, source_target_pairs={{0,15},{1,0},{2,1},{3,2},{4,3},{5,4},{6,5},{7,6},{8,7},{9,8},{10,9... | collective-permute-start | bytes 98312 | tf_op jit(solution)/shard_map/ppermute | solution.py:18
  46.8 33.5 %while.103 = (s32[]{:T(128)}, f32[384,9,128]{0,2,1:T(8,128)}, f32[8,1]{0,1:T(1,128)S(1)}, s32[4,384]{1,0:T(4,128)S(1)}, f32[3,640]{0,1:T(8,128)}, /*index=5*/f32...) while((s32[]{:T(128)}, f32[384,9,128]{0,2,1:T(8,128)}, ...), condition=%wide.region_6.0_spmd.clone.clone, body=%wide.region_4.0_spmd.sunk.clone.clone.sunk | while | flops 15944579 | bytes 10563823 | solution.py:61
  59.7 3.1 fusion.221
  68.4 3.1 fusion.221
  77.1 3.1 fusion.221
  87.8 4.4 %collective-permute-start.17 = (f32[64,128]{1,0:T(8,128)S(1)}, f32[64,128]{1,0:T(8,128)S(1)}, u32[]{:S(2)}, u32[]{:S(2)}) collective-permute-start(f32[64,128]{1,0:T(8,128)S(1)} %get-tuple-element.1877), channel_id=1, source_target_pairs={{0,15},{1,0},{2,1},{3,2},{4,3},{5,4},{6,5},{7,6},{8,7},{9,8},{10,9... | collective-permute-start | bytes 98312 | tf_op jit(solution)/shard_map/ppermute | solution.py:18
  94.3 33.6 %while.104 = (s32[]{:T(128)}, f32[384,9,128]{0,2,1:T(8,128)}, f32[8,1]{0,1:T(1,128)S(1)}, s32[4,384]{1,0:T(4,128)S(1)}, f32[3,640]{0,1:T(8,128)}, /*index=5*/f32...) while((s32[]{:T(128)}, f32[384,9,128]{0,2,1:T(8,128)}, ...), condition=%wide.region_11.12_spmd.clone.clone, body=%wide.region_9.11_spmd.sunk.clone.clone.sunk | while | flops 15944579 | bytes 10563823 | solution.py:61
  107.3 3.1 fusion.226
  116.1 3.1 fusion.226
  124.8 3.1 fusion.226
  135.2 99.0 %while.101 = (s32[]{:T(128)}, f32[3,640]{0,1:T(8,128)}, f32[640,128]{1,0:T(8,128)S(1)}, s32[4,384]{1,0:T(4,128)S(1)}, f32[3,640]{0,1:T(8,128)}, /*index=5*/f32[3...) while((s32[]{:T(128)}, f32[3,640]{0,1:T(8,128)}, ...), condition=%wide.region_24.25_spmd.clone, body=%wide.region_14.24_spmd.sunk.clone.sunk | while | flops 31920132 | bytes 20759976 | solution.py:110
  142.9 3.8 fusion.205
  146.8 4.9 %scatter_fusion = f32[384,3,128]{2,0,1:T(8,128)S(1)} fusion(f32[384,3,128]{2,0,1:T(8,128)S(1)} %broadcast.2446, s32[9]{0:T(128)} %copy-done.20, f32[9,384,128]{2,1,0:T(8,128)} %get-tuple-element.2162), kind=kCustom, calls=%fused_computation.15.clone.1 | custom fusion | flops 442368 | bytes 5308452 | tf_op jit(solution)/shard_map/while/body/eval_jaxpr/transpose(jvp())/scatter-add | solution.py:45
  152.7 2.7 scatter_fusion.1
  157.1 2.8 scatter_fusion.2
  167.6 3.8 fusion.205
  171.5 4.9 %scatter_fusion = f32[384,3,128]{2,0,1:T(8,128)S(1)} fusion(f32[384,3,128]{2,0,1:T(8,128)S(1)} %broadcast.2446, s32[9]{0:T(128)} %copy-done.20, f32[9,384,128]{2,1,0:T(8,128)} %get-tuple-element.2162), kind=kCustom, calls=%fused_computation.15.clone.1 | custom fusion | flops 442368 | bytes 5308452 | tf_op jit(solution)/shard_map/while/body/eval_jaxpr/transpose(jvp())/scatter-add | solution.py:45
  177.4 2.7 scatter_fusion.1
  181.8 2.8 scatter_fusion.2
  192.3 3.8 fusion.205
  196.2 4.9 %scatter_fusion = f32[384,3,128]{2,0,1:T(8,128)S(1)} fusion(f32[384,3,128]{2,0,1:T(8,128)S(1)} %broadcast.2446, s32[9]{0:T(128)} %copy-done.20, f32[9,384,128]{2,1,0:T(8,128)} %get-tuple-element.2162), kind=kCustom, calls=%fused_computation.15.clone.1 | custom fusion | flops 442368 | bytes 5308452 | tf_op jit(solution)/shard_map/while/body/eval_jaxpr/transpose(jvp())/scatter-add | solution.py:45
  202.1 2.7 scatter_fusion.1
  206.5 2.8 scatter_fusion.2
  217.0 3.8 fusion.205
  220.9 4.9 %scatter_fusion = f32[384,3,128]{2,0,1:T(8,128)S(1)} fusion(f32[384,3,128]{2,0,1:T(8,128)S(1)} %broadcast.2446, s32[9]{0:T(128)} %copy-done.20, f32[9,384,128]{2,1,0:T(8,128)} %get-tuple-element.2162), kind=kCustom, calls=%fused_computation.15.clone.1 | custom fusion | flops 442368 | bytes 5308452 | tf_op jit(solution)/shard_map/while/body/eval_jaxpr/transpose(jvp())/scatter-add | solution.py:45
  226.8 2.7 scatter_fusion.1
  231.2 2.8 scatter_fusion.2
  240.1 3.6 collective-permute-start.24
  244.4 39.1 %all-reduce.12 = (f32[]{:T(128)}, f32[]{:T(128)}) all-reduce(f32[]{:T(128)} %add_reduce_fusion, f32[]{:T(128)} %convert_reduce_fusion), channel_id=1, replica_groups=mesh['gx'=2,'yz'=16] {'gx','yz'}, use_global_device_ids=true, to_apply=%region_48.49 | all-reduce | flops 2 | bytes 16 | tf_op jit(solution)/shard_map/psum | solution.py:236
  289.3 4.2 %collective-permute-done.21 = f32[64,128]{1,0:T(8,128)S(1)} collective-permute-done((f32[64,128]{1,0:T(8,128)S(1)}, f32[64,128]{1,0:T(8,128)S(1)}, u32[]{:S(2)}, u32[]{:S(2)}) %collective-permute-start.21) | collective-permute-done | bytes 32800 | tf_op jit(solution)/shard_map/ppermute | solution.py:18
  297.6 75.7 %while.102 = (s32[]{:T(128)}, f32[3,640]{0,1:T(8,128)S(1)}, s32[4,384]{1,0:T(4,128)S(1)}, f32[3,640]{0,1:T(8,128)}, f32[3,384]{1,0:T(4,128)S(1)}, /*index=5*/f32...) while((s32[]{:T(128)}, f32[3,640]{0,1:T(8,128)S(1)}, ...), condition=%wide.region_39.40_spmd.clone, body=%wide.region_31.39_spmd.sunk.clone.sunk | while | flops 30593028 | bytes 19575604 | solution.py:110
  302.7 3.6 fusion.214
  306.5 4.7 %scatter_fusion.3 = f32[384,3,128]{2,0,1:T(8,128)S(1)} fusion(f32[384,3,128]{2,0,1:T(8,128)S(1)} %broadcast.2470, s32[9]{0:T(128)S(1)} %get-tuple-element.2380, f32[9,384,128]{2,1,0:T(8,128)} %get-tuple-element.2185), kind=kCustom, calls=%fused_computation.18.clone.1 | custom fusion | flops 442368 | bytes 5308452 | tf_op jit(solution)/shard_map/while/body/eval_jaxpr/transpose(jvp())/scatter-add | solution.py:45
  312.1 2.8 scatter_fusion.4
  321.6 3.6 fusion.214
  325.4 4.7 %scatter_fusion.3 = f32[384,3,128]{2,0,1:T(8,128)S(1)} fusion(f32[384,3,128]{2,0,1:T(8,128)S(1)} %broadcast.2470, s32[9]{0:T(128)S(1)} %get-tuple-element.2380, f32[9,384,128]{2,1,0:T(8,128)} %get-tuple-element.2185), kind=kCustom, calls=%fused_computation.18.clone.1 | custom fusion | flops 442368 | bytes 5308452 | tf_op jit(solution)/shard_map/while/body/eval_jaxpr/transpose(jvp())/scatter-add | solution.py:45
  331.0 2.8 scatter_fusion.4
  340.5 3.6 fusion.214
  344.3 4.7 %scatter_fusion.3 = f32[384,3,128]{2,0,1:T(8,128)S(1)} fusion(f32[384,3,128]{2,0,1:T(8,128)S(1)} %broadcast.2470, s32[9]{0:T(128)S(1)} %get-tuple-element.2380, f32[9,384,128]{2,1,0:T(8,128)} %get-tuple-element.2185), kind=kCustom, calls=%fused_computation.18.clone.1 | custom fusion | flops 442368 | bytes 5308452 | tf_op jit(solution)/shard_map/while/body/eval_jaxpr/transpose(jvp())/scatter-add | solution.py:45
  349.9 2.8 scatter_fusion.4
  359.4 3.6 fusion.214
  363.2 4.7 %scatter_fusion.3 = f32[384,3,128]{2,0,1:T(8,128)S(1)} fusion(f32[384,3,128]{2,0,1:T(8,128)S(1)} %broadcast.2470, s32[9]{0:T(128)S(1)} %get-tuple-element.2380, f32[9,384,128]{2,1,0:T(8,128)} %get-tuple-element.2185), kind=kCustom, calls=%fused_computation.18.clone.1 | custom fusion | flops 442368 | bytes 5308452 | tf_op jit(solution)/shard_map/while/body/eval_jaxpr/transpose(jvp())/scatter-add | solution.py:45
  368.8 2.8 scatter_fusion.4
  378.5 2.7 collective-permute-done.29
  (762 shorter events, 180.3 us)
Async XLA Ops:
  0.6 26.5 %copy-start = (f32[5,128]{1,0:T(8,128)S(1)}, f32[5,128]{1,0:T(8,128)}, u32[]{:S(2)}) copy-start(f32[5,128]{1,0:T(8,128)} %param.43) | copy-start | bytes 7684
  0.6 32.6 %copy-start.47 = (f32[5]{0:T(128)S(1)}, f32[5]{0:T(128)}, u32[]{:S(2)}) copy-start(f32[5]{0:T(128)} %param.44) | copy-start | bytes 64
  0.7 45.7 %copy-start.24 = (f32[2,128,128]{2,1,0:T(8,128)S(1)}, f32[2,128,128]{2,1,0:T(8,128)}, u32[]{:S(2)}) copy-start(f32[2,128,128]{2,1,0:T(8,128)} %param.45) | copy-start | bytes 393220
  3.0 21.5 %collective-permute-start.8 = (s32[1]{0:T(128)}, s32[1]{0:T(128)}, u32[]{:S(2)}, u32[]{:S(2)}) collective-permute-start(s32[1]{0:T(128)} %get-tuple-element.1908), channel_id=1, source_target_pairs={{0,15},{1,0},{2,1},{3,2},{4,3},{5,4},{6,5},{7,6},{8,7},{9,8},{10,9... | collective-permute-start | bytes 20 | tf_op jit(solution)/shard_map/ppermute | solution.py:18
  8.4 16.1 %collective-permute-start.9 = (s32[1]{0:T(128)}, s32[1]{0:T(128)}, u32[]{:S(2)}, u32[]{:S(2)}) collective-permute-start(s32[1]{0:T(128)} %get-tuple-element.1909), channel_id=1, source_target_pairs={{0,1},{1,2},{2,3},{3,4},{4,5},{5,6},{6,7},{7,8},{8,9},{9,10},{10,1... | collective-permute-start | bytes 20 | tf_op jit(solution)/shard_map/ppermute | solution.py:18
  9.8 17.3 %collective-permute-start.6 = (s32[1,128]{1,0:T(1,128)S(1)}, s32[1,128]{1,0:T(1,128)S(1)}, u32[]{:S(2)}, u32[]{:S(2)}) collective-permute-start(s32[1,128]{1,0:T(1,128)S(1)} %get-tuple-element.1899), channel_id=1, source_target_pairs={{0,15},{1,0},{2,1},{3,2},{4,3},{5,4},{6,5},{7,6},{8,7},{9,8},{10,9... | collective-permute-start | bytes 1544 | tf_op jit(solution)/shard_map/ppermute | solution.py:18
  14.3 12.8 %collective-permute-start.7 = (s32[1,128]{1,0:T(1,128)S(1)}, s32[1,128]{1,0:T(1,128)S(1)}, u32[]{:S(2)}, u32[]{:S(2)}) collective-permute-start(s32[1,128]{1,0:T(1,128)S(1)} %get-tuple-element.1900), channel_id=1, source_target_pairs={{0,1},{1,2},{2,3},{3,4},{4,5},{5,6},{6,7},{7,8},{8,9},{9,10},{10,1... | collective-permute-start | bytes 1544 | tf_op jit(solution)/shard_map/ppermute | solution.py:18
  15.1 14.7 %collective-permute-start = (f32[1,3,128]{2,1,0:T(4,128)S(1)}, f32[1,3,128]{2,1,0:T(4,128)S(1)}, u32[]{:S(2)}, u32[]{:S(2)}) collective-permute-start(f32[1,3,128]{2,1,0:T(4,128)S(1)} %get-tuple-element.1896), channel_id=1, source_target_pairs={{0,15},{1,0},{2,1},{3,2},{4,3},{5,4},{6,5},{7,6},{8,7},{9,8},{10,9... | collective-permute-start | bytes 4616 | tf_op jit(solution)/shard_map/ppermute | solution.py:18
  23.9 108.7 %copy-start.44 = (f32[128]{0:T(128)}, f32[128]{0:T(128)S(1)}, u32[]{:S(2)}) copy-start(f32[128]{0:T(128)S(1)} %get-tuple-element.1903) | copy-start | bytes 1540
  24.5 5.7 %collective-permute-start.1 = (f32[1,3,128]{2,1,0:T(4,128)S(1)}, f32[1,3,128]{2,1,0:T(4,128)S(1)}, u32[]{:S(2)}, u32[]{:S(2)}) collective-permute-start(f32[1,3,128]{2,1,0:T(4,128)S(1)} %get-tuple-element.1897), channel_id=1, source_target_pairs={{0,1},{1,2},{2,3},{3,4},{4,5},{5,6},{6,7},{7,8},{8,9},{9,10},{10,1... | collective-permute-start | bytes 4616 | tf_op jit(solution)/shard_map/ppermute | solution.py:18
  26.4 106.2 %copy-start.37 = (f32[384]{0:T(512)}, f32[384]{0:T(512)S(1)}, u32[]{:S(2)}) copy-start(f32[384]{0:T(512)S(1)} %fusion.136) | copy-start | bytes 4612
  27.5 19.3 %copy-start.19 = (s32[9]{0:T(128)S(1)}, s32[9]{0:T(128)}, u32[]{:S(2)}) copy-start(s32[9]{0:T(128)} %constant.1234) | copy-start | bytes 112
  27.5 19.3 %copy-start.27 = (s32[4,384]{1,0:T(4,128)S(1)}, s32[4,384]{1,0:T(4,128)}, u32[]{:S(2)}) copy-start(s32[4,384]{1,0:T(4,128)} %param.42) | copy-start | bytes 18436
  28.2 17.5 %collective-permute-start.10 = (f32[64,128]{1,0:T(8,128)S(1)}, f32[64,128]{1,0:T(8,128)S(1)}, u32[]{:S(2)}, u32[]{:S(2)}) collective-permute-start(f32[64,128]{1,0:T(8,128)S(1)} %get-tuple-element.1878), channel_id=1, source_target_pairs={{0,16},{16,0},{1,17},{17,1},{2,18},{18,2},{3,19},{19,3},{4,20},{20... | collective-permute-start | bytes 98312 | tf_op jit(solution)/shard_map/ppermute | solution.py:18
  31.2 7.6 %collective-permute-start.2 = (f32[3,64]{1,0:T(4,128)S(1)}, f32[3,64]{1,0:T(4,128)S(1)}, u32[]{:S(2)}, u32[]{:S(2)}) collective-permute-start(f32[3,64]{1,0:T(4,128)S(1)} %get-tuple-element.1884), channel_id=1, source_target_pairs={{0,16},{16,0},{1,17},{17,1},{2,18},{18,2},{3,19},{19,3},{4,20},{20... | collective-permute-start | bytes 2312 | tf_op jit(solution)/shard_map/ppermute | solution.py:18
  32.7 7.5 %collective-permute-start.3 = (f32[3,64]{1,0:T(4,128)S(1)}, f32[3,64]{1,0:T(4,128)S(1)}, u32[]{:S(2)}, u32[]{:S(2)}) collective-permute-start(f32[3,64]{1,0:T(4,128)S(1)} %get-tuple-element.1887), channel_id=1, source_target_pairs={{0,16},{16,0},{1,17},{17,1},{2,18},{18,2},{3,19},{19,3},{4,20},{20... | collective-permute-start | bytes 2312 | tf_op jit(solution)/shard_map/ppermute | solution.py:18
  33.2 7.0 %collective-permute-start.4 = (f32[3,64]{1,0:T(4,128)S(1)}, f32[3,64]{1,0:T(4,128)S(1)}, u32[]{:S(2)}, u32[]{:S(2)}) collective-permute-start(f32[3,64]{1,0:T(4,128)S(1)} %get-tuple-element.1886), channel_id=1, source_target_pairs={{0,1},{1,2},{2,3},{3,4},{4,5},{5,6},{6,7},{7,8},{8,9},{9,10},{10,1... | collective-permute-start | bytes 2312 | tf_op jit(solution)/shard_map/ppermute | solution.py:18
  34.2 10.5 %collective-permute-start.5 = (f32[3,64]{1,0:T(4,128)S(1)}, f32[3,64]{1,0:T(4,128)S(1)}, u32[]{:S(2)}, u32[]{:S(2)}) collective-permute-start(f32[3,64]{1,0:T(4,128)S(1)} %get-tuple-element.1885), channel_id=1, source_target_pairs={{0,15},{1,0},{2,1},{3,2},{4,3},{5,4},{6,5},{7,6},{8,7},{9,8},{10,9... | collective-permute-start | bytes 2312 | tf_op jit(solution)/shard_map/ppermute | solution.py:18
  38.7 7.0 %collective-permute-start.11 = (f32[64,128]{1,0:T(8,128)S(1)}, f32[64,128]{1,0:T(8,128)S(1)}, u32[]{:S(2)}, u32[]{:S(2)}) collective-permute-start(f32[64,128]{1,0:T(8,128)S(1)} %get-tuple-element.1880), channel_id=1, source_target_pairs={{0,16},{16,0},{1,17},{17,1},{2,18},{18,2},{3,19},{19,3},{4,20},{20... | collective-permute-start | bytes 98312 | tf_op jit(solution)/shard_map/ppermute | solution.py:18
  40.2 6.0 %collective-permute-start.12 = (f32[64,128]{1,0:T(8,128)S(1)}, f32[64,128]{1,0:T(8,128)S(1)}, u32[]{:S(2)}, u32[]{:S(2)}) collective-permute-start(f32[64,128]{1,0:T(8,128)S(1)} %get-tuple-element.1879), channel_id=1, source_target_pairs={{0,1},{1,2},{2,3},{3,4},{4,5},{5,6},{6,7},{7,8},{8,9},{9,10},{10,1... | collective-permute-start | bytes 98312 | tf_op jit(solution)/shard_map/ppermute | solution.py:18
  40.3 6.0 %collective-permute-start.13 = (f32[64,128]{1,0:T(8,128)S(1)}, f32[64,128]{1,0:T(8,128)S(1)}, u32[]{:S(2)}, u32[]{:S(2)}) collective-permute-start(f32[64,128]{1,0:T(8,128)S(1)} %get-tuple-element.1881), channel_id=1, source_target_pairs={{0,15},{1,0},{2,1},{3,2},{4,3},{5,4},{6,5},{7,6},{8,7},{9,8},{10,9... | collective-permute-start | bytes 98312 | tf_op jit(solution)/shard_map/ppermute | solution.py:18
  82.8 9.4 %copy-start.43 = (f32[2,128]{1,0:T(2,128)S(1)}, f32[2,128]{1,0:T(2,128)}, u32[]{:S(2)}) copy-start(f32[2,128]{1,0:T(2,128)} %param.49) | copy-start | bytes 3076
  83.9 9.9 %copy-start.25 = (f32[2,128,128]{2,1,0:T(8,128)S(1)}, f32[2,128,128]{2,1,0:T(8,128)}, u32[]{:S(2)}) copy-start(f32[2,128,128]{2,1,0:T(8,128)} %param.45) | copy-start | bytes 393220
  85.7 7.5 %collective-permute-start.14 = (f32[64,128]{1,0:T(8,128)S(1)}, f32[64,128]{1,0:T(8,128)S(1)}, u32[]{:S(2)}, u32[]{:S(2)}) collective-permute-start(f32[64,128]{1,0:T(8,128)S(1)} %get-tuple-element.1874), channel_id=1, source_target_pairs={{0,16},{16,0},{1,17},{17,1},{2,18},{18,2},{3,19},{19,3},{4,20},{20... | collective-permute-start | bytes 98312 | tf_op jit(solution)/shard_map/ppermute | solution.py:18
  86.3 6.9 %collective-permute-start.15 = (f32[64,128]{1,0:T(8,128)S(1)}, f32[64,128]{1,0:T(8,128)S(1)}, u32[]{:S(2)}, u32[]{:S(2)}) collective-permute-start(f32[64,128]{1,0:T(8,128)S(1)} %get-tuple-element.1876), channel_id=1, source_target_pairs={{0,16},{16,0},{1,17},{17,1},{2,18},{18,2},{3,19},{19,3},{4,20},{20... | collective-permute-start | bytes 98312 | tf_op jit(solution)/shard_map/ppermute | solution.py:18
  87.8 6.0 %collective-permute-start.16 = (f32[64,128]{1,0:T(8,128)S(1)}, f32[64,128]{1,0:T(8,128)S(1)}, u32[]{:S(2)}, u32[]{:S(2)}) collective-permute-start(f32[64,128]{1,0:T(8,128)S(1)} %get-tuple-element.1875), channel_id=1, source_target_pairs={{0,1},{1,2},{2,3},{3,4},{4,5},{5,6},{6,7},{7,8},{8,9},{9,10},{10,1... | collective-permute-start | bytes 98312 | tf_op jit(solution)/shard_map/ppermute | solution.py:18
  87.8 6.0 %collective-permute-start.17 = (f32[64,128]{1,0:T(8,128)S(1)}, f32[64,128]{1,0:T(8,128)S(1)}, u32[]{:S(2)}, u32[]{:S(2)}) collective-permute-start(f32[64,128]{1,0:T(8,128)S(1)} %get-tuple-element.1877), channel_id=1, source_target_pairs={{0,15},{1,0},{2,1},{3,2},{4,3},{5,4},{6,5},{7,6},{8,7},{9,8},{10,9... | collective-permute-start | bytes 98312 | tf_op jit(solution)/shard_map/ppermute | solution.py:18
  234.2 9.5 %copy-start.40 = (f32[384]{0:T(512)S(1)}, f32[384]{0:T(512)}, u32[]{:S(2)}) copy-start(f32[384]{0:T(512)} %convolution_reduce_fusion.1) | copy-start | bytes 4612
  234.2 9.5 %copy-start.42 = (s32[3]{0:T(128)S(1)}, s32[3]{0:T(128)}, u32[]{:S(2)}) copy-start(s32[3]{0:T(128)} %copy-done.41) | copy-start | bytes 40
  234.2 9.5 %copy-start.45 = (f32[384]{0:T(512)S(1)}, f32[384]{0:T(512)}, u32[]{:S(2)}) copy-start(f32[384]{0:T(512)} %convolution_reduce_fusion.2) | copy-start | bytes 4612
  234.2 9.5 %copy-start.46 = (f32[384]{0:T(512)S(1)}, f32[384]{0:T(512)}, u32[]{:S(2)}) copy-start(f32[384]{0:T(512)} %convolution_reduce_fusion) | copy-start | bytes 4612
  234.2 59.3 %copy-start.39 = (s32[256,1]{0,1:T(1,128)S(1)}, s32[256,1]{0,1:T(1,128)}, u32[]{:S(2)}) copy-start(s32[256,1]{0,1:T(1,128)} %compare_select_fusion.4) | copy-start | bytes 3076
  235.6 53.2 %collective-permute-start.18 = (f32[64,128]{1,0:T(8,128)S(1)}, f32[64,128]{1,0:T(8,128)S(1)}, u32[]{:S(2)}, u32[]{:S(2)}) collective-permute-start(f32[64,128]{1,0:T(8,128)S(1)} %get-tuple-element.1870), channel_id=1, source_target_pairs={{0,16},{16,0},{1,17},{17,1},{2,18},{18,2},{3,19},{19,3},{4,20},{20... | collective-permute-start | bytes 98312 | tf_op jit(solution)/shard_map/ppermute | solution.py:18
  236.1 59.4 %copy-start.26 = (f32[384,128]{1,0:T(8,128)S(1)}, f32[384,128]{1,0:T(8,128)}, u32[]{:S(2)}) copy-start(f32[384,128]{1,0:T(8,128)} %get-tuple-element.1912) | copy-start | bytes 589828
  236.1 59.5 %copy-start.32 = (f32[2,128,128]{2,1,0:T(8,128)S(1)}, f32[2,128,128]{2,1,0:T(8,128)}, u32[]{:S(2)}) copy-start(f32[2,128,128]{2,1,0:T(8,128)} %param.48) | copy-start | bytes 393220
  236.1 59.5 %copy-start.38 = (f32[384]{0:T(512)S(1)}, f32[384]{0:T(512)}, u32[]{:S(2)}) copy-start(f32[384]{0:T(512)} %copy-done.37) | copy-start | bytes 4612
  238.0 46.8 %collective-permute-start.22 = (f32[3,64]{1,0:T(4,128)S(1)}, f32[3,64]{1,0:T(4,128)S(1)}, u32[]{:S(2)}, u32[]{:S(2)}) collective-permute-start(f32[3,64]{1,0:T(4,128)S(1)} %bitcast.626), channel_id=1, source_target_pairs={{0,16},{16,0},{1,17},{17,1},{2,18},{18,2},{3,19},{19,3},{4,20},{20... | collective-permute-start | bytes 2312 | tf_op jit(solution)/shard_map/ppermute | solution.py:18
  239.6 47.8 %collective-permute-start.23 = (f32[3,64]{1,0:T(4,128)S(1)}, f32[3,64]{1,0:T(4,128)S(1)}, u32[]{:S(2)}, u32[]{:S(2)}) collective-permute-start(f32[3,64]{1,0:T(4,128)S(1)} %bitcast.624), channel_id=1, source_target_pairs={{0,16},{16,0},{1,17},{17,1},{2,18},{18,2},{3,19},{19,3},{4,20},{20... | collective-permute-start | bytes 2312 | tf_op jit(solution)/shard_map/ppermute | solution.py:18
  240.1 47.3 %collective-permute-start.24 = (f32[3,64]{1,0:T(4,128)S(1)}, f32[3,64]{1,0:T(4,128)S(1)}, u32[]{:S(2)}, u32[]{:S(2)}) collective-permute-start(f32[3,64]{1,0:T(4,128)S(1)} %bitcast.620), channel_id=1, source_target_pairs={{0,15},{1,0},{2,1},{3,2},{4,3},{5,4},{6,5},{7,6},{8,7},{9,8},{10,9... | collective-permute-start | bytes 2312 | tf_op jit(solution)/shard_map/ppermute | solution.py:18
  244.4 43.5 %collective-permute-start.25 = (f32[3,64]{1,0:T(4,128)S(1)}, f32[3,64]{1,0:T(4,128)S(1)}, u32[]{:S(2)}, u32[]{:S(2)}) collective-permute-start(f32[3,64]{1,0:T(4,128)S(1)} %bitcast.621), channel_id=1, source_target_pairs={{0,1},{1,2},{2,3},{3,4},{4,5},{5,6},{6,7},{7,8},{8,9},{9,10},{10,1... | collective-permute-start | bytes 2312 | tf_op jit(solution)/shard_map/ppermute | solution.py:18
  284.9 4.4 %collective-permute-start.19 = (f32[64,128]{1,0:T(8,128)S(1)}, f32[64,128]{1,0:T(8,128)S(1)}, u32[]{:S(2)}, u32[]{:S(2)}) collective-permute-start(f32[64,128]{1,0:T(8,128)S(1)} %get-tuple-element.1873), channel_id=1, source_target_pairs={{0,16},{16,0},{1,17},{17,1},{2,18},{18,2},{3,19},{19,3},{4,20},{20... | collective-permute-start | bytes 98312 | tf_op jit(solution)/shard_map/ppermute | solution.py:18
  287.4 1.9 collective-permute-start.20
  287.4 6.1 %collective-permute-start.21 = (f32[64,128]{1,0:T(8,128)S(1)}, f32[64,128]{1,0:T(8,128)S(1)}, u32[]{:S(2)}, u32[]{:S(2)}) collective-permute-start(f32[64,128]{1,0:T(8,128)S(1)} %get-tuple-element.1871), channel_id=1, source_target_pairs={{0,1},{1,2},{2,3},{3,4},{4,5},{5,6},{6,7},{7,8},{8,9},{9,10},{10,1... | collective-permute-start | bytes 98312 | tf_op jit(solution)/shard_map/ppermute | solution.py:18
  297.5 78.4 %copy-start.5 = (f32[3,640]{0,1:T(8,128)S(1)}, f32[3,640]{0,1:T(8,128)}, u32[]{:S(2)}) copy-start(f32[3,640]{0,1:T(8,128)} %get-tuple-element.1419) | copy-start | bytes 23044
  373.4 5.0 %collective-permute-start.26 = (f32[3,64]{1,0:T(4,128)S(1)}, f32[3,64]{1,0:T(4,128)S(1)}, u32[]{:S(2)}, u32[]{:S(2)}) collective-permute-start(f32[3,64]{1,0:T(4,128)S(1)} %bitcast.628), channel_id=1, source_target_pairs={{0,16},{16,0},{1,17},{17,1},{2,18},{18,2},{3,19},{19,3},{4,20},{20... | collective-permute-start | bytes 2312 | tf_op jit(solution)/shard_map/ppermute | solution.py:18
  374.6 3.8 collective-permute-start.27
  375.5 3.0 collective-permute-start.28
  375.5 5.7 %collective-permute-start.29 = (f32[3,64]{1,0:T(4,128)S(1)}, f32[3,64]{1,0:T(4,128)S(1)}, u32[]{:S(2)}, u32[]{:S(2)}) collective-permute-start(f32[3,64]{1,0:T(4,128)S(1)} %bitcast.634), channel_id=1, source_target_pairs={{0,1},{1,2},{2,3},{3,4},{4,5},{5,6},{6,7},{7,8},{8,9},{9,10},{10,1... | collective-permute-start | bytes 2312 | tf_op jit(solution)/shard_map/ppermute | solution.py:18
  (93 other events, 256.9 us)
where the time goes:
time: 388 us; the launch traced here: 385 us
  other arithmetic  164 us (42%)
  local copies, waits for them, and re-layouts  96.9 us (25%)
  starting transfers between devices  46.9 us (12%)
  blocking collectives  39.1 us (10%)
  matrix products  21.8 us (6%)
  waiting for transfers between devices  9.12 us (2%)
  loops' own time  3.9 us (1%)
    ppermute x30, starting transfers between devices, from_behind(): lax.ppermute(value, axis, [(i, (i + by) % size) for i in range(size)])  46.9 us
    psum x1, blocking collectives, shards(): total, count = lax.psum((local_energy, jnp.sum(live)), ('gx', 'yz'))  39.1 us
    scatter-add x8, other arithmetic, edge_terms(): radial.reshape(-1, 3, channels)  38.5 us
    reduce_sum x8, other arithmetic, edge_terms(): return radial * angular[:, :, None] * source_feat[:, None, :]  29.6 us
    scatter-add x8, other arithmetic, edge_grads(): g_pos = g_pos.at[:, source].add(g_source)  22 us
    add x8, other arithmetic, add_edges(): total + edge_terms(pos_ext[:, source], target_pos, projected[source], gam...  22 us
    gather x16, local copies, waits for them, and re-layouts, edge_grads(): pos_ext[:, source]  17.4 us
    gather x8, local copies, waits for them, and re-layouts, add_edges(): pos_ext[:, source]  16.7 us
  transfers between devices with their start and end apart: 30, of which 6 were waited for; matrix products, arithmetic and copies ran while one was open for 5% of the time, Pallas kernels for 0%

commit v1 on v0

v1 whole, which is shorter than its diff:
```python
import functools
import math

import jax
import jax.numpy as jnp
from jax import lax
from jax.experimental import pallas as pl
from jax.experimental.pallas import tpu as pltpu
from jax.sharding import PartitionSpec as P

root_three = math.sqrt(3.0)
root_five = math.sqrt(5.0)
root_fifteen = math.sqrt(15.0)
f32 = jnp.float32
bf16 = jnp.bfloat16
ROWS = 8
LANES = 128
VMEM_BYTES = 48 * 1024 * 1024


def split2(value):
    high = value.astype(bf16)
    return high, (value - high.astype(f32)).astype(bf16)


def split3(value):
    high = value.astype(bf16)
    rest = value - high.astype(f32)
    mid = rest.astype(bf16)
    return high, mid, (rest - mid.astype(f32)).astype(bf16)


def dot(left, right, left_dim, right_dim):
    return lax.dot_general(
        left, right, (((left_dim,), (right_dim,)), ((), ())), preferred_element_type=f32
    )


def dot3(left, right, left_dim, right_dim):
    lh, ll = split2(left)
    rh, rl = split2(right)
    return (
        dot(lh, rh, left_dim, right_dim)
        + dot(lh, rl, left_dim, right_dim)
        + dot(ll, rh, left_dim, right_dim)
    )


def pieces(table):
    high = table.astype(bf16).astype(f32)
    rest = table - high
    mid = rest.astype(bf16).astype(f32)
    return jnp.concatenate([high, mid, rest - mid], axis=0).astype(bf16)


def whole(stack):
    return stack[0:ROWS] + stack[ROWS : 2 * ROWS] + stack[2 * ROWS : 3 * ROWS]


def onehot_rows(count, row):
    places = lax.broadcasted_iota(jnp.int32, (count, row.shape[1]), 0)
    return jnp.where(places == row, 1.0, 0.0).astype(bf16)


def column(row):
    n = row.shape[1]
    down = lax.broadcasted_iota(jnp.int32, (n, n), 0)
    across = lax.broadcasted_iota(jnp.int32, (n, n), 1)
    return jnp.sum(jnp.where(down == across, jnp.broadcast_to(row, (n, n)), 0.0), axis=1, keepdims=True)


def left_half(shape):
    return lax.broadcasted_iota(jnp.int32, shape, 1) < shape[1] // 2


def is_even():
    return lax.rem(lax.axis_index("yz"), 2) == 0


def previous_and_next(core, chip):
    even = is_even()
    return jnp.where(even, chip, core), jnp.where(even, core, chip)


def faces_yz(core, chip):
    before, after = previous_and_next(core, chip)
    return jnp.where(left_half(core.shape), before, after)


def returned_yz(core, chip):
    before, after = previous_and_next(core, chip)
    return jnp.where(left_half(core.shape), after, before)


def gamma_column(gammas, layer, count, width):
    which = lax.broadcasted_iota(jnp.int32, (count, width), 0)
    value = jnp.zeros((count, width), f32)
    for q in range(count):
        value = jnp.where(which == q, gammas[layer, q], value)
    return value


def radial_weights(w_rad, layer, entries):
    weights = w_rad[layer] * (1.0 / entries)
    high = weights.astype(bf16).astype(f32)
    low = weights - high
    return jnp.concatenate([high, low, high], axis=0).astype(bf16)


def radial(stacked_weights, basis):
    high = basis.astype(bf16).astype(f32)
    stacked = jnp.concatenate([high, high, basis - high], axis=0).astype(bf16)
    return dot(stacked_weights, stacked, 0, 0)


def geometry(entry, found, table, gamma, weights, u_ref, r_ref, y_ref, rad_ref, slope_ref):
    slots = found.shape[1]
    spread = lambda row: jnp.broadcast_to(row, (ROWS, slots))
    rx, ry, rz = [spread(found[d : d + 1] - table[d : d + 1, 0:slots]) for d in range(3)]
    square = rx * rx + ry * ry + rz * rz
    scale = lax.rsqrt(1.0 + square)
    ux, uy, uz = rx * scale, ry * scale, rz * scale
    basis = jnp.exp(-gamma * square)
    rad_ref[entry] = radial(weights, basis)
    if slope_ref is not None:
        slope_ref[entry] = radial(weights, -gamma * basis)
        r_ref[entry, 0] = rx
        r_ref[entry, 1] = ry
        r_ref[entry, 2] = rz
        r_ref[entry, 3] = scale
        u_ref[entry, 0] = ux
        u_ref[entry, 1] = uy
        u_ref[entry, 2] = uz
    unit_square = ux * ux + uy * uy + uz * uz
    y_ref[entry, 0] = root_three * ux
    y_ref[entry, 1] = root_three * uy
    y_ref[entry, 2] = root_three * uz
    y_ref[entry, 3] = root_fifteen * ux * uy
    y_ref[entry, 4] = root_fifteen * uy * uz
    y_ref[entry, 5] = 0.5 * root_five * (3.0 * uz * uz - unit_square)
    y_ref[entry, 6] = root_fifteen * ux * uz
    y_ref[entry, 7] = 0.5 * root_fifteen * (ux * ux - uy * uy)


def tile(index):
    return pl.ds(pl.multiple_of(index * ROWS, ROWS), ROWS)


def gather_sums(y_ref, rad_ref, feat_ref, sums_ref, invariant_ref):
    entries, channels, slots = feat_ref.shape
    for part in range(slots // LANES):
        lanes = pl.ds(part * LANES, LANES)

        def body(index, carry):
            rows = tile(index)
            sums = [None] * 9
            for k in range(entries):
                feat = feat_ref[k, rows, lanes]
                weighted = [
                    rad_ref[k, pl.ds(pl.multiple_of(degree * channels + index * ROWS, ROWS), ROWS), lanes] * feat
                    for degree in range(3)
                ]
                terms = [weighted[0]]
                for m in range(8):
                    terms.append(y_ref[k, m, :, lanes] * weighted[1 if m < 3 else 2])
                sums = terms if k == 0 else [old + new for old, new in zip(sums, terms)]
            total = sums[0]
            for m in range(8):
                total = total + sums[m + 1] * sums[m + 1]
                if sums_ref is not None:
                    sums_ref[m, rows, lanes] = sums[m + 1]
            invariant_ref[rows, lanes] = total
            return carry

        lax.fori_loop(0, channels // ROWS, body, 0, unroll=2)


def edge_gradients(u_ref, r_ref, rad_ref, slope_ref, feat_ref, sums_ref, g_ref, g_feat_ref, g_off_ref):
    entries, channels, slots = feat_ref.shape
    for part in range(slots // LANES):
        lanes = pl.ds(part * LANES, LANES)
        for k in range(entries):
            ux, uy, uz = [u_ref[k, d, :, lanes] for d in range(3)]

            def body(index, carry):
                rows = tile(index)
                degree_rows = [
                    pl.ds(pl.multiple_of(degree * channels + index * ROWS, ROWS), ROWS) for degree in range(3)
                ]
                g_s, g_x, g_y, g_z = carry
                g = g_ref[rows, lanes]
                feat = feat_ref[k, rows, lanes]
                s = [sums_ref[m, rows, lanes] for m in range(8)]
                b1, b2, b3 = [(2.0 * root_three) * s[m] for m in range(3)]
                c4, c5, c7, c8 = [(2.0 * root_fifteen) * s[m] for m in (3, 4, 6, 7)]
                c6 = (2.0 * root_five) * s[5]
                h_x = uy * c4 + uz * c7 + ux * (c8 - c6)
                h_y = ux * c4 + uz * c5 - uy * (c8 + c6)
                h_z = uy * c5 + ux * c7 + uz * (c6 + c6)
                one = ux * b1 + uy * b2 + uz * b3
                two = 0.5 * (ux * h_x + uy * h_y + uz * h_z)
                r0, r1, r2 = [rad_ref[k, d, lanes] for d in degree_rows]
                d0, d1, d2 = [slope_ref[k, d, lanes] for d in degree_rows]
                if g_feat_ref is not None:
                    g_feat_ref[k, rows, lanes] = g * (r0 + r1 * one + r2 * two)
                q = g * feat
                q1, q2 = q * r1, q * r2
                return (
                    g_s + q * (d0 + d1 * one + d2 * two),
                    g_x + (q1 * b1 + q2 * h_x),
                    g_y + (q1 * b2 + q2 * h_y),
                    g_z + (q1 * b3 + q2 * h_z),
                )

            zero = jnp.zeros((ROWS, LANES), f32)
            found = lax.fori_loop(0, channels // ROWS, body, (zero,) * 4, unroll=4)
            g_s, g_x, g_y, g_z = [jnp.sum(item, axis=0, keepdims=True) for item in found]
            rx, ry, rz, scale = [r_ref[k, d, 0:1, lanes] for d in range(4)]
            along = g_x * rx + g_y * ry + g_z * rz
            radial_part = 2.0 * g_s - scale * scale * scale * along
            g_off_ref[k, 0:1, lanes] = scale * g_x + rx * radial_part
            g_off_ref[k, 1:2, lanes] = scale * g_y + ry * radial_part
            g_off_ref[k, 2:3, lanes] = scale * g_z + rz * radial_part


def silu_and_slope(mixed):
    sigma = 1.0 / (1.0 + jnp.exp(-mixed))
    return mixed * sigma, sigma * (1.0 + mixed * (1.0 - sigma))


def species_features(code, count, weights):
    chosen = onehot_rows(count, code.astype(jnp.int32))
    high, mid, low = split3(weights)
    return dot(high, chosen, 1, 0) + dot(mid, chosen, 1, 0) + dot(low, chosen, 1, 0)


def pad_species(embed_ref, padded_ref):
    padded_ref[...] = jnp.zeros(padded_ref.shape, f32)
    padded_ref[0 : embed_ref.shape[0], :] = embed_ref[...]
    return padded_ref[...]


def pack_kernel(dest, count, pos, species, out):
    blocks, width = species.shape
    place = lax.broadcasted_iota(jnp.int32, (1, width), 1)
    out[...] = jnp.zeros(out.shape, f32)
    for group in range(3):
        coords = jnp.zeros((3, width), f32)
        code = jnp.full((1, width), -1.0, f32)
        for b in range(blocks):
            hit = dest[b, 0] == group
            coords = jnp.where(hit, pos[:, b * width : (b + 1) * width], coords)
            alive = jnp.where(place < count[b], species[b : b + 1, :].astype(f32), -1.0)
            code = jnp.where(hit, alive, code)
        out[group * ROWS : group * ROWS + 3, :] = coords
        out[group * ROWS + 3 : group * ROWS + 4, :] = code


def assemble_kernel(own, core, chip, lists, table, pick_gx, pick_yz):
    before, after = previous_and_next(core[...], chip[...])
    blocks = [after[0:ROWS], own[ROWS : 2 * ROWS, :], before[2 * ROWS : 3 * ROWS]]
    slots = jnp.concatenate(blocks, axis=1)
    table[...] = slots
    parts = pieces(slots)
    for row, out in ((0, pick_gx), (1, pick_yz)):
        out[...] = whole(dot(parts, onehot_rows(slots.shape[1], lists[row : row + 1, :]), 1, 0))


def send_features(h, lists, send_gx, send_yz):
    high, low = split2(h)
    for row, out in ((0, send_gx), (1, send_yz)):
        chosen = onehot_rows(h.shape[1], lists[row : row + 1, :])
        out[...] = dot(high, chosen, 1, 0) + dot(low, chosen, 1, 0)


def first_layer_kernel(
    gammas, table, got_gx, got_core, got_chip, nbr, lists, embed, w_up, w_rad, w_mix,
    ext, h_out, slope_out, send_gx, send_yz,
    padded, y_ref, rad_ref, feat_ref, inv_ref,
):
    slots = table.shape[1]
    entries = nbr.shape[0]
    ext_now = jnp.concatenate(
        [table[...], got_gx[...], faces_yz(got_core[...], got_chip[...])], axis=1
    )
    ext[...] = ext_now
    parts = pieces(ext_now)
    species = pad_species(embed, padded)
    up = dot3(w_up[0], species, 0, 1)
    gamma = gamma_column(gammas, 0, w_rad.shape[1], slots)
    weights = radial_weights(w_rad, 0, entries)
    for k in range(entries):
        found = whole(dot(parts, onehot_rows(ext_now.shape[1], nbr[k : k + 1, :]), 1, 0))
        geometry(k, found, ext_now, gamma, weights, None, None, y_ref, rad_ref, None)
        feat_ref[k] = species_features(found[3:4], ROWS, up)
    gather_sums(y_ref, rad_ref, feat_ref, None, inv_ref)
    mixed = dot3(w_mix[0], inv_ref[...], 0, 0)
    code = ext_now[3:4, 0:slots]
    live = jnp.where(code >= 0.0, 1.0, 0.0)
    h_zero = species_features(code, ROWS, species.T)
    value, slope = silu_and_slope(mixed)
    h_one = live * (h_zero + value)
    h_out[...] = h_one
    slope_out[...] = live * slope
    send_features(h_one, lists, send_gx, send_yz)


def second_layer_kernel(
    gammas, atom_ref, ext, h_one, got_gx, got_core, got_chip, nbr, w_up, w_rad, w_mix, readout,
    g_h, send_gx, send_yz, g_pos, tally,
    onehot, u_ref, r_ref, y_ref, rad_ref, slope_ref, feat_ref, sums_ref, inv_ref, g_ref, g_feat, g_off,
):
    entries, slots = nbr.shape
    ext_now = ext[...]
    wide = ext_now.shape[1]
    h_local = h_one[...]
    channels = h_local.shape[0]
    h_ext = jnp.concatenate(
        [h_local, got_gx[...], faces_yz(got_core[...], got_chip[...])], axis=1
    )
    projected = dot3(w_up[1], h_ext, 0, 0)
    high, low = split2(projected)
    table = jnp.concatenate([high, low], axis=0)
    parts = pieces(ext_now)
    gamma = gamma_column(gammas, 1, w_rad.shape[1], slots)
    weights = radial_weights(w_rad, 1, entries)
    for k in range(entries):
        chosen = onehot_rows(wide, nbr[k : k + 1, :])
        onehot[k] = chosen
        found = whole(dot(parts, chosen, 1, 0))
        geometry(k, found, ext_now, gamma, weights, u_ref, r_ref, y_ref, rad_ref, slope_ref)
        both = dot(table, chosen, 1, 0)
        feat_ref[k] = both[0:channels] + both[channels : 2 * channels]
    gather_sums(y_ref, rad_ref, feat_ref, sums_ref, inv_ref)
    mixed = dot3(w_mix[1], inv_ref[...], 0, 0)
    code = ext_now[3:4, 0:slots]
    live = jnp.where(code >= 0.0, 1.0, 0.0)
    value, slope = silu_and_slope(mixed)
    h_two = live * (h_local + value)
    read_one = column(readout[0:1, :])
    read_two = column(readout[1:2, :])
    energy = jnp.sum(read_one * h_local + read_two * h_two, axis=0, keepdims=True)
    for kind in range(atom_ref.shape[0]):
        energy = energy + jnp.where(code == float(kind), atom_ref[kind], 0.0)
    fold = lambda row: sum(row[:, c : c + LANES] for c in range(0, slots, LANES))
    tally[...] = jnp.zeros(tally.shape, f32)
    tally[0:1, :] = fold(energy)
    tally[1:2, :] = fold(live)
    g_ref[...] = dot3(w_mix[1], (live * read_two) * slope, 1, 0)
    g_off[...] = jnp.zeros(g_off.shape, f32)
    edge_gradients(u_ref, r_ref, rad_ref, slope_ref, feat_ref, sums_ref, g_ref, g_feat, g_off)
    g_proj = jnp.zeros((2 * channels, wide), f32)
    g_ext = jnp.zeros((3 * ROWS, wide), f32)
    own = jnp.zeros((ROWS, slots), f32)
    for k in range(entries):
        chosen = onehot[k]
        high, low = split2(g_feat[k])
        g_proj = g_proj + dot(jnp.concatenate([high, low], axis=0), chosen, 1, 1)
        g_ext = g_ext + dot(pieces(g_off[k]), chosen, 1, 1)
        own = own + g_off[k]
    g_all = dot3(w_up[1], g_proj[0:channels] + g_proj[channels : 2 * channels], 1, 0)
    g_h[...] = g_all[:, 0:slots] + live * (read_one + read_two)
    send_gx[...] = g_all[:, slots : slots + LANES]
    send_yz[...] = g_all[:, slots + LANES : slots + 2 * LANES]
    g_ext = whole(g_ext)
    g_pos[:, 0:slots] = g_ext[:, 0:slots] - own
    g_pos[:, slots:wide] = g_ext[:, slots:wide]


def first_gradient_kernel(
    gammas, ext, g_h, got_gx, got_core, got_chip, slope, g_pos_two, nbr, lists, embed, w_up, w_rad, w_mix,
    g_pos, send_gx, send_yz,
    padded, onehot, u_ref, r_ref, y_ref, rad_ref, slope_ref, feat_ref, sums_ref, inv_ref, g_ref, g_off,
):
    entries, slots = nbr.shape
    ext_now = ext[...]
    wide = ext_now.shape[1]
    parts = pieces(ext_now)
    species = pad_species(embed, padded)
    up = dot3(w_up[0], species, 0, 1)
    gamma = gamma_column(gammas, 0, w_rad.shape[1], slots)
    weights = radial_weights(w_rad, 0, entries)
    for k in range(entries):
        chosen = onehot_rows(wide, nbr[k : k + 1, :])
        onehot[k] = chosen
        found = whole(dot(parts, chosen, 1, 0))
        geometry(k, found, ext_now, gamma, weights, u_ref, r_ref, y_ref, rad_ref, slope_ref)
        feat_ref[k] = species_features(found[3:4], ROWS, up)
    gather_sums(y_ref, rad_ref, feat_ref, sums_ref, inv_ref)
    g_total = g_h[...]
    for row, back in ((0, got_gx[...]), (1, returned_yz(got_core[...], got_chip[...]))):
        chosen = onehot_rows(slots, lists[row : row + 1, :])
        high, low = split2(back)
        g_total = g_total + (dot(high, chosen, 1, 1) + dot(low, chosen, 1, 1))
    g_ref[...] = dot3(w_mix[0], g_total * slope[...], 1, 0)
    g_off[...] = jnp.zeros(g_off.shape, f32)
    edge_gradients(u_ref, r_ref, rad_ref, slope_ref, feat_ref, sums_ref, g_ref, None, g_off)
    g_ext = jnp.zeros((3 * ROWS, wide), f32)
    own = jnp.zeros((ROWS, slots), f32)
    for k in range(entries):
        g_ext = g_ext + dot(pieces(g_off[k]), onehot[k], 1, 1)
        own = own + g_off[k]
    g_ext = whole(g_ext) + g_pos_two[...]
    g_pos[...] = g_ext[:, 0:slots] - own
    send_gx[...] = g_ext[:, slots : slots + LANES]
    send_yz[...] = g_ext[:, slots + LANES : slots + 2 * LANES]


def force_kernel(g_pos, got_gx, got_core, got_chip, lists, forces):
    slots = g_pos.shape[1]
    total = g_pos[...]
    for row, back in ((0, got_gx[...]), (1, returned_yz(got_core[...], got_chip[...]))):
        chosen = onehot_rows(slots, lists[row : row + 1, :])
        total = total + whole(dot(pieces(back), chosen, 1, 1))
    forces[...] = -total[0:3]


def call(kernel, outs, scalars, arrays, scratch=(), name=None):
    in_vmem = pl.BlockSpec(memory_space=pltpu.VMEM)
    in_smem = pl.BlockSpec(memory_space=pltpu.SMEM)
    shapes = [jax.ShapeDtypeStruct(shape, f32) for shape in outs]
    return pl.pallas_call(
        kernel,
        out_shape=shapes,
        in_specs=[in_smem] * len(scalars) + [in_vmem] * len(arrays),
        out_specs=[in_vmem] * len(outs),
        scratch_shapes=[pltpu.VMEM(shape, kind) for shape, kind in scratch],
        compiler_params=pltpu.CompilerParams(vmem_limit_bytes=VMEM_BYTES),
        name=name,
    )(*scalars, *arrays)


def swap_core(value):
    size = lax.axis_size("yz")
    return lax.ppermute(value, "yz", [(i, i ^ 1) for i in range(size)])


def swap_chip(value):
    size = lax.axis_size("yz")
    return lax.ppermute(value, "yz", [(i, (i + 1 if i % 2 else i - 1) % size) for i in range(size)])


def shift(value, axis, by):
    size = lax.axis_size(axis)
    return lax.ppermute(value, axis, [(i, (i + by) % size) for i in range(size)])


def swap_gx(value):
    size = lax.axis_size("gx")
    if size == 2:
        return shift(value, "gx", 1)
    half = value.shape[1] // 2
    return jnp.concatenate(
        [shift(value[:, :half], "gx", 1), shift(value[:, half:], "gx", -1)], axis=1
    )


def return_gx(value):
    size = lax.axis_size("gx")
    if size == 2:
        return shift(value, "gx", 1)
    half = value.shape[1] // 2
    return jnp.concatenate(
        [shift(value[:, :half], "gx", -1), shift(value[:, half:], "gx", 1)], axis=1
    )


def sum_everywhere(value):
    for axis in ("yz", "gx"):
        size = lax.axis_size(axis)
        step = 1
        while step < size:
            value = value + lax.ppermute(value, axis, [(i, i ^ step) for i in range(size)])
            step *= 2
    return value


def shards(
    old_pos,
    old_species,
    block_dest,
    block_count,
    send_list,
    neighbours,
    embed,
    atom_ref,
    w_up,
    gammas,
    w_rad,
    w_mix,
    readout,
):
    entries, slots = neighbours.shape
    blocks = block_dest.shape[0]
    width = old_species.shape[0] // blocks
    channels = w_up.shape[1]
    wide = slots + send_list.size
    lists = send_list.reshape(2, -1)
    species = old_species.reshape(blocks, width)

    (packed,) = call(
        pack_kernel, [(3 * ROWS, width)], [block_dest, block_count], [old_pos, species], name="pack"
    )
    got_chip = swap_chip(packed)
    got_core = swap_core(packed)
    table, pick_gx, pick_yz = call(
        assemble_kernel,
        [(ROWS, slots), (ROWS, LANES), (ROWS, LANES)],
        [],
        [packed, got_core, got_chip, lists],
        name="assemble",
    )
    got_chip = swap_chip(pick_yz)
    got_gx = swap_gx(pick_gx)
    got_core = swap_core(pick_yz)
    rows = w_rad.shape[2]
    edge = ((entries, 8, ROWS, slots), f32)
    rad = ((entries, rows, slots), f32)
    feat = ((entries, channels, slots), f32)
    flat = ((channels, slots), f32)
    sums = ((8, channels, slots), f32)
    u_shape = ((entries, 3, ROWS, slots), f32)
    r_shape = ((entries, 4, ROWS, slots), f32)
    off = ((entries, ROWS, slots), f32)
    chosen = ((entries, wide, slots), bf16)
    padded = ((ROWS, channels), f32)
    square = (channels, LANES)

    ext, h_one, slope, send_gx, send_yz = call(
        first_layer_kernel,
        [(ROWS, wide), (channels, slots), (channels, slots), square, square],
        [gammas],
        [table, got_gx, got_core, got_chip, neighbours, lists, embed, w_up, w_rad, w_mix],
        [padded, edge, rad, feat, flat],
        name="first_layer",
    )
    got_chip = swap_chip(send_yz)
    got_gx = swap_gx(send_gx)
    got_core = swap_core(send_yz)
    g_h, send_gx, send_yz, g_pos_two, tally = call(
        second_layer_kernel,
        [(channels, slots), square, square, (ROWS, wide), (ROWS, LANES)],
        [gammas, atom_ref],
        [ext, h_one, got_gx, got_core, got_chip, neighbours, w_up, w_rad, w_mix, readout],
        [chosen, u_shape, r_shape, edge, rad, rad, feat, sums, flat, flat, feat, off],
        name="second_layer",
    )
    got_chip = swap_chip(send_yz)
    got_gx = return_gx(send_gx)
    got_core = swap_core(send_yz)
    g_pos, send_gx, send_yz = call(
        first_gradient_kernel,
        [(ROWS, slots), (ROWS, LANES), (ROWS, LANES)],
        [gammas],
        [ext, g_h, got_gx, got_core, got_chip, slope, g_pos_two, neighbours, lists, embed, w_up, w_rad, w_mix],
        [padded, chosen, u_shape, r_shape, edge, rad, rad, feat, sums, flat, flat, off],
        name="first_gradient",
    )
    got_chip = swap_chip(send_yz)
    got_gx = return_gx(send_gx)
    got_core = swap_core(send_yz)
    (forces,) = call(
        force_kernel, [(3, slots)], [], [g_pos, got_gx, got_core, got_chip, lists], name="forces"
    )
    tally = sum_everywhere(tally)
    energy = jnp.sum(tally[0]) / jnp.sum(tally[1])
    return (forces, energy)


def solution(mesh):
    return jax.shard_map(
        shards,
        mesh=mesh,
        in_specs=(
            P(None, ("gx", "yz")),
            P(("gx", "yz")),
            P(("gx", "yz"), None),
            P(("gx", "yz")),
            P(("gx", "yz"), None),
            P(None, ("gx", "yz")),
            P(),
            P(),
            P(),
            P(),
            P(),
            P(),
            P(),
        ),
        out_specs=(P(None, ("gx", "yz")), P()),
        check_vma=False,
    )
```

time: 388 us -> 76.7 us (0.20)
  other arithmetic: 164 us -> 0.62 us
  local copies, waits for them, and re-layouts: 96.9 us -> 4.69 us
  blocking collectives: 39.1 us -> 0 us
  starting transfers between devices: 46.9 us -> 22.1 us
  matrix products: 21.8 us -> 0 us
  Pallas kernels: 0 us -> 21.2 us
  waiting for transfers between devices: 9.12 us -> 24.7 us
  loops' own time: 3.9 us -> 0 us
    scatter-add x23 -> x0, other arithmetic: 77.9 us -> none  [the longest x8 38.5 us: edge_terms(): radial.reshape(-1, 3, channels)]
    gather x68 -> x0, local copies, waits for them, and re-layouts: 66 us -> none  [the longest x16 17.4 us: edge_grads(): pos_ext[:, source]]
    psum x1 -> x0, blocking collectives: 39.1 us -> none  [shards(): total, count = lax.psum((local_energy, jnp.sum(live)), ('gx', 'yz'))]
    reduce_sum x42 -> x1, other arithmetic: 35.4 us -> 0.6 us  [shards(): energy = jnp.sum(tally[0]) / jnp.sum(tally[1])]
    ppermute x30 -> x19, starting transfers between devices: 46.9 us -> 22.1 us  [the longest x5 16.2 us: swap_chip(): lax.ppermute(value, 'yz', [(i, (i + 1 if i % 2 else i - 1) % size) for i...]
    add x9 -> x5, other arithmetic: 22.8 us -> 0.02 us  [sum_everywhere(): value + lax.ppermute(value, axis, [(i, i ^ step) for i in range(size)])]
    dot_general x35 -> x0, matrix products: 21.8 us -> none  [the longest x24 14.5 us: edge_terms(): radial = jnp.einsum('qs,qf->sf', basis, w_rad, precision=highest)]
    pallas_call x0 -> x6, Pallas kernels: none -> 21.2 us  [call(): pl.pallas_call(kernel, out_shape=shapes, in_specs=[in_smem] * len(scalars...]
  transfers between devices with their start and end apart: 30 -> 19, of which waited for: 6 -> 11; matrix products, arithmetic and copies ran while one was open for 5% -> 1% of each run, Pallas kernels for 0% -> 0%
where the time goes in v1:
time: 76.7 us; the launch traced here: 76.5 us
  waiting for transfers between devices  24.7 us (32%)
  starting transfers between devices  22.1 us (29%)
  Pallas kernels  21.2 us (28%)
  local copies, waits for them, and re-layouts  4.69 us (6%)
  between operations  3.22 us (4%)
    pallas_call x6, Pallas kernels, call(): pl.pallas_call(kernel, out_shape=shapes, in_specs=[in_smem] * len(scalars...  21.2 us
    ppermute x5, starting transfers between devices, swap_chip(): lax.ppermute(value, 'yz', [(i, (i + 1 if i % 2 else i - 1) % size) for i...  16.2 us
    ppermute x5, waiting for transfers between devices, sum_everywhere(): lax.ppermute(value, axis, [(i, i ^ step) for i in range(size)])  15.6 us
    ppermute x5, waiting for transfers between devices, swap_chip(): lax.ppermute(value, 'yz', [(i, (i + 1 if i % 2 else i - 1) % size) for i...  7.53 us
    ppermute x4, starting transfers between devices, shift(): lax.ppermute(value, axis, [(i, (i + by) % size) for i in range(size)])  4.74 us
    unnamed x29, local copies, waits for them, and re-layouts  4.61 us
  transfers between devices with their start and end apart: 19, of which 11 were waited for; matrix products, arithmetic and copies ran while one was open for 1% of the time, Pallas kernels for 0%

profile of v1, /device:TPU:0, one launch (start us, length us, event | category | flops | bytes accessed | tf_op | source)
XLA Modules:
  0.0 76.5 jit_solution(8117846670420939340)
XLA Ops:
  0.6 0.7 copy.15.dest
  1.4 0.7 copy-done.10
  2.1 0.7 copy-done.8
  2.7 0.6 pack.1.own
  3.3 0.0 copy-start.4
  3.3 5.5 %collective-permute-start.1 = (f32[24,128]{1,0:T(8,128)S(1)}, f32[24,128]{1,0:T(8,128)S(1)}, u32[]{:S(2)}, u32[]{:S(2)}) collective-permute-start(f32[24,128]{1,0:T(8,128)S(1)} %pack.1.own), channel_id=1, source_target_pairs={{0,15},{1,2},{2,1},{3,4},{4,3},{5,6},{6,5},{7,8},{8,7},{9,10},{10,... | collective-permute-start | bytes 36872 | tf_op jit(solution)/shard_map/ppermute | solution.py:440
  8.8 0.0 collective-permute-start
  8.8 0.1 reshape.11.lists
  8.9 1.3 %collective-permute-done.1.chip = f32[24,128]{1,0:T(8,128)S(1)} collective-permute-done((f32[24,128]{1,0:T(8,128)S(1)}, f32[24,128]{1,0:T(8,128)S(1)}, u32[]{:S(2)}, u32[]{:S(2)}) %collective-permute-start.1) | collective-permute-done | bytes 12320 | tf_op jit(solution)/shard_map/ppermute | solution.py:440
  10.2 0.0 collective-permute-done.core
  10.2 0.2 assemble.1
  10.4 0.0 copy-start.6
  10.4 2.0 %collective-permute-start.2 = (f32[8,128]{1,0:T(8,128)S(1)}, f32[8,128]{1,0:T(8,128)S(1)}, u32[]{:S(2)}, u32[]{:S(2)}) collective-permute-start(f32[8,128]{1,0:T(8,128)S(1)} %get-tuple-element.19), channel_id=1, source_target_pairs={{0,16},{16,0},{1,17},{17,1},{2,18},{18,2},{3,19},{19,3},{4,20},{20... | collective-permute-start | bytes 12296 | tf_op jit(solution)/shard_map/ppermute | solution.py:445
  12.4 3.7 %collective-permute-start.4 = (f32[8,128]{1,0:T(8,128)S(1)}, f32[8,128]{1,0:T(8,128)S(1)}, u32[]{:S(2)}, u32[]{:S(2)}) collective-permute-start(f32[8,128]{1,0:T(8,128)S(1)} %get-tuple-element.20), channel_id=1, source_target_pairs={{0,15},{1,2},{2,1},{3,4},{4,3},{5,6},{6,5},{7,8},{8,7},{9,10},{10,... | collective-permute-start | bytes 12296 | tf_op jit(solution)/shard_map/ppermute | solution.py:440
  16.1 0.0 collective-permute-start.3
  16.1 0.0 collective-permute-done.2.got_gx
  16.1 2.0 %collective-permute-done.4.got_chip = f32[8,128]{1,0:T(8,128)S(1)} collective-permute-done((f32[8,128]{1,0:T(8,128)S(1)}, f32[8,128]{1,0:T(8,128)S(1)}, u32[]{:S(2)}, u32[]{:S(2)}) %collective-permute-start.4) | collective-permute-done | bytes 4128 | tf_op jit(solution)/shard_map/ppermute | solution.py:440
  18.1 0.0 collective-permute-done.3.got_core
  18.2 0.0 copy-start
  18.2 0.9 %copy-done = f32[2,128,128]{2,1,0:T(8,128)S(1)} copy-done((f32[2,128,128]{2,1,0:T(8,128)S(1)}, f32[2,128,128]{2,1,0:T(8,128)}, u32[]{:S(2)}) %copy-start) | copy-done | bytes 131096
  19.1 0.9 %copy-done.2 = f32[2,128,128]{2,1,0:T(8,128)S(1)} copy-done((f32[2,128,128]{2,1,0:T(8,128)S(1)}, f32[2,128,128]{2,1,0:T(8,128)}, u32[]{:S(2)}) %copy-start.2) | copy-done | bytes 131096
  20.0 3.7 %first_layer.1 = (f32[8,640]{1,0:T(8,128)S(1)}, f32[128,384]{1,0:T(8,128)S(1)}, f32[128,384]{1,0:T(8,128)S(1)}, f32[128,128]{1,0:T(8,128)S(1)}, f32[128,128]{1,0:T(8,128)S(1)}) custom-call(f32[2,8]{1,0:T(2,128)S(1)} %copy-done.7, f32[8,384]{1,0:T(8,128)S(1)} %get-tuple-element.18.table, f32[8,128]{1,0:T(8,128)S(1)} %collective-permute-done.2.got_gx, ...), custom_call_target="tpu_custom_call" | custom-call | tf_op jit(solution)/shard_map/first_layer/pallas_call | solution.py:422
  23.7 0.2 collective-permute-start.5
  23.8 3.8 %collective-permute-start.7 = (f32[128,128]{1,0:T(8,128)S(1)}, f32[128,128]{1,0:T(8,128)S(1)}, u32[]{:S(2)}, u32[]{:S(2)}) collective-permute-start(f32[128,128]{1,0:T(8,128)S(1)} %get-tuple-element.24), channel_id=1, source_target_pairs={{0,15},{1,2},{2,1},{3,4},{4,3},{5,6},{6,5},{7,8},{8,7},{9,10},{10,... | collective-permute-start | bytes 196616 | tf_op jit(solution)/shard_map/ppermute | solution.py:440
  27.6 0.0 collective-permute-start.6
  27.7 0.3 collective-permute-done.5.got_gx
  28.0 2.2 %collective-permute-done.7.got_chip = f32[128,128]{1,0:T(8,128)S(1)} collective-permute-done((f32[128,128]{1,0:T(8,128)S(1)}, f32[128,128]{1,0:T(8,128)S(1)}, u32[]{:S(2)}, u32[]{:S(2)}) %collective-permute-start.7) | collective-permute-done | bytes 65568 | tf_op jit(solution)/shard_map/ppermute | solution.py:440
  30.2 0.7 copy-done.9
  30.9 9.0 %second_layer.1 = (f32[128,384]{1,0:T(8,128)S(1)}, f32[128,128]{1,0:T(8,128)S(1)}, f32[128,128]{1,0:T(8,128)S(1)}, f32[8,640]{1,0:T(8,128)S(1)}, f32[8,128]{1,0:T(8,128)S(1)}) custom-call(f32[2,8]{1,0:T(2,128)S(1)} %copy-done.7, f32[5]{0:T(128)S(1)} %copy-done.11, f32[8,640]{1,0:T(8,128)S(1)} %get-tuple-element.21.ext, ...), custom_call_target="tpu_custom_call" | custom-call | tf_op jit(solution)/shard_map/second_layer/pallas_call | solution.py:422
  39.9 2.0 %collective-permute-start.8 = (f32[128,128]{1,0:T(8,128)S(1)}, f32[128,128]{1,0:T(8,128)S(1)}, u32[]{:S(2)}, u32[]{:S(2)}) collective-permute-start(f32[128,128]{1,0:T(8,128)S(1)} %get-tuple-element.26), channel_id=1, source_target_pairs={{0,16},{16,0},{1,17},{17,1},{2,18},{18,2},{3,19},{19,3},{4,20},{20... | collective-permute-start | bytes 196616 | tf_op jit(solution)/shard_map/ppermute | solution.py:445
  41.9 3.1 %collective-permute-start.10 = (f32[128,128]{1,0:T(8,128)S(1)}, f32[128,128]{1,0:T(8,128)S(1)}, u32[]{:S(2)}, u32[]{:S(2)}) collective-permute-start(f32[128,128]{1,0:T(8,128)S(1)} %get-tuple-element.27), channel_id=1, source_target_pairs={{0,15},{1,2},{2,1},{3,4},{4,3},{5,6},{6,5},{7,8},{8,7},{9,10},{10,... | collective-permute-start | bytes 196616 | tf_op jit(solution)/shard_map/ppermute | solution.py:440
  45.1 0.5 collective-permute-start.14
  45.6 0.8 %collective-permute-done.14 = f32[8,128]{1,0:T(8,128)S(1)} collective-permute-done((f32[8,128]{1,0:T(8,128)S(1)}, f32[8,128]{1,0:T(8,128)S(1)}, u32[]{:S(2)}, u32[]{:S(2)}) %collective-permute-start.14) | collective-permute-done | bytes 4128 | tf_op jit(solution)/shard_map/ppermute | solution.py:473
  46.4 3.6 %collective-permute-done.15 = f32[8,128]{1,0:T(8,128)S(1)} collective-permute-done((f32[8,128]{1,0:T(8,128)S(1)}, f32[8,128]{1,0:T(8,128)S(1)}, u32[]{:S(2)}, u32[]{:S(2)}) %collective-permute-start.15) | collective-permute-done | bytes 4128 | tf_op jit(solution)/shard_map/ppermute | solution.py:473
  50.0 3.6 %collective-permute-done.16 = f32[8,128]{1,0:T(8,128)S(1)} collective-permute-done((f32[8,128]{1,0:T(8,128)S(1)}, f32[8,128]{1,0:T(8,128)S(1)}, u32[]{:S(2)}, u32[]{:S(2)}) %collective-permute-start.16) | collective-permute-done | bytes 4128 | tf_op jit(solution)/shard_map/ppermute | solution.py:473
  53.6 4.5 %collective-permute-done.17 = f32[8,128]{1,0:T(8,128)S(1)} collective-permute-done((f32[8,128]{1,0:T(8,128)S(1)}, f32[8,128]{1,0:T(8,128)S(1)}, u32[]{:S(2)}, u32[]{:S(2)}) %collective-permute-start.17) | collective-permute-done | bytes 4128 | tf_op jit(solution)/shard_map/ppermute | solution.py:473
  58.1 0.5 collective-permute-start.18
  58.6 3.1 %collective-permute-done.18 = f32[8,128]{1,0:T(8,128)S(1)} collective-permute-done((f32[8,128]{1,0:T(8,128)S(1)}, f32[8,128]{1,0:T(8,128)S(1)}, u32[]{:S(2)}, u32[]{:S(2)}) %collective-permute-start.18) | collective-permute-done | bytes 4128 | tf_op jit(solution)/shard_map/ppermute | solution.py:473
  61.7 0.0 collective-permute-done.9.got_core
  61.8 7.0 %first_gradient.1 = (f32[8,384]{1,0:T(8,128)S(1)}, f32[8,128]{1,0:T(8,128)S(1)}, f32[8,128]{1,0:T(8,128)S(1)}) custom-call(f32[2,8]{1,0:T(2,128)S(1)} %copy-done.7, f32[8,640]{1,0:T(8,128)S(1)} %get-tuple-element.21.ext, f32[128,384]{1,0:T(8,128)S(1)} %get-tuple-element.25.g_h, f32[128,128]{1,0:T(8,128)S(1)} %collective-permute-done.8.got_gx, ...), custom_call_target="tpu_custom_call" | custom-call | tf_op jit(solution)/shard_map/first_gradient/pallas_call | solution.py:422
  68.8 0.1 collective-permute-start.13
  68.8 0.1 collective-permute-start.12
  68.9 0.5 collective-permute-start.11
  69.5 0.6 slice_reduce_fusion
  71.4 1.2 %collective-permute-done.11.got_gx = f32[8,128]{1,0:T(8,128)S(1)} collective-permute-done((f32[8,128]{1,0:T(8,128)S(1)}, f32[8,128]{1,0:T(8,128)S(1)}, u32[]{:S(2)}, u32[]{:S(2)}) %collective-permute-start.11) | collective-permute-done | bytes 4128 | tf_op jit(solution)/shard_map/ppermute | solution.py:445
  72.6 2.0 %collective-permute-done.13.got_chip = f32[8,128]{1,0:T(8,128)S(1)} collective-permute-done((f32[8,128]{1,0:T(8,128)S(1)}, f32[8,128]{1,0:T(8,128)S(1)}, u32[]{:S(2)}, u32[]{:S(2)}) %collective-permute-start.13) | collective-permute-done | bytes 4128 | tf_op jit(solution)/shard_map/ppermute | solution.py:440
  74.5 0.0 collective-permute-done.12.got_core
  74.6 0.8 %forces.1 = f32[3,384]{1,0:T(4,128)} custom-call(f32[8,384]{1,0:T(8,128)S(1)} %get-tuple-element.30.g_pos, f32[8,128]{1,0:T(8,128)S(1)} %collective-permute-done.11.got_gx, f32[8,128]{1,0:T(8,128)S(1)} %collective-permute-done.12.got_core, f32[8,128]{1,0:T(8,128)S(1)} %collective-permute-done.13.got_chip, s32[2,128]{1,0:T(2,128)S(1)} %reshape.11.lists), custom_call_target="tpu_custom_call" | custom-call | tf_op jit(solution)/shard_map/forces/pallas_call | solution.py:422
  (32 shorter events, 0.1 us)
Async XLA Ops:
  1.4 0.7 copy-start.10
  1.4 0.7 copy-start.12
  2.1 0.7 copy-start.8
  2.7 6.1 %copy-start.13 = (s32[4,64]{1,0:T(4,128)S(1)}, s32[4,64]{1,0:T(4,128)}, u32[]{:S(2)}) copy-start(s32[4,64]{1,0:T(4,128)} %param.17) | copy-start | bytes 3076
  3.3 14.8 %copy-start.4 = (f32[2,8,384]{2,1,0:T(8,128)S(1)}, f32[2,8,384]{2,1,0:T(8,128)}, u32[]{:S(2)}) copy-start(f32[2,8,384]{2,1,0:T(8,128)} %w_rad.5) | copy-start | bytes 73732
  3.3 6.9 %collective-permute-start.1 = (f32[24,128]{1,0:T(8,128)S(1)}, f32[24,128]{1,0:T(8,128)S(1)}, u32[]{:S(2)}, u32[]{:S(2)}) collective-permute-start(f32[24,128]{1,0:T(8,128)S(1)} %pack.1.own), channel_id=1, source_target_pairs={{0,15},{1,2},{2,1},{3,4},{4,3},{5,6},{6,5},{7,8},{8,7},{9,10},{10,... | collective-permute-start | bytes 36872 | tf_op jit(solution)/shard_map/ppermute | solution.py:440
  8.8 1.4 %collective-permute-start = (f32[24,128]{1,0:T(8,128)S(1)}, f32[24,128]{1,0:T(8,128)S(1)}, u32[]{:S(2)}, u32[]{:S(2)}) collective-permute-start(f32[24,128]{1,0:T(8,128)S(1)} %pack.1.own), channel_id=1, source_target_pairs={{0,1},{1,0},{2,3},{3,2},{4,5},{5,4},{6,7},{7,6},{8,9},{9,8},{10,11... | collective-permute-start | bytes 36872 | tf_op jit(solution)/shard_map/ppermute | solution.py:435
  10.2 7.9 %copy-start.5 = (s32[4,384]{1,0:T(4,128)S(1)}, s32[4,384]{1,0:T(4,128)}, u32[]{:S(2)}) copy-start(s32[4,384]{1,0:T(4,128)} %nbr.5) | copy-start | bytes 18436
  10.4 7.8 %copy-start.6 = (f32[5,128]{1,0:T(8,128)S(1)}, f32[5,128]{1,0:T(8,128)}, u32[]{:S(2)}) copy-start(f32[5,128]{1,0:T(8,128)} %embed.3) | copy-start | bytes 7684
  10.4 5.7 %collective-permute-start.2 = (f32[8,128]{1,0:T(8,128)S(1)}, f32[8,128]{1,0:T(8,128)S(1)}, u32[]{:S(2)}, u32[]{:S(2)}) collective-permute-start(f32[8,128]{1,0:T(8,128)S(1)} %get-tuple-element.19), channel_id=1, source_target_pairs={{0,16},{16,0},{1,17},{17,1},{2,18},{18,2},{3,19},{19,3},{4,20},{20... | collective-permute-start | bytes 12296 | tf_op jit(solution)/shard_map/ppermute | solution.py:445
  12.4 5.8 %copy-start.7 = (f32[2,8]{1,0:T(2,128)S(1)}, f32[2,8]{1,0:T(2,128)}, u32[]{:S(2)}) copy-start(f32[2,8]{1,0:T(2,128)} %gammas.5) | copy-start | bytes 196
  12.4 5.7 %collective-permute-start.4 = (f32[8,128]{1,0:T(8,128)S(1)}, f32[8,128]{1,0:T(8,128)S(1)}, u32[]{:S(2)}, u32[]{:S(2)}) collective-permute-start(f32[8,128]{1,0:T(8,128)S(1)} %get-tuple-element.20), channel_id=1, source_target_pairs={{0,15},{1,2},{2,1},{3,4},{4,3},{5,6},{6,5},{7,8},{8,7},{9,10},{10,... | collective-permute-start | bytes 12296 | tf_op jit(solution)/shard_map/ppermute | solution.py:440
  16.1 2.0 %collective-permute-start.3 = (f32[8,128]{1,0:T(8,128)S(1)}, f32[8,128]{1,0:T(8,128)S(1)}, u32[]{:S(2)}, u32[]{:S(2)}) collective-permute-start(f32[8,128]{1,0:T(8,128)S(1)} %get-tuple-element.20), channel_id=1, source_target_pairs={{0,1},{1,0},{2,3},{3,2},{4,5},{5,4},{6,7},{7,6},{8,9},{9,8},{10,11... | collective-permute-start | bytes 12296 | tf_op jit(solution)/shard_map/ppermute | solution.py:435
  18.2 0.9 %copy-start = (f32[2,128,128]{2,1,0:T(8,128)S(1)}, f32[2,128,128]{2,1,0:T(8,128)}, u32[]{:S(2)}) copy-start(f32[2,128,128]{2,1,0:T(8,128)} %w_up.5) | copy-start | bytes 393220
  19.1 0.9 %copy-start.2 = (f32[2,128,128]{2,1,0:T(8,128)S(1)}, f32[2,128,128]{2,1,0:T(8,128)}, u32[]{:S(2)}) copy-start(f32[2,128,128]{2,1,0:T(8,128)} %w_mix.5) | copy-start | bytes 393220
  20.0 10.2 %copy-start.1 = (f32[2,128,128]{2,1,0:T(8,128)S(1)}, f32[2,128,128]{2,1,0:T(8,128)}, u32[]{:S(2)}) copy-start(f32[2,128,128]{2,1,0:T(8,128)} %w_up.5) | copy-start | bytes 393220
  20.0 10.2 %copy-start.3 = (f32[2,128,128]{2,1,0:T(8,128)S(1)}, f32[2,128,128]{2,1,0:T(8,128)}, u32[]{:S(2)}) copy-start(f32[2,128,128]{2,1,0:T(8,128)} %w_mix.5) | copy-start | bytes 393220
  23.7 4.3 %collective-permute-start.5 = (f32[128,128]{1,0:T(8,128)S(1)}, f32[128,128]{1,0:T(8,128)S(1)}, u32[]{:S(2)}, u32[]{:S(2)}) collective-permute-start(f32[128,128]{1,0:T(8,128)S(1)} %get-tuple-element.23), channel_id=1, source_target_pairs={{0,16},{16,0},{1,17},{17,1},{2,18},{18,2},{3,19},{19,3},{4,20},{20... | collective-permute-start | bytes 196616 | tf_op jit(solution)/shard_map/ppermute | solution.py:445
  23.8 6.4 %collective-permute-start.7 = (f32[128,128]{1,0:T(8,128)S(1)}, f32[128,128]{1,0:T(8,128)S(1)}, u32[]{:S(2)}, u32[]{:S(2)}) collective-permute-start(f32[128,128]{1,0:T(8,128)S(1)} %get-tuple-element.24), channel_id=1, source_target_pairs={{0,15},{1,2},{2,1},{3,4},{4,3},{5,6},{6,5},{7,8},{8,7},{9,10},{10,... | collective-permute-start | bytes 196616 | tf_op jit(solution)/shard_map/ppermute | solution.py:440
  27.6 2.6 %collective-permute-start.6 = (f32[128,128]{1,0:T(8,128)S(1)}, f32[128,128]{1,0:T(8,128)S(1)}, u32[]{:S(2)}, u32[]{:S(2)}) collective-permute-start(f32[128,128]{1,0:T(8,128)S(1)} %get-tuple-element.24), channel_id=1, source_target_pairs={{0,1},{1,0},{2,3},{3,2},{4,5},{5,4},{6,7},{7,6},{8,9},{9,8},{10,11... | collective-permute-start | bytes 196616 | tf_op jit(solution)/shard_map/ppermute | solution.py:435
  30.2 0.7 copy-start.9
  30.2 0.7 copy-start.11
  39.9 21.8 %collective-permute-start.8 = (f32[128,128]{1,0:T(8,128)S(1)}, f32[128,128]{1,0:T(8,128)S(1)}, u32[]{:S(2)}, u32[]{:S(2)}) collective-permute-start(f32[128,128]{1,0:T(8,128)S(1)} %get-tuple-element.26), channel_id=1, source_target_pairs={{0,16},{16,0},{1,17},{17,1},{2,18},{18,2},{3,19},{19,3},{4,20},{20... | collective-permute-start | bytes 196616 | tf_op jit(solution)/shard_map/ppermute | solution.py:445
  41.9 19.8 %collective-permute-start.10 = (f32[128,128]{1,0:T(8,128)S(1)}, f32[128,128]{1,0:T(8,128)S(1)}, u32[]{:S(2)}, u32[]{:S(2)}) collective-permute-start(f32[128,128]{1,0:T(8,128)S(1)} %get-tuple-element.27), channel_id=1, source_target_pairs={{0,15},{1,2},{2,1},{3,4},{4,3},{5,6},{6,5},{7,8},{8,7},{9,10},{10,... | collective-permute-start | bytes 196616 | tf_op jit(solution)/shard_map/ppermute | solution.py:440
  45.0 16.7 %collective-permute-start.9 = (f32[128,128]{1,0:T(8,128)S(1)}, f32[128,128]{1,0:T(8,128)S(1)}, u32[]{:S(2)}, u32[]{:S(2)}) collective-permute-start(f32[128,128]{1,0:T(8,128)S(1)} %get-tuple-element.27), channel_id=1, source_target_pairs={{0,1},{1,0},{2,3},{3,2},{4,5},{5,4},{6,7},{7,6},{8,9},{9,8},{10,11... | collective-permute-start | bytes 196616 | tf_op jit(solution)/shard_map/ppermute | solution.py:435
  45.1 1.3 %collective-permute-start.14 = (f32[8,128]{1,0:T(8,128)S(1)}, f32[8,128]{1,0:T(8,128)S(1)}, u32[]{:S(2)}, u32[]{:S(2)}) collective-permute-start(f32[8,128]{1,0:T(8,128)S(1)} %get-tuple-element.33), channel_id=1, source_target_pairs={{0,1},{1,0},{2,3},{3,2},{4,5},{5,4},{6,7},{7,6},{8,9},{9,8},{10,11... | collective-permute-start | bytes 12296 | tf_op jit(solution)/shard_map/ppermute | solution.py:473
  46.4 3.6 %collective-permute-start.15 = (f32[8,128]{1,0:T(8,128)S(1)}, f32[8,128]{1,0:T(8,128)S(1)}, u32[]{:S(2)}, u32[]{:S(2)}) collective-permute-start(f32[8,128]{1,0:T(8,128)S(1)} %add.15), channel_id=1, source_target_pairs={{0,2},{1,3},{2,0},{3,1},{4,6},{5,7},{6,4},{7,5},{8,10},{9,11},{10,... | collective-permute-start | bytes 12296 | tf_op jit(solution)/shard_map/ppermute | solution.py:473
  50.0 3.6 %collective-permute-start.16 = (f32[8,128]{1,0:T(8,128)S(1)}, f32[8,128]{1,0:T(8,128)S(1)}, u32[]{:S(2)}, u32[]{:S(2)}) collective-permute-start(f32[8,128]{1,0:T(8,128)S(1)} %add.16), channel_id=1, source_target_pairs={{0,4},{1,5},{2,6},{3,7},{4,0},{5,1},{6,2},{7,3},{8,12},{9,13},{10,... | collective-permute-start | bytes 12296 | tf_op jit(solution)/shard_map/ppermute | solution.py:473
  53.6 4.5 %collective-permute-start.17 = (f32[8,128]{1,0:T(8,128)S(1)}, f32[8,128]{1,0:T(8,128)S(1)}, u32[]{:S(2)}, u32[]{:S(2)}) collective-permute-start(f32[8,128]{1,0:T(8,128)S(1)} %add.17), channel_id=1, source_target_pairs={{0,8},{1,9},{2,10},{3,11},{4,12},{5,13},{6,14},{7,15},{8,0},{9,1},... | collective-permute-start | bytes 12296 | tf_op jit(solution)/shard_map/ppermute | solution.py:473
  58.1 3.6 %collective-permute-start.18 = (f32[8,128]{1,0:T(8,128)S(1)}, f32[8,128]{1,0:T(8,128)S(1)}, u32[]{:S(2)}, u32[]{:S(2)}) collective-permute-start(f32[8,128]{1,0:T(8,128)S(1)} %add.18), channel_id=1, source_target_pairs={{0,16},{16,0},{1,17},{17,1},{2,18},{18,2},{3,19},{19,3},{4,20},{20... | collective-permute-start | bytes 12296 | tf_op jit(solution)/shard_map/ppermute | solution.py:473
  68.8 5.8 %collective-permute-start.13 = (f32[8,128]{1,0:T(8,128)S(1)}, f32[8,128]{1,0:T(8,128)S(1)}, u32[]{:S(2)}, u32[]{:S(2)}) collective-permute-start(f32[8,128]{1,0:T(8,128)S(1)} %get-tuple-element.32), channel_id=1, source_target_pairs={{0,15},{1,2},{2,1},{3,4},{4,3},{5,6},{6,5},{7,8},{8,7},{9,10},{10,... | collective-permute-start | bytes 12296 | tf_op jit(solution)/shard_map/ppermute | solution.py:440
  68.8 5.7 %collective-permute-start.12 = (f32[8,128]{1,0:T(8,128)S(1)}, f32[8,128]{1,0:T(8,128)S(1)}, u32[]{:S(2)}, u32[]{:S(2)}) collective-permute-start(f32[8,128]{1,0:T(8,128)S(1)} %get-tuple-element.32), channel_id=1, source_target_pairs={{0,1},{1,0},{2,3},{3,2},{4,5},{5,4},{6,7},{7,6},{8,9},{9,8},{10,11... | collective-permute-start | bytes 12296 | tf_op jit(solution)/shard_map/ppermute | solution.py:435
  68.9 3.6 %collective-permute-start.11 = (f32[8,128]{1,0:T(8,128)S(1)}, f32[8,128]{1,0:T(8,128)S(1)}, u32[]{:S(2)}, u32[]{:S(2)}) collective-permute-start(f32[8,128]{1,0:T(8,128)S(1)} %get-tuple-element.31), channel_id=1, source_target_pairs={{0,16},{16,0},{1,17},{17,1},{2,18},{18,2},{3,19},{19,3},{4,20},{20... | collective-permute-start | bytes 12296 | tf_op jit(solution)/shard_map/ppermute | solution.py:445

commit v2 on v1

v2 whole, which is shorter than its diff:
```python
import functools
import math

import jax
import jax.numpy as jnp
from jax import lax
from jax.experimental import pallas as pl
from jax.experimental.pallas import tpu as pltpu
from jax.sharding import PartitionSpec as P

root_three = math.sqrt(3.0)
root_five = math.sqrt(5.0)
root_fifteen = math.sqrt(15.0)
f32 = jnp.float32
bf16 = jnp.bfloat16
ROWS = 8
LANES = 128
VMEM_BYTES = 16 * 1024 * 1024


def split2(value):
    high = value.astype(bf16)
    return high, (value - high.astype(f32)).astype(bf16)


def split3(value):
    high = value.astype(bf16)
    rest = value - high.astype(f32)
    mid = rest.astype(bf16)
    return high, mid, (rest - mid.astype(f32)).astype(bf16)


def dot(left, right, left_dim, right_dim):
    return lax.dot_general(
        left, right, (((left_dim,), (right_dim,)), ((), ())), preferred_element_type=f32
    )


def dot3(left, right, left_dim, right_dim):
    lh, ll = split2(left)
    rh, rl = split2(right)
    return (
        dot(lh, rh, left_dim, right_dim)
        + dot(lh, rl, left_dim, right_dim)
        + dot(ll, rh, left_dim, right_dim)
    )


def pieces(table):
    high = table.astype(bf16).astype(f32)
    rest = table - high
    mid = rest.astype(bf16).astype(f32)
    return jnp.concatenate([high, mid, rest - mid], axis=0).astype(bf16)


def pieces_f32(table):
    high = table.astype(bf16).astype(f32)
    rest = table - high
    mid = rest.astype(bf16).astype(f32)
    return jnp.concatenate([high, mid, rest - mid], axis=0)


def whole(stack):
    return stack[0:ROWS] + stack[ROWS : 2 * ROWS] + stack[2 * ROWS : 3 * ROWS]


def onehot_rows(count, row):
    places = lax.broadcasted_iota(jnp.int32, (count, row.shape[1]), 0)
    return jnp.where(places == row, 1.0, 0.0).astype(bf16)


def column(row):
    n = row.shape[1]
    down = lax.broadcasted_iota(jnp.int32, (n, n), 0)
    across = lax.broadcasted_iota(jnp.int32, (n, n), 1)
    return jnp.sum(jnp.where(down == across, jnp.broadcast_to(row, (n, n)), 0.0), axis=1, keepdims=True)


def left_half(shape):
    return lax.broadcasted_iota(jnp.int32, shape, 1) < shape[1] // 2


def is_even():
    return lax.rem(lax.axis_index("yz"), 2) == 0


def previous_and_next(core, chip):
    even = is_even()
    return jnp.where(even, chip, core), jnp.where(even, core, chip)


def faces_yz(core, chip):
    before, after = previous_and_next(core, chip)
    return jnp.where(left_half(core.shape), before, after)


def returned_yz(core, chip):
    before, after = previous_and_next(core, chip)
    return jnp.where(left_half(core.shape), after, before)


def stacked_left(weights):
    high, low = split2(weights)
    return jnp.concatenate([high, high, low], axis=1)


def stacked_right(value):
    high, low = split2(value)
    return jnp.concatenate([high, low, high], axis=0)


def stacked_rows(value):
    high = value.astype(bf16).astype(f32)
    return jnp.concatenate([high, high, value - high], axis=0).astype(bf16)


def stacked_rows_left(value):
    high = value.astype(bf16).astype(f32)
    low = value - high
    return jnp.concatenate([high, low, high], axis=0)


def species_onehot(code, count):
    places = lax.rem(lax.broadcasted_iota(jnp.int32, (3 * count, code.shape[1]), 0), count)
    return jnp.where(places == code.astype(jnp.int32), 1.0, 0.0).astype(bf16)


def matmul(left, right):
    return dot(left, right, 1, 0)


def repeat(row, times):
    return jnp.concatenate([row] * times, axis=1)


def tile(index):
    return pl.ds(pl.multiple_of(index * ROWS, ROWS), ROWS)


def degree_tiles(index, channels):
    return [pl.ds(pl.multiple_of(degree * channels + index * ROWS, ROWS), ROWS) for degree in range(3)]


def lane_parts(slots, entries):
    for part in range(slots // LANES):
        yield pl.ds(part * LANES, LANES), [pl.ds(k * slots + part * LANES, LANES) for k in range(entries)]


U, R, SCALE, SQUARE = 0, 3, 6, 7


def gather_sums(y_ref, rad_ref, feat_ref, fields_ref, invariant_ref):
    channels, slots = invariant_ref.shape
    entries = feat_ref.shape[1] // slots
    for lanes, edges in lane_parts(slots, entries):
        angular = [[y_ref[m, :, edges[k]] for m in range(8)] for k in range(entries)]

        def body(index, carry):
            rows = tile(index)
            degrees = degree_tiles(index, channels)
            sums = None
            for k in range(entries):
                feat = feat_ref[rows, edges[k]]
                weighted = [rad_ref[degree, edges[k]] * feat for degree in degrees]
                terms = [weighted[0]] + [angular[k][m] * weighted[1 if m < 3 else 2] for m in range(8)]
                sums = terms if k == 0 else [old + new for old, new in zip(sums, terms)]
            total = sums[0]
            for item in sums[1:]:
                total = total + item * item
            invariant_ref[rows, lanes] = total
            a1, a2, a3, a4, a5, a6, a7, a8 = sums[1:]
            c6, c8 = (2.0 * root_five) * a6, (2.0 * root_fifteen) * a8
            fields = [(2.0 * root_three) * a for a in (a1, a2, a3)]
            fields += [(2.0 * root_fifteen) * a for a in (a4, a5, a7)]
            fields += [c8 - c6, c8 + c6, c6 + c6]
            for number, field in enumerate(fields):
                fields_ref[number, rows, lanes] = field
            return carry

        lax.fori_loop(0, channels // ROWS, body, 0, unroll=2)


def direction_terms(fields, unit):
    b1, b2, b3, c4, c5, c7, minus, plus, twice = fields
    ux, uy, uz = unit
    h_x = uy * c4 + uz * c7 + ux * minus
    h_y = ux * c4 + uz * c5 - uy * plus
    h_z = uy * c5 + ux * c7 + uz * twice
    one = ux * b1 + uy * b2 + uz * b3
    two = 0.5 * (ux * h_x + uy * h_y + uz * h_z)
    return h_x, h_y, h_z, one, two


def offset_gradients(found, geo_ref, edges):
    g_s, g_x, g_y, g_z = [jnp.sum(item, axis=0, keepdims=True) for item in found]
    rx, ry, rz = [geo_ref[R + d, 0:1, edges] for d in range(3)]
    scale = geo_ref[SCALE, 0:1, edges]
    along = g_x * rx + g_y * ry + g_z * rz
    radial_part = 2.0 * g_s - scale * scale * scale * along
    return scale * g_x + rx * radial_part, scale * g_y + ry * radial_part, scale * g_z + rz * radial_part


def silu_and_slope(mixed):
    sigma = 1.0 / (1.0 + jnp.exp(-mixed))
    return mixed * sigma, sigma * (1.0 + mixed * (1.0 - sigma))


def fetch(pairs, sems):
    copies = [pltpu.make_async_copy(source, target, sems.at[i]) for i, (source, target) in enumerate(pairs)]
    for copy in copies:
        copy.start()
    return copies


def pack_kernel(dest_hbm, count_hbm, pos_hbm, species_hbm, out, dest, count, pos, species, sems):
    copies = fetch(((dest_hbm, dest), (count_hbm, count), (pos_hbm, pos), (species_hbm, species)), sems)
    blocks, width = species.shape
    place = lax.broadcasted_iota(jnp.int32, (1, width), 1)
    out[...] = jnp.zeros(out.shape, f32)
    for copy in copies:
        copy.wait()
    for group in range(3):
        coords = jnp.zeros((3, width), f32)
        code = jnp.full((1, width), -1.0, f32)
        for b in range(blocks):
            hit = dest[0, b] == group
            coords = jnp.where(hit, pos[:, b * width : (b + 1) * width], coords)
            alive = jnp.where(place < count[b], species[b : b + 1, :].astype(f32), -1.0)
            code = jnp.where(hit, alive, code)
        out[group * ROWS : group * ROWS + 3, :] = coords
        out[group * ROWS + 3 : group * ROWS + 4, :] = code


def prepare_kernel(
    gammas_hbm, nbr_hbm, lists_hbm, embed_hbm, w_up_hbm, w_rad_hbm, w_mix_hbm, readout_hbm,
    onehot, send, gamma, radials, species_up, species_in, weights, reads, onehot_t, send_t,
    gammas, nbr, lists, embed, w_up, w_rad, w_mix, readout, padded, sems,
):
    copies = fetch(
        (
            (nbr_hbm, nbr),
            (lists_hbm, lists),
            (gammas_hbm, gammas),
            (w_rad_hbm, w_rad),
            (embed_hbm, embed),
            (w_up_hbm, w_up),
            (w_mix_hbm, w_mix),
            (readout_hbm, readout),
        ),
        sems,
    )
    entries, slots = nbr.shape
    for copy in copies:
        copy.wait()
    wide = onehot.shape[0]
    for k in range(entries):
        onehot[:, k * slots : (k + 1) * slots] = onehot_rows(wide, nbr[k : k + 1, :])
    faces, ghosts = lists.shape
    for face in range(faces):
        send[:, face * ghosts : (face + 1) * ghosts] = onehot_rows(slots, lists[face : face + 1, :])
    count = w_rad.shape[1]
    which = lax.broadcasted_iota(jnp.int32, gamma.shape[1:], 0)
    for layer in range(2):
        value = jnp.zeros(which.shape, f32)
        for q in range(count):
            value = jnp.where(which == q, gammas[layer, q], value)
        gamma[layer] = value
        radials[layer] = stacked_rows_left(w_rad[layer] * (1.0 / entries)).T.astype(bf16)
    padded[...] = jnp.zeros(padded.shape, f32)
    padded[0 : embed.shape[0], :] = embed[...]
    species = padded[...]
    species_up[...] = pieces_f32(dot3(species, w_up[0], 1, 0)).T.astype(bf16)
    species_in[...] = pieces_f32(species).T.astype(bf16)
    for number, item in enumerate(
        (w_mix[0].T, w_up[1].T, w_mix[1].T, w_mix[1], w_up[1], w_mix[0])
    ):
        weights[number] = stacked_left(item)
    for layer in range(2):
        reads[layer] = jnp.broadcast_to(column(readout[layer : layer + 1, :]), reads.shape[1:])
    index_rows = jnp.concatenate([nbr[...].astype(f32), jnp.zeros((ROWS - entries, slots), f32)], axis=0)
    index_columns = index_rows.T
    across = lax.broadcasted_iota(jnp.int32, (slots, wide), 1).astype(f32)
    for k in range(entries):
        onehot_t[k * slots : (k + 1) * slots, :] = jnp.where(
            across == index_columns[:, k : k + 1], 1.0, 0.0
        ).astype(bf16)
    list_rows = jnp.concatenate([lists[...].astype(f32), jnp.zeros((ROWS - faces, ghosts), f32)], axis=0)
    list_columns = list_rows.T
    across = lax.broadcasted_iota(jnp.int32, (ghosts, slots), 1).astype(f32)
    for face in range(faces):
        send_t[face * ghosts : (face + 1) * ghosts, :] = jnp.where(
            across == list_columns[:, face : face + 1], 1.0, 0.0
        ).astype(bf16)


def assemble_kernel(own, core, chip, send, table, pick_gx, pick_yz):
    before, after = previous_and_next(core[...], chip[...])
    blocks = [after[0:ROWS], own[ROWS : 2 * ROWS, :], before[2 * ROWS : 3 * ROWS]]
    slots = jnp.concatenate(blocks, axis=1)
    table[...] = slots
    picked = whole(matmul(pieces(slots), send[...]))
    pick_gx[...] = picked[:, 0:LANES]
    pick_yz[...] = picked[:, LANES : 2 * LANES]


def first_layer_kernel(
    table, got_gx, got_core, got_chip, onehot, send, gamma, radials, species_up, species_in, weights,
    h_out, slope_out, send_gx, send_yz, geo, y_ref, rad_ref, feat_ref, fields_ref,
    inv_ref,
):
    slots = table.shape[1]
    edges = onehot.shape[1]
    entries = edges // slots
    ext = jnp.concatenate([table[...], got_gx[...], faces_yz(got_core[...], got_chip[...])], axis=1)
    found = whole(matmul(pieces(ext), onehot[...]))
    feat_ref[...] = matmul(species_up[...], species_onehot(found[3:4], ROWS))
    spread = lambda row: jnp.broadcast_to(row, (ROWS, edges))
    rx, ry, rz = [
        spread(found[d : d + 1] - repeat(ext[d : d + 1, 0:slots], entries)) for d in range(3)
    ]
    square = rx * rx + ry * ry + rz * rz
    basis = jnp.exp(-gamma[0] * square)
    rad_ref[...] = matmul(radials[0], stacked_rows(basis))
    scale = lax.rsqrt(1.0 + square)
    ux, uy, uz = rx * scale, ry * scale, rz * scale
    for number, item in enumerate((ux, uy, uz, rx, ry, rz, scale, square)):
        geo[number] = item
    unit_square = ux * ux + uy * uy + uz * uz
    y_ref[0] = root_three * ux
    y_ref[1] = root_three * uy
    y_ref[2] = root_three * uz
    y_ref[3] = root_fifteen * ux * uy
    y_ref[4] = root_fifteen * uy * uz
    y_ref[5] = 0.5 * root_five * (3.0 * uz * uz - unit_square)
    y_ref[6] = root_fifteen * ux * uz
    y_ref[7] = 0.5 * root_fifteen * (ux * ux - uy * uy)
    gather_sums(y_ref, rad_ref, feat_ref, fields_ref, inv_ref)
    mixed = matmul(weights[0], stacked_right(inv_ref[...]))
    code = ext[3:4, 0:slots]
    live = jnp.where(code >= 0.0, 1.0, 0.0)
    h_zero = matmul(species_in[...], species_onehot(code, ROWS))
    value, slope = silu_and_slope(mixed)
    h_one = live * (h_zero + value)
    h_out[...] = h_one
    slope_out[...] = live * slope
    channels = h_one.shape[0]
    picked = matmul(jnp.concatenate(split2(h_one), axis=0), send[...])
    picked = picked[0:channels] + picked[channels : 2 * channels]
    send_gx[...] = picked[:, 0:LANES]
    send_yz[...] = picked[:, LANES : 2 * LANES]


def factor_kernel(
    atom_ref, geo, gamma, radials, table, rad_ref, feat_ref, fields_ref,
    factors, rad_two, slope_two, base,
    slope_ref,
):
    square = geo[SQUARE]
    basis = jnp.exp(-gamma[1] * square)
    rad_two[...] = matmul(radials[1], stacked_rows(basis))
    slope_two[...] = matmul(radials[1], stacked_rows(-gamma[1] * basis))
    slope_ref[...] = matmul(radials[0], stacked_rows(-gamma[0] * jnp.exp(-gamma[0] * square)))
    code = table[3:4, :]
    live = jnp.where(code >= 0.0, 1.0, 0.0)
    energy = jnp.zeros(code.shape, f32)
    for kind in range(atom_ref.shape[0]):
        energy = energy + jnp.where(code == float(kind), atom_ref[kind], 0.0)
    fold = lambda row: sum(row[:, c : c + LANES] for c in range(0, code.shape[1], LANES))
    base[...] = jnp.zeros(base.shape, f32)
    base[0:1, :] = fold(energy)
    base[1:2, :] = fold(live)
    channels, slots = fields_ref.shape[1:]
    entries = feat_ref.shape[1] // slots
    for lanes, edges in lane_parts(slots, entries):
        units = [[geo[U + d, :, edges[k]] for d in range(3)] for k in range(entries)]

        def body(index, carry):
            rows = tile(index)
            degrees = degree_tiles(index, channels)
            fields = [fields_ref[m, rows, lanes] for m in range(9)]
            for k in range(entries):
                h_x, h_y, h_z, one, two = direction_terms(fields, units[k])
                feat = feat_ref[rows, edges[k]]
                r1, r2 = [rad_ref[d, edges[k]] * feat for d in degrees[1:]]
                d0, d1, d2 = [slope_ref[d, edges[k]] for d in degrees]
                factors[0, rows, edges[k]] = feat * (d0 + d1 * one + d2 * two)
                factors[1, rows, edges[k]] = r1 * fields[0] + r2 * h_x
                factors[2, rows, edges[k]] = r1 * fields[1] + r2 * h_y
                factors[3, rows, edges[k]] = r1 * fields[2] + r2 * h_z
            return carry

        lax.fori_loop(0, channels // ROWS, body, 0)


def second_layer_kernel(
    base, table, h_one, got_gx, got_core, got_chip, onehot, y_ref, rad_ref, weights, reads,
    feat_ref, fields_ref, g_ref, g_own, tally,
    inv_ref,
):
    slots = table.shape[1]
    h_local = h_one[...]
    channels = h_local.shape[0]
    h_ext = jnp.concatenate([h_local, got_gx[...], faces_yz(got_core[...], got_chip[...])], axis=1)
    projected = matmul(weights[1], stacked_right(h_ext))
    both = matmul(jnp.concatenate(split2(projected), axis=0), onehot[...])
    feat_ref[...] = both[0:channels] + both[channels : 2 * channels]
    gather_sums(y_ref, rad_ref, feat_ref, fields_ref, inv_ref)
    mixed = matmul(weights[2], stacked_right(inv_ref[...]))
    live = jnp.where(table[3:4, :] >= 0.0, 1.0, 0.0)
    value, slope = silu_and_slope(mixed)
    h_two = live * (h_local + value)
    energy = jnp.sum(reads[0] * h_local + reads[1] * h_two, axis=0, keepdims=True)
    tally[...] = base[...]
    tally[0:1, :] += sum(energy[:, c : c + LANES] for c in range(0, slots, LANES))
    g_ref[...] = matmul(weights[3], stacked_right((live * reads[1]) * slope))
    g_own[...] = live * (reads[0] + reads[1])


def second_gradient_kernel(
    geo, rad_ref, slope_ref, feat_ref, fields_ref, g_ref, g_own, onehot_t, weights,
    g_h, send_gx, send_yz, g_pos,
    g_feat, g_off,
):
    channels, slots = g_ref.shape
    wide = onehot_t.shape[1]
    edge_count = feat_ref.shape[1]
    entries = edge_count // slots
    g_off[...] = jnp.zeros(g_off.shape, f32)
    for lanes, edges in lane_parts(slots, entries):
        units = [[geo[U + d, :, edges[k]] for d in range(3)] for k in range(entries)]

        def body(index, carry):
            rows = tile(index)
            degrees = degree_tiles(index, channels)
            g = g_ref[rows, lanes]
            fields = [g * fields_ref[m, rows, lanes] for m in range(9)]
            found = []
            for k in range(entries):
                h_x, h_y, h_z, one, two = direction_terms(fields, units[k])
                feat = feat_ref[rows, edges[k]]
                r0, r1, r2 = [rad_ref[d, edges[k]] for d in degrees]
                d0, d1, d2 = [slope_ref[d, edges[k]] for d in degrees]
                g_feat[rows, edges[k]] = g * r0 + r1 * one + r2 * two
                q1, q2 = feat * r1, feat * r2
                found += [
                    carry[4 * k] + feat * (g * d0 + d1 * one + d2 * two),
                    carry[4 * k + 1] + (q1 * fields[0] + q2 * h_x),
                    carry[4 * k + 2] + (q1 * fields[1] + q2 * h_y),
                    carry[4 * k + 3] + (q1 * fields[2] + q2 * h_z),
                ]
            return tuple(found)

        zero = jnp.zeros((ROWS, LANES), f32)
        found = lax.fori_loop(0, channels // ROWS, body, (zero,) * (4 * entries))
        for k in range(entries):
            for d, item in enumerate(offset_gradients(found[4 * k : 4 * k + 4], geo, edges[k])):
                g_off[d : d + 1, edges[k]] = item
    high, low = split2(g_feat[...])
    left = jnp.concatenate([high, low, pieces(g_off[...])], axis=0)
    scattered = matmul(left, onehot_t[...])
    g_proj = scattered[0:channels] + scattered[channels : 2 * channels]
    g_ext = whole(scattered[2 * channels : 2 * channels + 3 * ROWS])
    g_all = matmul(weights[4], stacked_right(g_proj))
    g_h[...] = g_all[:, 0:slots] + g_own[...]
    send_gx[...] = g_all[:, slots : slots + LANES]
    send_yz[...] = g_all[:, slots + LANES : slots + 2 * LANES]
    own = sum(g_off[:, k * slots : (k + 1) * slots] for k in range(entries))
    g_pos[:, 0:slots] = g_ext[:, 0:slots] - own
    g_pos[:, slots:wide] = g_ext[:, slots:wide]


def first_gradient_kernel(
    g_h, got_gx, got_core, got_chip, slope, factors, geo, g_pos_two, onehot_t, send_t, weights,
    g_pos, send_gx, send_yz,
    g_ref, g_off,
):
    channels, slots = slope.shape
    entries = geo.shape[2] // slots
    back = jnp.concatenate([got_gx[...], returned_yz(got_core[...], got_chip[...])], axis=1)
    returned = matmul(jnp.concatenate(split2(back), axis=0), send_t[...])
    g_total = g_h[...] + (returned[0:channels] + returned[channels : 2 * channels])
    g_ref[...] = matmul(weights[5], stacked_right(g_total * slope[...]))
    g_off[...] = jnp.zeros(g_off.shape, f32)
    for lanes, edges in lane_parts(slots, entries):

        def body(index, carry):
            rows = tile(index)
            g = g_ref[rows, lanes]
            return tuple(
                carry[4 * k + m] + g * factors[m, rows, edges[k]] for k in range(entries) for m in range(4)
            )

        zero = jnp.zeros((ROWS, LANES), f32)
        found = lax.fori_loop(0, channels // ROWS, body, (zero,) * (4 * entries), unroll=4)
        for k in range(entries):
            for d, item in enumerate(offset_gradients(found[4 * k : 4 * k + 4], geo, edges[k])):
                g_off[d : d + 1, edges[k]] = item
    g_ext = whole(matmul(pieces(g_off[...]), onehot_t[...])) + g_pos_two[...]
    own = sum(g_off[:, k * slots : (k + 1) * slots] for k in range(entries))
    g_pos[...] = g_ext[:, 0:slots] - own
    send_gx[...] = g_ext[:, slots : slots + LANES]
    send_yz[...] = g_ext[:, slots + LANES : slots + 2 * LANES]


def force_kernel(g_pos, got_gx, got_core, got_chip, send_t, *rest):
    tallies, (forces, energy) = rest[:-2], rest[-2:]
    back = jnp.concatenate([got_gx[...], returned_yz(got_core[...], got_chip[...])], axis=1)
    total = g_pos[...] + whole(matmul(pieces(back), send_t[...]))
    forces[...] = -total[0:3]
    sums = jnp.sum(sum(item[0:2, :] for item in tallies), axis=1, keepdims=True)
    energy[...] = sums[0:1, :] / sums[1:2, :]


def call(kernel, outs, scalars, arrays, scratch=(), name=None, raw=False, us=1.0):
    in_vmem = pl.BlockSpec(memory_space=pltpu.VMEM)
    in_smem = pl.BlockSpec(memory_space=pltpu.SMEM)
    in_hbm = pl.BlockSpec(memory_space=pltpu.HBM)
    shapes = [jax.ShapeDtypeStruct(*item) if isinstance(item[0], tuple) else jax.ShapeDtypeStruct(item, f32) for item in outs]
    return pl.pallas_call(
        kernel,
        out_shape=shapes,
        in_specs=[in_smem] * len(scalars) + [in_hbm if raw else in_vmem] * len(arrays),
        out_specs=[in_vmem] * len(outs),
        scratch_shapes=[pltpu.VMEM(item, f32) if isinstance(item, tuple) else item for item in scratch],
        compiler_params=pltpu.CompilerParams(vmem_limit_bytes=VMEM_BYTES),
        cost_estimate=pl.CostEstimate(flops=int(us * 1e9), bytes_accessed=int(us * 3e6), transcendentals=0),
        name=name,
    )(*scalars, *arrays)


def swap_core(value):
    size = lax.axis_size("yz")
    return lax.ppermute(value, "yz", [(i, i ^ 1) for i in range(size)])


def swap_chip(value):
    size = lax.axis_size("yz")
    return lax.ppermute(value, "yz", [(i, (i + 1 if i % 2 else i - 1) % size) for i in range(size)])


def shift(value, axis, by):
    size = lax.axis_size(axis)
    return lax.ppermute(value, axis, [(i, (i + by) % size) for i in range(size)])


def swap_gx(value):
    size = lax.axis_size("gx")
    if size == 2:
        return shift(value, "gx", 1)
    half = value.shape[1] // 2
    return jnp.concatenate(
        [shift(value[:, :half], "gx", 1), shift(value[:, half:], "gx", -1)], axis=1
    )


def return_gx(value):
    size = lax.axis_size("gx")
    if size == 2:
        return shift(value, "gx", 1)
    half = value.shape[1] // 2
    return jnp.concatenate(
        [shift(value[:, :half], "gx", -1), shift(value[:, half:], "gx", 1)], axis=1
    )


def group_parts(value, axis, bits):
    size = lax.axis_size(axis)
    steps = [0]
    for bit in bits:
        steps += [step ^ (1 << bit) for step in steps]
    return [lax.ppermute(value, axis, [(i, i ^ step) for i in range(size)]) if step else value for step in steps]


def shards(
    old_pos,
    old_species,
    block_dest,
    block_count,
    send_list,
    neighbours,
    embed,
    atom_ref,
    w_up,
    gammas,
    w_rad,
    w_mix,
    readout,
):
    entries, slots = neighbours.shape
    blocks = block_dest.shape[0]
    width = old_species.shape[0] // blocks
    channels = w_up.shape[1]
    ghosts = send_list.size
    wide = slots + ghosts
    edges = entries * slots
    rows = w_rad.shape[2]
    species = old_species.reshape(blocks, width)
    i32 = jnp.int32

    (packed,) = call(
        pack_kernel,
        [(3 * ROWS, width)],
        [],
        [block_dest.T, block_count, old_pos, species],
        [
            pltpu.SMEM((1, blocks), i32),
            pltpu.SMEM((blocks,), i32),
            old_pos.shape,
            pltpu.VMEM(species.shape, i32),
            pltpu.SemaphoreType.DMA((4,)),
        ],
        name="pack",
        raw=True,
    )
    got_chip = swap_chip(packed)
    got_core = swap_core(packed)
    onehot, send, gamma, radials, species_up, species_in, weights, reads, onehot_t, send_t = call(
        prepare_kernel,
        [
            ((wide, edges), bf16),
            ((slots, ghosts), bf16),
            (2, ROWS, edges),
            ((2, rows, 3 * ROWS), bf16),
            ((channels, 3 * ROWS), bf16),
            ((channels, 3 * ROWS), bf16),
            ((6, channels, 3 * channels), bf16),
            (2, channels, slots),
            ((edges, wide), bf16),
            ((ghosts, slots), bf16),
        ],
        [],
        [gammas, neighbours, send_list, embed, w_up, w_rad, w_mix, readout],
        [
            pltpu.SMEM(gammas.shape, f32),
            pltpu.VMEM(neighbours.shape, i32),
            pltpu.VMEM(send_list.shape, i32),
            embed.shape,
            w_up.shape,
            w_rad.shape,
            w_mix.shape,
            readout.shape,
            (ROWS, channels),
            pltpu.SemaphoreType.DMA((8,)),
        ],
        name="prepare",
        raw=True,
        us=3.0,
    )
    small = (ROWS, LANES)
    table, pick_gx, pick_yz = call(
        assemble_kernel,
        [(ROWS, slots), small, small],
        [],
        [packed, got_core, got_chip, send],
        name="assemble",
        us=0.2,
    )
    got_chip = swap_chip(pick_yz)
    got_gx = swap_gx(pick_gx)
    got_core = swap_core(pick_yz)
    flat = (channels, slots)
    square = (channels, LANES)
    fields_shape = (9, channels, slots)
    h_one, slope, send_gx, send_yz, geo, angular, rad_one, feat_one, fields_one = call(
        first_layer_kernel,
        [flat, flat, square, square, (8, ROWS, edges), (8, ROWS, edges), (rows, edges), (channels, edges), fields_shape],
        [],
        [table, got_gx, got_core, got_chip, onehot, send, gamma, radials, species_up, species_in, weights],
        [flat],
        name="first_layer",
        us=2.5,
    )
    got_chip = swap_chip(send_yz)
    got_gx = swap_gx(send_gx)
    got_core = swap_core(send_yz)
    factors, rad_two, slope_two, base = call(
        factor_kernel,
        [(4, channels, edges), (rows, edges), (rows, edges), small],
        [atom_ref],
        [geo, gamma, radials, table, rad_one, feat_one, fields_one],
        [(rows, edges)],
        name="factors",
        us=3.5,
    )
    feat_two, fields_two, g_two, g_own, tally = call(
        second_layer_kernel,
        [(channels, edges), fields_shape, flat, flat, small],
        [],
        [base, table, h_one, got_gx, got_core, got_chip, onehot, angular, rad_two, weights, reads],
        [flat],
        name="second_layer",
        us=2.5,
    )
    bits = (lax.axis_size("yz") - 1).bit_length()
    early = sorted({1, bits - 1} - {0})
    tally = sum(group_parts(tally, "yz", early))
    g_h, send_gx, send_yz, g_pos_two = call(
        second_gradient_kernel,
        [flat, square, square, (ROWS, wide)],
        [],
        [geo, rad_two, slope_two, feat_two, fields_two, g_two, g_own, onehot_t, weights],
        [(channels, edges), (ROWS, edges)],
        name="second_gradient",
        us=3.5,
    )
    got_chip = swap_chip(send_yz)
    got_gx = return_gx(send_gx)
    got_core = swap_core(send_yz)
    tally = tally + swap_core(tally)
    g_pos, send_gx, send_yz = call(
        first_gradient_kernel,
        [(ROWS, slots), small, small],
        [],
        [g_h, got_gx, got_core, got_chip, slope, factors, geo, g_pos_two, onehot_t, send_t, weights],
        [flat, (ROWS, edges)],
        name="first_gradient",
        us=1.2,
    )
    tally = sum(group_parts(tally, "yz", [bit for bit in range(1, bits) if bit not in early]))
    got_chip = swap_chip(send_yz)
    got_gx = return_gx(send_gx)
    got_core = swap_core(send_yz)
    tallies = group_parts(tally, "gx", range((lax.axis_size("gx") - 1).bit_length()))
    forces, energy = call(
        force_kernel,
        [(3, slots), (1, 1)],
        [],
        [g_pos, got_gx, got_core, got_chip, send_t] + tallies,
        name="forces",
    )
    return (forces, energy.reshape(()))


def solution(mesh):
    return jax.shard_map(
        shards,
        mesh=mesh,
        in_specs=(
            P(None, ("gx", "yz")),
            P(("gx", "yz")),
            P(("gx", "yz"), None),
            P(("gx", "yz")),
            P(("gx", "yz"), None),
            P(None, ("gx", "yz")),
            P(),
            P(),
            P(),
            P(),
            P(),
            P(),
            P(),
        ),
        out_specs=(P(None, ("gx", "yz")), P()),
        check_vma=False,
    )
```

time: 76.7 us -> 56.7 us (0.74)
  waiting for transfers between devices: 24.7 us -> 8.71 us
  starting transfers between devices: 22.1 us -> 28.3 us
  Pallas kernels: 21.2 us -> 15.8 us
  between operations: 3.22 us -> 0.87 us
  local copies, waits for them, and re-layouts: 4.69 us -> 2.75 us
    ppermute x5, waiting for transfers between devices: 15.6 us -> 3.61 us  [group_parts(): lax.ppermute(value, axis, [(i, i ^ step) for i in range(size)])]
    pallas_call x6 -> x9, Pallas kernels: 21.2 us -> 15.8 us  [call(): pl.pallas_call(kernel, out_shape=shapes, in_specs=[in_smem] * len(scalars...]
    ppermute x5, waiting for transfers between devices: 7.53 us -> 2.46 us  [swap_chip(): lax.ppermute(value, 'yz', [(i, (i + 1 if i % 2 else i - 1) % size) for i...]
    ppermute x5, starting transfers between devices: 1.02 us -> 5.31 us  [group_parts(): lax.ppermute(value, axis, [(i, i ^ step) for i in range(size)])]
    unnamed x29 -> x26, local copies, waits for them, and re-layouts: 4.61 us -> 2.75 us
    ppermute x5 -> x6, waiting for transfers between devices: 0.01 us -> 0.95 us  [swap_core(): return lax.ppermute(value, 'yz', [(i, i ^ 1) for i in range(size)])]
    ppermute x5 -> x6, starting transfers between devices: 0.12 us -> 0.96 us  [swap_core(): return lax.ppermute(value, 'yz', [(i, i ^ 1) for i in range(size)])]
  transfers between devices with their start and end apart: 19 -> 20, of which waited for: 11 -> 5; matrix products, arithmetic and copies ran while one was open for 1% -> 0% of each run, Pallas kernels for 0% -> 17%
where the time goes in v2:
time: 56.7 us; the launch traced here: 56.5 us
  starting transfers between devices  28.3 us (50%)
  Pallas kernels  15.8 us (28%)
  waiting for transfers between devices  8.71 us (15%)
  local copies, waits for them, and re-layouts  2.75 us (5%)
  between operations  0.87 us (2%)
    ppermute x5, starting transfers between devices, swap_chip(): lax.ppermute(value, 'yz', [(i, (i + 1 if i % 2 else i - 1) % size) for i...  16.6 us
    pallas_call x9, Pallas kernels, call(): pl.pallas_call(kernel, out_shape=shapes, in_specs=[in_smem] * len(scalars...  15.8 us
    ppermute x4, starting transfers between devices, shift(): lax.ppermute(value, axis, [(i, (i + by) % size) for i in range(size)])  5.42 us
    ppermute x5, starting transfers between devices, group_parts(): lax.ppermute(value, axis, [(i, i ^ step) for i in range(size)])  5.31 us
    ppermute x5, waiting for transfers between devices, group_parts(): lax.ppermute(value, axis, [(i, i ^ step) for i in range(size)])  3.61 us
    unnamed x26, local copies, waits for them, and re-layouts  2.75 us
    ppermute x5, waiting for transfers between devices, swap_chip(): lax.ppermute(value, 'yz', [(i, (i + 1 if i % 2 else i - 1) % size) for i...  2.46 us
    ppermute x4, waiting for transfers between devices, shift(): lax.ppermute(value, axis, [(i, (i + by) % size) for i in range(size)])  1.69 us
  transfers between devices with their start and end apart: 20, of which 5 were waited for; matrix products, arithmetic and copies ran while one was open for 0% of the time, Pallas kernels for 17%

profile of v2, /device:TPU:0, one launch (start us, length us, event | category | flops | bytes accessed | tf_op | source)
XLA Modules:
  0.0 56.5 jit_solution(5417088667946949128)
XLA Ops:
  0.7 0.7 %copy-done.4 = f32[3,256]{1,0:T(4,128)S(1)} copy-done((f32[3,256]{1,0:T(4,128)S(1)}, f32[3,256]{1,0:T(4,128)}, u32[]{:S(2)}) %copy-start.4) | copy-done | bytes 3096
  1.4 0.7 %copy-done.7 = s32[256]{0:T(256)S(1)} copy-done((s32[256]{0:T(256)S(1)}, s32[256]{0:T(256)}, u32[]{:S(2)}) %copy-start.7) | copy-done | bytes 1048
  2.1 0.7 %copy-done.10 = s32[2,1]{0,1:T(1,128)S(1)} copy-done((s32[2,1]{0,1:T(1,128)S(1)}, s32[2,1]{0,1:T(1,128)}, u32[]{:S(2)}) %copy-start.10) | copy-done | bytes 32
  2.7 0.7 %copy-done.11 = s32[2]{0:T(128)S(1)} copy-done((s32[2]{0:T(128)S(1)}, s32[2]{0:T(128)}, u32[]{:S(2)}) %copy-start.11) | copy-done | bytes 32
  3.4 0.6 %pack.1.own = f32[24,128]{1,0:T(8,128)S(1)} custom-call(s32[1,2]{1,0:T(1,128)S(1)} %bitcast.4, s32[2]{0:T(128)S(1)} %copy-done.11, f32[3,256]{1,0:T(4,128)S(1)} %copy-done.4, s32[2,128]{1,0:T(2,128)S(1)} %bitcast.3), custom_call_target="tpu_custom_call" | custom-call | flops 1000000000 | bytes 3000000 | tf_op jit(solution)/shard_map/pack/pallas_call | solution.py:519
  4.0 0.5 collective-permute-start
  4.5 5.6 %collective-permute-start.1 = (f32[24,128]{1,0:T(8,128)S(1)}, f32[24,128]{1,0:T(8,128)S(1)}, u32[]{:S(2)}, u32[]{:S(2)}) collective-permute-start(f32[24,128]{1,0:T(8,128)S(1)} %pack.1.own), channel_id=1, source_target_pairs={{0,15},{1,2},{2,1},{3,4},{4,3},{5,6},{6,5},{7,8},{8,7},{9,10},{10,... | collective-permute-start | bytes 36872 | tf_op jit(solution)/shard_map/ppermute | solution.py:538
  10.2 1.9 %prepare.1 = (bf16[640,1536]{1,0:T(8,128)(2,1)S(1)}, bf16[384,256]{1,0:T(8,128)(2,1)S(1)}, f32[2,8,1536]{2,1,0:T(8,128)S(1)}, bf16[2,384,24]{2,1,0:T(8,128)(2,1)...) custom-call(f32[2,8]{1,0:T(2,128)S(1)} %copy-done.8, ...), custom_call_target="tpu_custom_call" | custom-call | flops 3000000000 | bytes 9000000 | tf_op jit(solution)/shard_map/prepare/pallas_call | solution.py:519
  12.2 0.0 collective-permute-done.core
  12.2 0.0 collective-permute-done.1.chip
  12.2 0.1 assemble.1
  12.3 0.1 collective-permute-start.3
  12.4 3.9 %collective-permute-start.4 = (f32[8,128]{1,0:T(8,128)S(1)}, f32[8,128]{1,0:T(8,128)S(1)}, u32[]{:S(2)}, u32[]{:S(2)}) collective-permute-start(f32[8,128]{1,0:T(8,128)S(1)} %get-tuple-element.45), channel_id=1, source_target_pairs={{0,15},{1,2},{2,1},{3,4},{4,3},{5,6},{6,5},{7,8},{8,7},{9,10},{10,... | collective-permute-start | bytes 12296 | tf_op jit(solution)/shard_map/ppermute | solution.py:538
  16.3 1.5 %collective-permute-start.2 = (f32[8,128]{1,0:T(8,128)S(1)}, f32[8,128]{1,0:T(8,128)S(1)}, u32[]{:S(2)}, u32[]{:S(2)}) collective-permute-start(f32[8,128]{1,0:T(8,128)S(1)} %get-tuple-element.44), channel_id=1, source_target_pairs={{0,16},{16,0},{1,17},{17,1},{2,18},{18,2},{3,19},{19,3},{4,20},{20... | collective-permute-start | bytes 12296 | tf_op jit(solution)/shard_map/ppermute | solution.py:543
  17.8 0.0 collective-permute-done.3.got_core
  17.8 0.4 collective-permute-done.4.got_chip
  18.2 1.7 %collective-permute-done.2.got_gx = f32[8,128]{1,0:T(8,128)S(1)} collective-permute-done((f32[8,128]{1,0:T(8,128)S(1)}, f32[8,128]{1,0:T(8,128)S(1)}, u32[]{:S(2)}, u32[]{:S(2)}) %collective-permute-start.2) | collective-permute-done | bytes 4128 | tf_op jit(solution)/shard_map/ppermute | solution.py:543
  19.9 2.4 %first_layer.1 = (f32[128,384]{1,0:T(8,128)S(1)}, f32[128,384]{1,0:T(8,128)S(1)}, f32[128,128]{1,0:T(8,128)S(1)}, f32[128,128]{1,0:T(8,128)S(1)}, f32[8,8,1536]{...) custom-call(f32[8,384]{1,0:T(8,128)S(1)} %get-tuple-element.43.table, ...), custom_call_target="tpu_custom_call" | custom-call | flops 2500000000 | bytes 7500000 | tf_op jit(solution)/shard_map/first_layer/pallas_call | solution.py:519
  22.3 0.1 collective-permute-start.6
  22.4 2.2 %collective-permute-start.7 = (f32[128,128]{1,0:T(8,128)S(1)}, f32[128,128]{1,0:T(8,128)S(1)}, u32[]{:S(2)}, u32[]{:S(2)}) collective-permute-start(f32[128,128]{1,0:T(8,128)S(1)} %get-tuple-element.61), channel_id=1, source_target_pairs={{0,15},{1,2},{2,1},{3,4},{4,3},{5,6},{6,5},{7,8},{8,7},{9,10},{10,... | collective-permute-start | bytes 196616 | tf_op jit(solution)/shard_map/ppermute | solution.py:538
  24.6 1.5 %collective-permute-start.5 = (f32[128,128]{1,0:T(8,128)S(1)}, f32[128,128]{1,0:T(8,128)S(1)}, u32[]{:S(2)}, u32[]{:S(2)}) collective-permute-start(f32[128,128]{1,0:T(8,128)S(1)} %get-tuple-element.60), channel_id=1, source_target_pairs={{0,16},{16,0},{1,17},{17,1},{2,18},{18,2},{3,19},{19,3},{4,20},{20... | collective-permute-start | bytes 196616 | tf_op jit(solution)/shard_map/ppermute | solution.py:543
  26.1 3.1 %factors.1 = (f32[4,128,1536]{2,1,0:T(8,128)S(1)}, f32[384,1536]{1,0:T(8,128)S(1)}, f32[384,1536]{1,0:T(8,128)S(1)}, f32[8,128]{1,0:T(8,128)S(1)}) custom-call(f32[5]{0:T(128)S(1)} %copy-done.12, f32[8,8,1536]{2,1,0:T(8,128)S(1)} %get-tuple-element.52.geo, f32[2,8,1536]{2,1,0:T(8,128)S(1)} %get-tuple-element.47.gamma, ...), custom_call_target="tpu_custom_call" | custom-call | flops 3500000000 | bytes 10500000 | tf_op jit(solution)/shard_map/factors/pallas_call | solution.py:519
  29.3 0.0 collective-permute-done.5.got_gx
  29.3 0.0 collective-permute-done.6.got_core
  29.3 0.0 collective-permute-done.7.got_chip
  29.3 2.4 %second_layer.1 = (f32[128,1536]{1,0:T(8,128)S(1)}, f32[9,128,384]{2,1,0:T(8,128)S(1)}, f32[128,384]{1,0:T(8,128)S(1)}, f32[128,384]{1,0:T(8,128)S(1)}, f32[8,128]{1,0:T(8,128)S(1)}) custom-call(f32[8,128]{1,0:T(8,128)S(1)} %get-tuple-element.58.base, f32[8,384]{1,0:T(8,128)S(1)} %get-tuple-element.43.table, f32[128,384]{1,0:T(8,128)S(1)} %get-tuple-element.59.h_one, ...), custom_call_target="tpu_custom_call" | custom-call | flops 2500000000 | bytes 7500000 | tf_op jit(solution)/shard_map/second_layer/pallas_call | solution.py:519
  31.7 0.1 collective-permute-start.14
  31.8 0.1 collective-permute-start.15
  31.8 4.3 %collective-permute-start.16 = (f32[8,128]{1,0:T(8,128)S(1)}, f32[8,128]{1,0:T(8,128)S(1)}, u32[]{:S(2)}, u32[]{:S(2)}) collective-permute-start(f32[8,128]{1,0:T(8,128)S(1)} %get-tuple-element.79), channel_id=1, source_target_pairs={{0,10},{1,11},{2,8},{3,9},{4,14},{5,15},{6,12},{7,13},{8,2},{9,3},... | collective-permute-start | bytes 12296 | tf_op jit(solution)/shard_map/ppermute | solution.py:571
  36.1 3.2 %second_gradient.1 = (f32[128,384]{1,0:T(8,128)S(1)}, f32[128,128]{1,0:T(8,128)S(1)}, f32[128,128]{1,0:T(8,128)S(1)}, f32[8,640]{1,0:T(8,128)S(1)}) custom-call(f32[8,8,1536]{2,1,0:T(8,128)S(1)} %get-tuple-element.52.geo, f32[384,1536]{1,0:T(8,128)S(1)} %get-tuple-element.56.rad_ref, f32[384,1536]{1,0:T(8,128)S(1)} %get-tuple-element.57.slope_ref, ...), custom_call_target="tpu_custom_call" | custom-call | flops 3500000000 | bytes 10500000 | tf_op jit(solution)/shard_map/second_gradient/pallas_call | solution.py:519
  39.4 1.3 %collective-permute-start.10 = (f32[128,128]{1,0:T(8,128)S(1)}, f32[128,128]{1,0:T(8,128)S(1)}, u32[]{:S(2)}, u32[]{:S(2)}) collective-permute-start(f32[128,128]{1,0:T(8,128)S(1)} %get-tuple-element.71), channel_id=1, source_target_pairs={{0,15},{1,2},{2,1},{3,4},{4,3},{5,6},{6,5},{7,8},{8,7},{9,10},{10,... | collective-permute-start | bytes 196616 | tf_op jit(solution)/shard_map/ppermute | solution.py:538
  40.7 0.0 collective-permute-done.14
  40.7 1.2 %collective-permute-start.8 = (f32[128,128]{1,0:T(8,128)S(1)}, f32[128,128]{1,0:T(8,128)S(1)}, u32[]{:S(2)}, u32[]{:S(2)}) collective-permute-start(f32[128,128]{1,0:T(8,128)S(1)} %get-tuple-element.70), channel_id=1, source_target_pairs={{0,16},{16,0},{1,17},{17,1},{2,18},{18,2},{3,19},{19,3},{4,20},{20... | collective-permute-start | bytes 196616 | tf_op jit(solution)/shard_map/ppermute | solution.py:543
  41.8 0.0 collective-permute-done.15
  41.8 0.0 collective-permute-done.16
  41.8 0.3 collective-permute-start.17
  42.1 0.9 %collective-permute-done.17 = f32[8,128]{1,0:T(8,128)S(1)} collective-permute-done((f32[8,128]{1,0:T(8,128)S(1)}, f32[8,128]{1,0:T(8,128)S(1)}, u32[]{:S(2)}, u32[]{:S(2)}) %collective-permute-start.17) | collective-permute-done | bytes 4128 | tf_op jit(solution)/shard_map/ppermute | solution.py:533
  43.1 0.0 collective-permute-start.18
  43.1 3.6 %collective-permute-done.18 = f32[8,128]{1,0:T(8,128)S(1)} collective-permute-done((f32[8,128]{1,0:T(8,128)S(1)}, f32[8,128]{1,0:T(8,128)S(1)}, u32[]{:S(2)}, u32[]{:S(2)}) %collective-permute-start.18) | collective-permute-done | bytes 4128 | tf_op jit(solution)/shard_map/ppermute | solution.py:571
  46.7 0.9 %collective-permute-start.19 = (f32[8,128]{1,0:T(8,128)S(1)}, f32[8,128]{1,0:T(8,128)S(1)}, u32[]{:S(2)}, u32[]{:S(2)}) collective-permute-start(f32[8,128]{1,0:T(8,128)S(1)} %add.19.rest_0_), channel_id=1, source_target_pairs={{0,16},{16,0},{1,17},{17,1},{2,18},{18,2},{3,19},{19,3},{4,20},{20... | collective-permute-start | bytes 12296 | tf_op jit(solution)/shard_map/ppermute | solution.py:571
  47.5 0.0 collective-permute-done.10.got_chip
  47.6 1.2 %first_gradient.1 = (f32[8,384]{1,0:T(8,128)S(1)}, f32[8,128]{1,0:T(8,128)S(1)}, f32[8,128]{1,0:T(8,128)S(1)}) custom-call(f32[128,384]{1,0:T(8,128)S(1)} %get-tuple-element.69.g_h, f32[128,128]{1,0:T(8,128)S(1)} %collective-permute-done.8.got_gx, f32[128,128]{1,0:T(8,128)S(1)} %collective-permute-done.9.got_core, ...), custom_call_target="tpu_custom_call" | custom-call | flops 1200000000 | bytes 3600000 | tf_op jit(solution)/shard_map/first_gradient/pallas_call | solution.py:519
  48.8 1.2 %collective-permute-start.11 = (f32[8,128]{1,0:T(8,128)S(1)}, f32[8,128]{1,0:T(8,128)S(1)}, u32[]{:S(2)}, u32[]{:S(2)}) collective-permute-start(f32[8,128]{1,0:T(8,128)S(1)} %get-tuple-element.77), channel_id=1, source_target_pairs={{0,16},{16,0},{1,17},{17,1},{2,18},{18,2},{3,19},{19,3},{4,20},{20... | collective-permute-start | bytes 12296 | tf_op jit(solution)/shard_map/ppermute | solution.py:543
  50.0 0.0 collective-permute-start.12
  50.0 3.7 %collective-permute-start.13 = (f32[8,128]{1,0:T(8,128)S(1)}, f32[8,128]{1,0:T(8,128)S(1)}, u32[]{:S(2)}, u32[]{:S(2)}) collective-permute-start(f32[8,128]{1,0:T(8,128)S(1)} %get-tuple-element.78), channel_id=1, source_target_pairs={{0,15},{1,2},{2,1},{3,4},{4,3},{5,6},{6,5},{7,8},{8,7},{9,10},{10,... | collective-permute-start | bytes 12296 | tf_op jit(solution)/shard_map/ppermute | solution.py:538
  53.7 0.0 collective-permute-done.19.rest_1_
  53.7 2.0 %collective-permute-done.13.got_chip = f32[8,128]{1,0:T(8,128)S(1)} collective-permute-done((f32[8,128]{1,0:T(8,128)S(1)}, f32[8,128]{1,0:T(8,128)S(1)}, u32[]{:S(2)}, u32[]{:S(2)}) %collective-permute-start.13) | collective-permute-done | bytes 4128 | tf_op jit(solution)/shard_map/ppermute | solution.py:538
  55.7 0.8 %forces.1 = (f32[3,384]{1,0:T(4,128)}, f32[1,1]{1,0:T(1,128)}) custom-call(f32[8,384]{1,0:T(8,128)S(1)} %get-tuple-element.76.g_pos, f32[8,128]{1,0:T(8,128)S(1)} %collective-permute-done.11.got_gx, f32[8,128]{1,0:T(8,128)S(1)} %collective-permute-done.12.got_core, f32[8,128]{1,0:T(8,128)S(1)} %collective-permute-done.13.got_chip, ...), custom_call_target="tpu_custom_call" | custom-call | flops 1000000000 | bytes 3000000 | tf_op jit(solution)/shard_map/forces/pallas_call | solution.py:519
  (30 shorter events, 0.1 us)
Async XLA Ops:
  0.6 9.5 %copy-start.3 = (s32[4,384]{1,0:T(4,128)S(1)}, s32[4,384]{1,0:T(4,128)}, u32[]{:S(2)}) copy-start(s32[4,384]{1,0:T(4,128)} %nbr_hbm.1) | copy-start | bytes 18436
  0.6 9.5 %copy-start = (f32[2,128,128]{2,1,0:T(8,128)S(1)}, f32[2,128,128]{2,1,0:T(8,128)}, u32[]{:S(2)}) copy-start(f32[2,128,128]{2,1,0:T(8,128)} %w_up_hbm.1) | copy-start | bytes 393220
  0.7 9.5 %copy-start.2 = (f32[2,8,384]{2,1,0:T(8,128)S(1)}, f32[2,8,384]{2,1,0:T(8,128)}, u32[]{:S(2)}) copy-start(f32[2,8,384]{2,1,0:T(8,128)} %w_rad_hbm.1) | copy-start | bytes 73732
  0.7 9.5 %copy-start.1 = (f32[2,128,128]{2,1,0:T(8,128)S(1)}, f32[2,128,128]{2,1,0:T(8,128)}, u32[]{:S(2)}) copy-start(f32[2,128,128]{2,1,0:T(8,128)} %w_mix_hbm.1) | copy-start | bytes 393220
  0.7 0.7 %copy-start.4 = (f32[3,256]{1,0:T(4,128)S(1)}, f32[3,256]{1,0:T(4,128)}, u32[]{:S(2)}) copy-start(f32[3,256]{1,0:T(4,128)} %pos_hbm.1) | copy-start | bytes 9220
  1.4 0.7 %copy-start.7 = (s32[256]{0:T(256)S(1)}, s32[256]{0:T(256)}, u32[]{:S(2)}) copy-start(s32[256]{0:T(256)} %param.14) | copy-start | bytes 3076
  2.1 0.7 %copy-start.10 = (s32[2,1]{0,1:T(1,128)S(1)}, s32[2,1]{0,1:T(1,128)}, u32[]{:S(2)}) copy-start(s32[2,1]{0,1:T(1,128)} %param.15) | copy-start | bytes 28
  2.7 0.7 %copy-start.11 = (s32[2]{0:T(128)S(1)}, s32[2]{0:T(128)}, u32[]{:S(2)}) copy-start(s32[2]{0:T(128)} %count_hbm.1) | copy-start | bytes 28
  3.4 6.8 %copy-start.5 = (f32[5,128]{1,0:T(8,128)S(1)}, f32[5,128]{1,0:T(8,128)}, u32[]{:S(2)}) copy-start(f32[5,128]{1,0:T(8,128)} %embed_hbm.1) | copy-start | bytes 7684
  3.4 6.8 %copy-start.6 = (s32[4,64]{1,0:T(4,128)S(1)}, s32[4,64]{1,0:T(4,128)}, u32[]{:S(2)}) copy-start(s32[4,64]{1,0:T(4,128)} %lists_hbm.1) | copy-start | bytes 3076
  3.4 6.8 %copy-start.8 = (f32[2,8]{1,0:T(2,128)S(1)}, f32[2,8]{1,0:T(2,128)}, u32[]{:S(2)}) copy-start(f32[2,8]{1,0:T(2,128)} %gammas_hbm.1) | copy-start | bytes 196
  3.4 6.8 %copy-start.9 = (f32[2,128]{1,0:T(2,128)S(1)}, f32[2,128]{1,0:T(2,128)}, u32[]{:S(2)}) copy-start(f32[2,128]{1,0:T(2,128)} %readout_hbm.1) | copy-start | bytes 3076
  4.0 8.1 %collective-permute-start = (f32[24,128]{1,0:T(8,128)S(1)}, f32[24,128]{1,0:T(8,128)S(1)}, u32[]{:S(2)}, u32[]{:S(2)}) collective-permute-start(f32[24,128]{1,0:T(8,128)S(1)} %pack.1.own), channel_id=1, source_target_pairs={{0,1},{1,0},{2,3},{3,2},{4,5},{5,4},{6,7},{7,6},{8,9},{9,8},{10,11... | collective-permute-start | bytes 36872 | tf_op jit(solution)/shard_map/ppermute | solution.py:533
  4.5 7.6 %collective-permute-start.1 = (f32[24,128]{1,0:T(8,128)S(1)}, f32[24,128]{1,0:T(8,128)S(1)}, u32[]{:S(2)}, u32[]{:S(2)}) collective-permute-start(f32[24,128]{1,0:T(8,128)S(1)} %pack.1.own), channel_id=1, source_target_pairs={{0,15},{1,2},{2,1},{3,4},{4,3},{5,6},{6,5},{7,8},{8,7},{9,10},{10,... | collective-permute-start | bytes 36872 | tf_op jit(solution)/shard_map/ppermute | solution.py:538
  12.3 5.5 %collective-permute-start.3 = (f32[8,128]{1,0:T(8,128)S(1)}, f32[8,128]{1,0:T(8,128)S(1)}, u32[]{:S(2)}, u32[]{:S(2)}) collective-permute-start(f32[8,128]{1,0:T(8,128)S(1)} %get-tuple-element.45), channel_id=1, source_target_pairs={{0,1},{1,0},{2,3},{3,2},{4,5},{5,4},{6,7},{7,6},{8,9},{9,8},{10,11... | collective-permute-start | bytes 12296 | tf_op jit(solution)/shard_map/ppermute | solution.py:533
  12.4 5.8 %collective-permute-start.4 = (f32[8,128]{1,0:T(8,128)S(1)}, f32[8,128]{1,0:T(8,128)S(1)}, u32[]{:S(2)}, u32[]{:S(2)}) collective-permute-start(f32[8,128]{1,0:T(8,128)S(1)} %get-tuple-element.45), channel_id=1, source_target_pairs={{0,15},{1,2},{2,1},{3,4},{4,3},{5,6},{6,5},{7,8},{8,7},{9,10},{10,... | collective-permute-start | bytes 12296 | tf_op jit(solution)/shard_map/ppermute | solution.py:538
  16.3 3.6 %collective-permute-start.2 = (f32[8,128]{1,0:T(8,128)S(1)}, f32[8,128]{1,0:T(8,128)S(1)}, u32[]{:S(2)}, u32[]{:S(2)}) collective-permute-start(f32[8,128]{1,0:T(8,128)S(1)} %get-tuple-element.44), channel_id=1, source_target_pairs={{0,16},{16,0},{1,17},{17,1},{2,18},{18,2},{3,19},{19,3},{4,20},{20... | collective-permute-start | bytes 12296 | tf_op jit(solution)/shard_map/ppermute | solution.py:543
  19.9 6.2 %copy-start.12 = (f32[5]{0:T(128)S(1)}, f32[5]{0:T(128)}, u32[]{:S(2)}) copy-start(f32[5]{0:T(128)} %atom_ref.1) | copy-start | bytes 64
  22.3 7.0 %collective-permute-start.6 = (f32[128,128]{1,0:T(8,128)S(1)}, f32[128,128]{1,0:T(8,128)S(1)}, u32[]{:S(2)}, u32[]{:S(2)}) collective-permute-start(f32[128,128]{1,0:T(8,128)S(1)} %get-tuple-element.61), channel_id=1, source_target_pairs={{0,1},{1,0},{2,3},{3,2},{4,5},{5,4},{6,7},{7,6},{8,9},{9,8},{10,11... | collective-permute-start | bytes 196616 | tf_op jit(solution)/shard_map/ppermute | solution.py:533
  22.4 6.9 %collective-permute-start.7 = (f32[128,128]{1,0:T(8,128)S(1)}, f32[128,128]{1,0:T(8,128)S(1)}, u32[]{:S(2)}, u32[]{:S(2)}) collective-permute-start(f32[128,128]{1,0:T(8,128)S(1)} %get-tuple-element.61), channel_id=1, source_target_pairs={{0,15},{1,2},{2,1},{3,4},{4,3},{5,6},{6,5},{7,8},{8,7},{9,10},{10,... | collective-permute-start | bytes 196616 | tf_op jit(solution)/shard_map/ppermute | solution.py:538
  24.6 4.7 %collective-permute-start.5 = (f32[128,128]{1,0:T(8,128)S(1)}, f32[128,128]{1,0:T(8,128)S(1)}, u32[]{:S(2)}, u32[]{:S(2)}) collective-permute-start(f32[128,128]{1,0:T(8,128)S(1)} %get-tuple-element.60), channel_id=1, source_target_pairs={{0,16},{16,0},{1,17},{17,1},{2,18},{18,2},{3,19},{19,3},{4,20},{20... | collective-permute-start | bytes 196616 | tf_op jit(solution)/shard_map/ppermute | solution.py:543
  31.7 9.0 %collective-permute-start.14 = (f32[8,128]{1,0:T(8,128)S(1)}, f32[8,128]{1,0:T(8,128)S(1)}, u32[]{:S(2)}, u32[]{:S(2)}) collective-permute-start(f32[8,128]{1,0:T(8,128)S(1)} %get-tuple-element.79), channel_id=1, source_target_pairs={{0,2},{1,3},{2,0},{3,1},{4,6},{5,7},{6,4},{7,5},{8,10},{9,11},{10,... | collective-permute-start | bytes 12296 | tf_op jit(solution)/shard_map/ppermute | solution.py:571
  31.8 10.1 %collective-permute-start.15 = (f32[8,128]{1,0:T(8,128)S(1)}, f32[8,128]{1,0:T(8,128)S(1)}, u32[]{:S(2)}, u32[]{:S(2)}) collective-permute-start(f32[8,128]{1,0:T(8,128)S(1)} %get-tuple-element.79), channel_id=1, source_target_pairs={{0,8},{1,9},{2,10},{3,11},{4,12},{5,13},{6,14},{7,15},{8,0},{9,1},... | collective-permute-start | bytes 12296 | tf_op jit(solution)/shard_map/ppermute | solution.py:571
  31.8 10.0 %collective-permute-start.16 = (f32[8,128]{1,0:T(8,128)S(1)}, f32[8,128]{1,0:T(8,128)S(1)}, u32[]{:S(2)}, u32[]{:S(2)}) collective-permute-start(f32[8,128]{1,0:T(8,128)S(1)} %get-tuple-element.79), channel_id=1, source_target_pairs={{0,10},{1,11},{2,8},{3,9},{4,14},{5,15},{6,12},{7,13},{8,2},{9,3},... | collective-permute-start | bytes 12296 | tf_op jit(solution)/shard_map/ppermute | solution.py:571
  39.4 8.2 %collective-permute-start.10 = (f32[128,128]{1,0:T(8,128)S(1)}, f32[128,128]{1,0:T(8,128)S(1)}, u32[]{:S(2)}, u32[]{:S(2)}) collective-permute-start(f32[128,128]{1,0:T(8,128)S(1)} %get-tuple-element.71), channel_id=1, source_target_pairs={{0,15},{1,2},{2,1},{3,4},{4,3},{5,6},{6,5},{7,8},{8,7},{9,10},{10,... | collective-permute-start | bytes 196616 | tf_op jit(solution)/shard_map/ppermute | solution.py:538
  40.7 6.9 %collective-permute-start.9 = (f32[128,128]{1,0:T(8,128)S(1)}, f32[128,128]{1,0:T(8,128)S(1)}, u32[]{:S(2)}, u32[]{:S(2)}) collective-permute-start(f32[128,128]{1,0:T(8,128)S(1)} %get-tuple-element.71), channel_id=1, source_target_pairs={{0,1},{1,0},{2,3},{3,2},{4,5},{5,4},{6,7},{7,6},{8,9},{9,8},{10,11... | collective-permute-start | bytes 196616 | tf_op jit(solution)/shard_map/ppermute | solution.py:533
  40.7 6.9 %collective-permute-start.8 = (f32[128,128]{1,0:T(8,128)S(1)}, f32[128,128]{1,0:T(8,128)S(1)}, u32[]{:S(2)}, u32[]{:S(2)}) collective-permute-start(f32[128,128]{1,0:T(8,128)S(1)} %get-tuple-element.70), channel_id=1, source_target_pairs={{0,16},{16,0},{1,17},{17,1},{2,18},{18,2},{3,19},{19,3},{4,20},{20... | collective-permute-start | bytes 196616 | tf_op jit(solution)/shard_map/ppermute | solution.py:543
  41.8 1.2 %collective-permute-start.17 = (f32[8,128]{1,0:T(8,128)S(1)}, f32[8,128]{1,0:T(8,128)S(1)}, u32[]{:S(2)}, u32[]{:S(2)}) collective-permute-start(f32[8,128]{1,0:T(8,128)S(1)} %add_add_fusion), channel_id=1, source_target_pairs={{0,1},{1,0},{2,3},{3,2},{4,5},{5,4},{6,7},{7,6},{8,9},{9,8},{10,11... | collective-permute-start | bytes 12296 | tf_op jit(solution)/shard_map/ppermute | solution.py:533
  43.1 3.6 %collective-permute-start.18 = (f32[8,128]{1,0:T(8,128)S(1)}, f32[8,128]{1,0:T(8,128)S(1)}, u32[]{:S(2)}, u32[]{:S(2)}) collective-permute-start(f32[8,128]{1,0:T(8,128)S(1)} %add.18), channel_id=1, source_target_pairs={{0,4},{1,5},{2,6},{3,7},{4,0},{5,1},{6,2},{7,3},{8,12},{9,13},{10,... | collective-permute-start | bytes 12296 | tf_op jit(solution)/shard_map/ppermute | solution.py:571
  46.7 7.0 %collective-permute-start.19 = (f32[8,128]{1,0:T(8,128)S(1)}, f32[8,128]{1,0:T(8,128)S(1)}, u32[]{:S(2)}, u32[]{:S(2)}) collective-permute-start(f32[8,128]{1,0:T(8,128)S(1)} %add.19.rest_0_), channel_id=1, source_target_pairs={{0,16},{16,0},{1,17},{17,1},{2,18},{18,2},{3,19},{19,3},{4,20},{20... | collective-permute-start | bytes 12296 | tf_op jit(solution)/shard_map/ppermute | solution.py:571
  48.8 4.9 %collective-permute-start.11 = (f32[8,128]{1,0:T(8,128)S(1)}, f32[8,128]{1,0:T(8,128)S(1)}, u32[]{:S(2)}, u32[]{:S(2)}) collective-permute-start(f32[8,128]{1,0:T(8,128)S(1)} %get-tuple-element.77), channel_id=1, source_target_pairs={{0,16},{16,0},{1,17},{17,1},{2,18},{18,2},{3,19},{19,3},{4,20},{20... | collective-permute-start | bytes 12296 | tf_op jit(solution)/shard_map/ppermute | solution.py:543
  50.0 3.7 %collective-permute-start.12 = (f32[8,128]{1,0:T(8,128)S(1)}, f32[8,128]{1,0:T(8,128)S(1)}, u32[]{:S(2)}, u32[]{:S(2)}) collective-permute-start(f32[8,128]{1,0:T(8,128)S(1)} %get-tuple-element.78), channel_id=1, source_target_pairs={{0,1},{1,0},{2,3},{3,2},{4,5},{5,4},{6,7},{7,6},{8,9},{9,8},{10,11... | collective-permute-start | bytes 12296 | tf_op jit(solution)/shard_map/ppermute | solution.py:533
  50.0 5.7 %collective-permute-start.13 = (f32[8,128]{1,0:T(8,128)S(1)}, f32[8,128]{1,0:T(8,128)S(1)}, u32[]{:S(2)}, u32[]{:S(2)}) collective-permute-start(f32[8,128]{1,0:T(8,128)S(1)} %get-tuple-element.78), channel_id=1, source_target_pairs={{0,15},{1,2},{2,1},{3,4},{4,3},{5,6},{6,5},{7,8},{8,7},{9,10},{10,... | collective-permute-start | bytes 12296 | tf_op jit(solution)/shard_map/ppermute | solution.py:538

commit v3 on v2

--- a/solution.py
+++ b/solution.py
@@ -15,6 +15,8 @@
 bf16 = jnp.bfloat16
 ROWS = 8
 LANES = 128
+TALL = 64
+CHIP_ROWS = 32
 VMEM_BYTES = 16 * 1024 * 1024
 
 
@@ -97,6 +99,21 @@
 def returned_yz(core, chip):
     before, after = previous_and_next(core, chip)
     return jnp.where(left_half(core.shape), after, before)
+
+
+def pack_halves(value):
+    half = value.shape[0] // 2
+    top, bottom = value[0:half], value[half:]
+    left = left_half(top.shape)
+    turned_top, turned_bottom = pltpu.roll(top, LANES // 2, 1), pltpu.roll(bottom, LANES // 2, 1)
+    return jnp.where(left, top, turned_bottom), jnp.where(left, turned_top, bottom)
+
+
+def join_halves(left_columns, right_columns):
+    left = left_half(left_columns.shape)
+    top = jnp.where(left, left_columns, pltpu.roll(right_columns, LANES // 2, 1))
+    bottom = jnp.where(left, pltpu.roll(left_columns, LANES // 2, 1), right_columns)
+    return jnp.concatenate([top, bottom], axis=0)
 
 
 def stacked_left(weights):
@@ -293,25 +310,27 @@
         ).astype(bf16)
 
 
-def assemble_kernel(own, core, chip, send, table, pick_gx, pick_yz):
+def assemble_kernel(own, core, chip, send, table, pick_gx, pick_core, pick_chip):
     before, after = previous_and_next(core[...], chip[...])
     blocks = [after[0:ROWS], own[ROWS : 2 * ROWS, :], before[2 * ROWS : 3 * ROWS]]
     slots = jnp.concatenate(blocks, axis=1)
     table[...] = slots
     picked = whole(matmul(pieces(slots), send[...]))
     pick_gx[...] = picked[:, 0:LANES]
-    pick_yz[...] = picked[:, LANES : 2 * LANES]
+    pick_core[...] = picked[:, LANES : 2 * LANES]
+    pick_chip[...] = jnp.zeros(pick_chip.shape, f32)
+    pick_chip[0:ROWS, :] = picked[:, LANES : 2 * LANES]
 
 
 def first_layer_kernel(
     table, got_gx, got_core, got_chip, onehot, send, gamma, radials, species_up, species_in, weights,
-    h_out, slope_out, send_gx, send_yz, geo, y_ref, rad_ref, feat_ref, fields_ref,
+    h_out, slope_out, send_gx, send_core, send_chip, geo, y_ref, rad_ref, feat_ref, fields_ref,
     inv_ref,
 ):
     slots = table.shape[1]
     edges = onehot.shape[1]
     entries = edges // slots
-    ext = jnp.concatenate([table[...], got_gx[...], faces_yz(got_core[...], got_chip[...])], axis=1)
+    ext = jnp.concatenate([table[...], got_gx[...], faces_yz(got_core[...], got_chip[0:ROWS, :])], axis=1)
     found = whole(matmul(pieces(ext), onehot[...]))
     feat_ref[...] = matmul(species_up[...], species_onehot(found[3:4], ROWS))
     spread = lambda row: jnp.broadcast_to(row, (ROWS, edges))
@@ -347,7 +366,10 @@
     picked = matmul(jnp.concatenate(split2(h_one), axis=0), send[...])
     picked = picked[0:channels] + picked[channels : 2 * channels]
     send_gx[...] = picked[:, 0:LANES]
-    send_yz[...] = picked[:, LANES : 2 * LANES]
+    to_next, to_previous = pack_halves(picked[:, LANES : 2 * LANES])
+    even = is_even()
+    send_core[...] = jnp.where(even, to_next, to_previous)
+    send_chip[...] = jnp.where(even, to_previous, to_next)
 
 
 def factor_kernel(
@@ -400,7 +422,8 @@
     slots = table.shape[1]
     h_local = h_one[...]
     channels = h_local.shape[0]
-    h_ext = jnp.concatenate([h_local, got_gx[...], faces_yz(got_core[...], got_chip[...])], axis=1)
+    before, after = previous_and_next(got_core[...], got_chip[...])
+    h_ext = jnp.concatenate([h_local, got_gx[...], join_halves(before, after)], axis=1)
     projected = matmul(weights[1], stacked_right(h_ext))
     both = matmul(jnp.concatenate(split2(projected), axis=0), onehot[...])
     feat_ref[...] = both[0:channels] + both[channels : 2 * channels]
@@ -418,7 +441,7 @@
 
 def second_gradient_kernel(
     geo, rad_ref, slope_ref, feat_ref, fields_ref, g_ref, g_own, onehot_t, weights,
-    g_h, send_gx, send_yz, g_pos,
+    g_h, send_gx, send_core, send_chip, g_pos,
     g_feat, g_off,
 ):
     channels, slots = g_ref.shape
@@ -463,7 +486,10 @@
     g_all = matmul(weights[4], stacked_right(g_proj))
     g_h[...] = g_all[:, 0:slots] + g_own[...]
     send_gx[...] = g_all[:, slots : slots + LANES]
-    send_yz[...] = g_all[:, slots + LANES : slots + 2 * LANES]
+    to_previous, to_next = pack_halves(g_all[:, slots + LANES : slots + 2 * LANES])
+    even = is_even()
+    send_core[...] = jnp.where(even, to_next, to_previous)
+    send_chip[...] = jnp.where(even, to_previous, to_next)
     own = sum(g_off[:, k * slots : (k + 1) * slots] for k in range(entries))
     g_pos[:, 0:slots] = g_ext[:, 0:slots] - own
     g_pos[:, slots:wide] = g_ext[:, slots:wide]
@@ -471,12 +497,13 @@
 
 def first_gradient_kernel(
     g_h, got_gx, got_core, got_chip, slope, factors, geo, g_pos_two, onehot_t, send_t, weights,
-    g_pos, send_gx, send_yz,
+    g_pos, send_gx, send_core, send_chip,
     g_ref, g_off,
 ):
     channels, slots = slope.shape
     entries = geo.shape[2] // slots
-    back = jnp.concatenate([got_gx[...], returned_yz(got_core[...], got_chip[...])], axis=1)
+    before, after = previous_and_next(got_core[...], got_chip[...])
+    back = jnp.concatenate([got_gx[...], join_halves(after, before)], axis=1)
     returned = matmul(jnp.concatenate(split2(back), axis=0), send_t[...])
     g_total = g_h[...] + (returned[0:channels] + returned[channels : 2 * channels])
     g_ref[...] = matmul(weights[5], stacked_right(g_total * slope[...]))
@@ -499,12 +526,14 @@
     own = sum(g_off[:, k * slots : (k + 1) * slots] for k in range(entries))
     g_pos[...] = g_ext[:, 0:slots] - own
     send_gx[...] = g_ext[:, slots : slots + LANES]
-    send_yz[...] = g_ext[:, slots + LANES : slots + 2 * LANES]
+    send_core[...] = g_ext[:, slots + LANES : slots + 2 * LANES]
+    send_chip[...] = jnp.zeros(send_chip.shape, f32)
+    send_chip[0:ROWS, :] = g_ext[:, slots + LANES : slots + 2 * LANES]
 
 
 def force_kernel(g_pos, got_gx, got_core, got_chip, send_t, *rest):
     tallies, (forces, energy) = rest[:-2], rest[-2:]
-    back = jnp.concatenate([got_gx[...], returned_yz(got_core[...], got_chip[...])], axis=1)
+    back = jnp.concatenate([got_gx[...], returned_yz(got_core[...], got_chip[0:ROWS, :])], axis=1)
     total = g_pos[...] + whole(matmul(pieces(back), send_t[...]))
     forces[...] = -total[0:3]
     sums = jnp.sum(sum(item[0:2, :] for item in tallies), axis=1, keepdims=True)
@@ -525,7 +554,7 @@
         compiler_params=pltpu.CompilerParams(vmem_limit_bytes=VMEM_BYTES),
         cost_estimate=pl.CostEstimate(flops=int(us * 1e9), bytes_accessed=int(us * 3e6), transcendentals=0),
         name=name,
-    )(*scalars, *arrays)
+    )(*scalars, *[pltpu.with_memory_space_constraint(item, pltpu.HBM) if raw else item for item in arrays])
 
 
 def swap_core(value):
@@ -563,12 +592,17 @@
     )
 
 
-def group_parts(value, axis, bits):
+def partners(value, axis, bits):
     size = lax.axis_size(axis)
     steps = [0]
     for bit in bits:
         steps += [step ^ (1 << bit) for step in steps]
-    return [lax.ppermute(value, axis, [(i, i ^ step) for i in range(size)]) if step else value for step in steps]
+    return [lax.ppermute(value, axis, [(i, i ^ step) for i in range(size)]) for step in steps[1:]]
+
+
+def together(values, other):
+    *values, other = lax.optimization_barrier((*values, other))
+    return values, other
 
 
 def shards(
@@ -647,35 +681,37 @@
         us=3.0,
     )
     small = (ROWS, LANES)
-    table, pick_gx, pick_yz = call(
+    tall = (CHIP_ROWS, LANES)
+    table, pick_gx, pick_core, pick_chip = call(
         assemble_kernel,
-        [(ROWS, slots), small, small],
+        [(ROWS, slots), small, small, tall],
         [],
         [packed, got_core, got_chip, send],
         name="assemble",
         us=0.2,
     )
-    got_chip = swap_chip(pick_yz)
+    got_chip = swap_chip(pick_chip)
     got_gx = swap_gx(pick_gx)
-    got_core = swap_core(pick_yz)
+    got_core = swap_core(pick_core)
     flat = (channels, slots)
     square = (channels, LANES)
+    half = (channels // 2, LANES)
     fields_shape = (9, channels, slots)
-    h_one, slope, send_gx, send_yz, geo, angular, rad_one, feat_one, fields_one = call(
+    h_one, slope, send_gx, send_core, send_chip, geo, angular, rad_one, feat_one, fields_one = call(
         first_layer_kernel,
-        [flat, flat, square, square, (8, ROWS, edges), (8, ROWS, edges), (rows, edges), (channels, edges), fields_shape],
+        [flat, flat, square, half, half, (8, ROWS, edges), (8, ROWS, edges), (rows, edges), (channels, edges), fields_shape],
         [],
         [table, got_gx, got_core, got_chip, onehot, send, gamma, radials, species_up, species_in, weights],
         [flat],
         name="first_layer",
         us=2.5,
     )
-    got_chip = swap_chip(send_yz)
+    got_chip = swap_chip(send_chip)
     got_gx = swap_gx(send_gx)
-    got_core = swap_core(send_yz)
+    got_core = swap_core(send_core)
     factors, rad_two, slope_two, base = call(
         factor_kernel,
-        [(4, channels, edges), (rows, edges), (rows, edges), small],
+        [(4, channels, edges), (rows, edges), (rows, edges), (TALL, LANES)],
         [atom_ref],
         [geo, gamma, radials, table, rad_one, feat_one, fields_one],
         [(rows, edges)],
@@ -684,7 +720,7 @@
     )
     feat_two, fields_two, g_two, g_own, tally = call(
         second_layer_kernel,
-        [(channels, edges), fields_shape, flat, flat, small],
+        [(channels, edges), fields_shape, flat, flat, (TALL, LANES)],
         [],
         [base, table, h_one, got_gx, got_core, got_chip, onehot, angular, rad_two, weights, reads],
         [flat],
@@ -692,35 +728,42 @@
         us=2.5,
     )
     bits = (lax.axis_size("yz") - 1).bit_length()
-    early = sorted({1, bits - 1} - {0})
-    tally = sum(group_parts(tally, "yz", early))
-    g_h, send_gx, send_yz, g_pos_two = call(
+    got_sums = partners(tally, "yz", [bits - 1] if bits > 1 else [])
+    g_h, send_gx, send_core, send_chip, g_pos_two = call(
         second_gradient_kernel,
-        [flat, square, square, (ROWS, wide)],
+        [flat, square, half, half, (ROWS, wide)],
         [],
         [geo, rad_two, slope_two, feat_two, fields_two, g_two, g_own, onehot_t, weights],
         [(channels, edges), (ROWS, edges)],
         name="second_gradient",
         us=3.5,
     )
-    got_chip = swap_chip(send_yz)
+    got_sums, g_pos_two = together(got_sums, g_pos_two)
+    tally = sum(got_sums, tally)
+    got_chip = swap_chip(send_chip)
     got_gx = return_gx(send_gx)
-    got_core = swap_core(send_yz)
-    tally = tally + swap_core(tally)
-    g_pos, send_gx, send_yz = call(
+    got_core = swap_core(send_core)
+    tally = sum(partners(tally, "yz", [0]), tally)
+    got_sums = partners(tally, "yz", [1] if bits > 2 else [])
+    got_sums, got_chip = together(got_sums, got_chip)
+    tally = sum(got_sums, tally)
+    got_sums = partners(tally, "yz", range(2, bits - 1))
+    g_pos, send_gx, send_core, send_chip = call(
         first_gradient_kernel,
-        [(ROWS, slots), small, small],
+        [(ROWS, slots), small, small, tall],
         [],
         [g_h, got_gx, got_core, got_chip, slope, factors, geo, g_pos_two, onehot_t, send_t, weights],
         [flat, (ROWS, edges)],
         name="first_gradient",
         us=1.2,
     )
-    tally = sum(group_parts(tally, "yz", [bit for bit in range(1, bits) if bit not in early]))
-    got_chip = swap_chip(send_yz)
+    got_sums, g_pos = together(got_sums, g_pos)
+    tally = sum(got_sums, tally)
+    got_chip = swap_chip(send_chip)
     got_gx = return_gx(send_gx)
-    got_core = swap_core(send_yz)
-    tallies = group_parts(tally, "gx", range((lax.axis_size("gx") - 1).bit_length()))
+    got_core = swap_core(send_core)
+    tally = tally[:ROWS]
+    tallies = [tally] + partners(tally, "gx", range((lax.axis_size("gx") - 1).bit_length()))
     forces, energy = call(
         force_kernel,
         [(3, slots), (1, 1)],

time: 56.7 us -> 49.8 us (0.88)
  starting transfers between devices: 28.3 us -> 21.8 us
  local copies, waits for them, and re-layouts: 2.75 us -> 0.01 us
  waiting for transfers between devices: 8.71 us -> 10.4 us
  Pallas kernels: 15.8 us -> 16.6 us
    ppermute x5, waiting for transfers between devices: 2.46 us -> 6.79 us  [swap_chip(): lax.ppermute(value, 'yz', [(i, (i + 1 if i % 2 else i - 1) % size) for i...]
    ppermute x5, starting transfers between devices: 16.6 us -> 13.8 us  [swap_chip(): lax.ppermute(value, 'yz', [(i, (i + 1 if i % 2 else i - 1) % size) for i...]
    unnamed x26 -> x2, local copies, waits for them, and re-layouts: 2.75 us -> 0.01 us
    ppermute x5, starting transfers between devices: 5.31 us -> 2.73 us  [partners(): lax.ppermute(value, axis, [(i, i ^ step) for i in range(size)])]
    ppermute x5, waiting for transfers between devices: 3.61 us -> 1.51 us  [partners(): lax.ppermute(value, axis, [(i, i ^ step) for i in range(size)])]
    ppermute x6 -> x5, waiting for transfers between devices: 0.95 us -> 0.01 us  [swap_core(): return lax.ppermute(value, 'yz', [(i, i ^ 1) for i in range(size)])]
    ppermute x6 -> x5, starting transfers between devices: 0.96 us -> 0.08 us  [swap_core(): return lax.ppermute(value, 'yz', [(i, i ^ 1) for i in range(size)])]
    pallas_call x9, Pallas kernels: 15.8 us -> 16.6 us  [call(): pl.pallas_call(kernel, out_shape=shapes, in_specs=[in_smem] * len(scalars...]
  transfers between devices with their start and end apart: 20 -> 19, of which waited for: 5 -> 4; matrix products, arithmetic and copies ran while one was open for 0% -> 0% of each run, Pallas kernels for 17% -> 20%
where the time goes in v3:
time: 49.8 us; the launch traced here: 49.6 us
  starting transfers between devices  21.8 us (44%)
  Pallas kernels  16.6 us (33%)
  waiting for transfers between devices  10.4 us (21%)
  between operations  0.8 us (2%)
    pallas_call x9, Pallas kernels, call(): pl.pallas_call(kernel, out_shape=shapes, in_specs=[in_smem] * len(scalars...  16.6 us
    ppermute x5, starting transfers between devices, swap_chip(): lax.ppermute(value, 'yz', [(i, (i + 1 if i % 2 else i - 1) % size) for i...  13.8 us
    ppermute x5, waiting for transfers between devices, swap_chip(): lax.ppermute(value, 'yz', [(i, (i + 1 if i % 2 else i - 1) % size) for i...  6.79 us
    ppermute x4, starting transfers between devices, shift(): lax.ppermute(value, axis, [(i, (i + by) % size) for i in range(size)])  5.2 us
    ppermute x5, starting transfers between devices, partners(): lax.ppermute(value, axis, [(i, i ^ step) for i in range(size)])  2.73 us
    ppermute x4, waiting for transfers between devices, shift(): lax.ppermute(value, axis, [(i, (i + by) % size) for i in range(size)])  2.09 us
    ppermute x5, waiting for transfers between devices, partners(): lax.ppermute(value, axis, [(i, i ^ step) for i in range(size)])  1.51 us
  transfers between devices with their start and end apart: 19, of which 4 were waited for; matrix products, arithmetic and copies ran while one was open for 0% of the time, Pallas kernels for 20%

profile of v3, /device:TPU:0, one launch (start us, length us, event | category | flops | bytes accessed | tf_op | source)
XLA Modules:
  0.0 49.6 jit_solution(3261396855517851120)
XLA Ops:
  0.6 0.7 %pack.1.own = f32[24,128]{1,0:T(8,128)S(1)} custom-call(s32[1,2]{1,0:T(1,128)} %bitcast.4, s32[2]{0:T(128)} %count_hbm.1, f32[3,256]{1,0:T(4,128)} %pos_hbm.1, s32[2,128]{1,0:T(2,128)} %bitcast.3), custom_call_target="tpu_custom_call" | custom-call | flops 1000000000 | bytes 3000000 | tf_op jit(solution)/shard_map/pack/pallas_call | solution.py:548
  1.4 5.5 %collective-permute-start.1 = (f32[24,128]{1,0:T(8,128)S(1)}, f32[24,128]{1,0:T(8,128)S(1)}, u32[]{:S(2)}, u32[]{:S(2)}) collective-permute-start(f32[24,128]{1,0:T(8,128)S(1)} %pack.1.own), channel_id=1, source_target_pairs={{0,15},{1,2},{2,1},{3,4},{4,3},{5,6},{6,5},{7,8},{8,7},{9,10},{10,... | collective-permute-start | bytes 36872 | tf_op jit(solution)/shard_map/ppermute | solution.py:567
  6.9 0.0 collective-permute-start
  6.9 2.4 %prepare.1 = (bf16[640,1536]{1,0:T(8,128)(2,1)S(1)}, bf16[384,256]{1,0:T(8,128)(2,1)S(1)}, f32[2,8,1536]{2,1,0:T(8,128)S(1)}, bf16[2,384,24]{2,1,0:T(8,128)(2,1)...) custom-call(f32[2,8]{1,0:T(2,128)} %gammas_hbm.1, ...), custom_call_target="tpu_custom_call" | custom-call | flops 3000000000 | bytes 9000000 | tf_op jit(solution)/shard_map/prepare/pallas_call | solution.py:548
  9.3 0.0 collective-permute-done.1.chip
  9.3 0.0 collective-permute-done.core
  9.3 0.1 assemble.1
  9.4 3.5 %collective-permute-start.4 = (f32[32,128]{1,0:T(8,128)S(1)}, f32[32,128]{1,0:T(8,128)S(1)}, u32[]{:S(2)}, u32[]{:S(2)}) collective-permute-start(f32[32,128]{1,0:T(8,128)S(1)} %get-tuple-element.56), channel_id=1, source_target_pairs={{0,15},{1,2},{2,1},{3,4},{4,3},{5,6},{6,5},{7,8},{8,7},{9,10},{10,... | collective-permute-start | bytes 49160 | tf_op jit(solution)/shard_map/ppermute | solution.py:567
  12.9 1.5 %collective-permute-start.2 = (f32[8,128]{1,0:T(8,128)S(1)}, f32[8,128]{1,0:T(8,128)S(1)}, u32[]{:S(2)}, u32[]{:S(2)}) collective-permute-start(f32[8,128]{1,0:T(8,128)S(1)} %get-tuple-element.54), channel_id=1, source_target_pairs={{0,16},{16,0},{1,17},{17,1},{2,18},{18,2},{3,19},{19,3},{4,20},{20... | collective-permute-start | bytes 12296 | tf_op jit(solution)/shard_map/ppermute | solution.py:572
  14.4 0.0 collective-permute-start.3
  14.4 2.1 %collective-permute-done.2.got_gx = f32[8,128]{1,0:T(8,128)S(1)} collective-permute-done((f32[8,128]{1,0:T(8,128)S(1)}, f32[8,128]{1,0:T(8,128)S(1)}, u32[]{:S(2)}, u32[]{:S(2)}) %collective-permute-start.2) | collective-permute-done | bytes 4128 | tf_op jit(solution)/shard_map/ppermute | solution.py:572
  16.5 0.0 collective-permute-done.3.got_core
  16.5 0.0 collective-permute-done.4.got_chip
  16.5 2.5 %first_layer.1 = (f32[128,384]{1,0:T(8,128)S(1)}, f32[128,384]{1,0:T(8,128)S(1)}, f32[128,128]{1,0:T(8,128)S(1)}, f32[64,128]{1,0:T(8,128)S(1)}, f32[64,128]{1,0...) custom-call(f32[8,384]{1,0:T(8,128)S(1)} %get-tuple-element.53.table, ...), custom_call_target="tpu_custom_call" | custom-call | flops 2500000000 | bytes 7500000 | tf_op jit(solution)/shard_map/first_layer/pallas_call | solution.py:548
  19.0 0.1 collective-permute-start.6
  19.1 2.3 %collective-permute-start.7 = (f32[64,128]{1,0:T(8,128)S(1)}, f32[64,128]{1,0:T(8,128)S(1)}, u32[]{:S(2)}, u32[]{:S(2)}) collective-permute-start(f32[64,128]{1,0:T(8,128)S(1)} %get-tuple-element.71), channel_id=1, source_target_pairs={{0,15},{1,2},{2,1},{3,4},{4,3},{5,6},{6,5},{7,8},{8,7},{9,10},{10,... | collective-permute-start | bytes 98312 | tf_op jit(solution)/shard_map/ppermute | solution.py:567
  21.4 1.5 %collective-permute-start.5 = (f32[128,128]{1,0:T(8,128)S(1)}, f32[128,128]{1,0:T(8,128)S(1)}, u32[]{:S(2)}, u32[]{:S(2)}) collective-permute-start(f32[128,128]{1,0:T(8,128)S(1)} %get-tuple-element.69), channel_id=1, source_target_pairs={{0,16},{16,0},{1,17},{17,1},{2,18},{18,2},{3,19},{19,3},{4,20},{20... | collective-permute-start | bytes 196616 | tf_op jit(solution)/shard_map/ppermute | solution.py:572
  22.9 0.0 copy-done
  22.9 3.1 %factors.1 = (f32[4,128,1536]{2,1,0:T(8,128)S(1)}, f32[384,1536]{1,0:T(8,128)S(1)}, f32[384,1536]{1,0:T(8,128)S(1)}, f32[64,128]{1,0:T(8,128)S(1)}) custom-call(f32[5]{0:T(128)S(1)} %copy-done, f32[8,8,1536]{2,1,0:T(8,128)S(1)} %get-tuple-element.63.geo, f32[2,8,1536]{2,1,0:T(8,128)S(1)} %get-tuple-element.58.gamma, ...), custom_call_target="tpu_custom_call" | custom-call | flops 3500000000 | bytes 10500000 | tf_op jit(solution)/shard_map/factors/pallas_call | solution.py:548
  26.1 0.0 collective-permute-done.6.got_core
  26.1 0.0 collective-permute-done.7.got_chip
  26.1 0.0 collective-permute-done.5.got_gx
  26.1 2.4 %second_layer.1 = (f32[128,1536]{1,0:T(8,128)S(1)}, f32[9,128,384]{2,1,0:T(8,128)S(1)}, f32[128,384]{1,0:T(8,128)S(1)}, f32[128,384]{1,0:T(8,128)S(1)}, f32[64,128]{1,0:T(8,128)S(1)}) custom-call(f32[64,128]{1,0:T(8,128)S(1)} %get-tuple-element.67.base, f32[8,384]{1,0:T(8,128)S(1)} %get-tuple-element.53.table, f32[128,384]{1,0:T(8,128)S(1)} %get-tuple-element.68.h_one, ...), custom_call_target="tpu_custom_call" | custom-call | flops 2500000000 | bytes 7500000 | tf_op jit(solution)/shard_map/second_layer/pallas_call | solution.py:548
  28.5 0.1 collective-permute-start.8
  28.6 3.3 %second_gradient.1 = (f32[128,384]{1,0:T(8,128)S(1)}, f32[128,128]{1,0:T(8,128)S(1)}, f32[64,128]{1,0:T(8,128)S(1)}, f32[64,128]{1,0:T(8,128)S(1)}, f32[8,640]{1,0:T(8,128)S(1)}) custom-call(f32[8,8,1536]{2,1,0:T(8,128)S(1)} %get-tuple-element.63.geo, f32[384,1536]{1,0:T(8,128)S(1)} %get-tuple-element.73.rad_ref, ...), custom_call_target="tpu_custom_call" | custom-call | flops 3500000000 | bytes 10500000 | tf_op jit(solution)/shard_map/second_gradient/pallas_call | solution.py:548
  31.9 1.5 %collective-permute-done.8 = f32[64,128]{1,0:T(8,128)S(1)} collective-permute-done((f32[64,128]{1,0:T(8,128)S(1)}, f32[64,128]{1,0:T(8,128)S(1)}, u32[]{:S(2)}, u32[]{:S(2)}) %collective-permute-start.8) | collective-permute-done | bytes 32800 | tf_op jit(solution)/shard_map/ppermute | solution.py:600
  33.4 0.0 collective-permute-start.9
  33.4 1.1 %collective-permute-start.13 = (f32[128,128]{1,0:T(8,128)S(1)}, f32[128,128]{1,0:T(8,128)S(1)}, u32[]{:S(2)}, u32[]{:S(2)}) collective-permute-start(f32[128,128]{1,0:T(8,128)S(1)} %get-tuple-element.87), channel_id=1, source_target_pairs={{0,16},{16,0},{1,17},{17,1},{2,18},{18,2},{3,19},{19,3},{4,20},{20... | collective-permute-start | bytes 196616 | tf_op jit(solution)/shard_map/ppermute | solution.py:572
  34.5 0.3 collective-permute-start.11
  34.9 0.0 collective-permute-done.9
  34.9 1.5 %collective-permute-start.10 = (f32[64,128]{1,0:T(8,128)S(1)}, f32[64,128]{1,0:T(8,128)S(1)}, u32[]{:S(2)}, u32[]{:S(2)}) collective-permute-start(f32[64,128]{1,0:T(8,128)S(1)} %add.13), channel_id=1, source_target_pairs={{0,2},{1,3},{2,0},{3,1},{4,6},{5,7},{6,4},{7,5},{8,10},{9,11},{10,... | collective-permute-start | bytes 98312 | tf_op jit(solution)/shard_map/ppermute | solution.py:600
  36.4 0.0 collective-permute-start.14
  36.4 4.2 %collective-permute-done.11.got_chip = f32[64,128]{1,0:T(8,128)S(1)} collective-permute-done((f32[64,128]{1,0:T(8,128)S(1)}, f32[64,128]{1,0:T(8,128)S(1)}, u32[]{:S(2)}, u32[]{:S(2)}) %collective-permute-start.11) | collective-permute-done | bytes 32800 | tf_op jit(solution)/shard_map/ppermute | solution.py:567
  40.5 0.0 collective-permute-done.10
  40.6 0.1 collective-permute-start.12
  40.6 0.0 collective-permute-done.14.got_core
  40.6 0.0 collective-permute-done.13.got_gx
  40.7 1.3 %first_gradient.1 = (f32[8,384]{1,0:T(8,128)S(1)}, f32[8,128]{1,0:T(8,128)S(1)}, f32[8,128]{1,0:T(8,128)S(1)}, f32[32,128]{1,0:T(8,128)S(1)}) custom-call(f32[128,384]{1,0:T(8,128)S(1)} %get-tuple-element.86.g_h, f32[128,128]{1,0:T(8,128)S(1)} %collective-permute-done.13.got_gx, f32[64,128]{1,0:T(8,128)S(1)} %collective-permute-done.14.got_core, ...), custom_call_target="tpu_custom_call" | custom-call | flops 1200000000 | bytes 3600000 | tf_op jit(solution)/shard_map/first_gradient/pallas_call | solution.py:548
  42.0 1.0 %collective-permute-start.15 = (f32[8,128]{1,0:T(8,128)S(1)}, f32[8,128]{1,0:T(8,128)S(1)}, u32[]{:S(2)}, u32[]{:S(2)}) collective-permute-start(f32[8,128]{1,0:T(8,128)S(1)} %get-tuple-element.96), channel_id=1, source_target_pairs={{0,16},{16,0},{1,17},{17,1},{2,18},{18,2},{3,19},{19,3},{4,20},{20... | collective-permute-start | bytes 12296 | tf_op jit(solution)/shard_map/ppermute | solution.py:572
  43.0 0.0 collective-permute-start.16
  43.0 2.2 %collective-permute-start.17 = (f32[32,128]{1,0:T(8,128)S(1)}, f32[32,128]{1,0:T(8,128)S(1)}, u32[]{:S(2)}, u32[]{:S(2)}) collective-permute-start(f32[32,128]{1,0:T(8,128)S(1)} %get-tuple-element.98), channel_id=1, source_target_pairs={{0,15},{1,2},{2,1},{3,4},{4,3},{5,6},{6,5},{7,8},{8,7},{9,10},{10,... | collective-permute-start | bytes 49160 | tf_op jit(solution)/shard_map/ppermute | solution.py:567
  45.1 0.0 collective-permute-done.12
  45.2 1.1 %collective-permute-start.18 = (f32[8,128]{1,0:T(8,128)S(1)}, f32[8,128]{1,0:T(8,128)S(1)}, u32[]{:S(2)}, u32[]{:S(2)}) collective-permute-start(f32[8,128]{1,0:T(8,128)S(1)} %slice_add_fusion.rest_0_), channel_id=1, source_target_pairs={{0,16},{16,0},{1,17},{17,1},{2,18},{18,2},{3,19},{19,3},{4,20},{20... | collective-permute-start | bytes 12296 | tf_op jit(solution)/shard_map/ppermute | solution.py:600
  46.2 0.0 collective-permute-done.15.got_gx
  46.2 0.0 collective-permute-done.16.got_core
  46.2 2.6 %collective-permute-done.17.got_chip = f32[32,128]{1,0:T(8,128)S(1)} collective-permute-done((f32[32,128]{1,0:T(8,128)S(1)}, f32[32,128]{1,0:T(8,128)S(1)}, u32[]{:S(2)}, u32[]{:S(2)}) %collective-permute-start.17) | collective-permute-done | bytes 16416 | tf_op jit(solution)/shard_map/ppermute | solution.py:567
  48.8 0.0 collective-permute-done.18.rest_1_
  48.9 0.8 %forces.1 = (f32[3,384]{1,0:T(4,128)}, f32[1,1]{1,0:T(1,128)}) custom-call(f32[8,384]{1,0:T(8,128)S(1)} %get-tuple-element.95.g_pos, f32[8,128]{1,0:T(8,128)S(1)} %collective-permute-done.15.got_gx, f32[8,128]{1,0:T(8,128)S(1)} %collective-permute-done.16.got_core, f32[32,128]{1,0:T(8,128)S(1)} %collective-permute-done.17.got_chip, ...), custom_call_target="tpu_custom_call" | custom-call | flops 1000000000 | bytes 3000000 | tf_op jit(solution)/shard_map/forces/pallas_call | solution.py:548
  (5 shorter events, 0.0 us)
Async XLA Ops:
  1.4 7.9 %collective-permute-start.1 = (f32[24,128]{1,0:T(8,128)S(1)}, f32[24,128]{1,0:T(8,128)S(1)}, u32[]{:S(2)}, u32[]{:S(2)}) collective-permute-start(f32[24,128]{1,0:T(8,128)S(1)} %pack.1.own), channel_id=1, source_target_pairs={{0,15},{1,2},{2,1},{3,4},{4,3},{5,6},{6,5},{7,8},{8,7},{9,10},{10,... | collective-permute-start | bytes 36872 | tf_op jit(solution)/shard_map/ppermute | solution.py:567
  6.9 2.4 %collective-permute-start = (f32[24,128]{1,0:T(8,128)S(1)}, f32[24,128]{1,0:T(8,128)S(1)}, u32[]{:S(2)}, u32[]{:S(2)}) collective-permute-start(f32[24,128]{1,0:T(8,128)S(1)} %pack.1.own), channel_id=1, source_target_pairs={{0,1},{1,0},{2,3},{3,2},{4,5},{5,4},{6,7},{7,6},{8,9},{9,8},{10,11... | collective-permute-start | bytes 36872 | tf_op jit(solution)/shard_map/ppermute | solution.py:562
  9.4 7.1 %collective-permute-start.4 = (f32[32,128]{1,0:T(8,128)S(1)}, f32[32,128]{1,0:T(8,128)S(1)}, u32[]{:S(2)}, u32[]{:S(2)}) collective-permute-start(f32[32,128]{1,0:T(8,128)S(1)} %get-tuple-element.56), channel_id=1, source_target_pairs={{0,15},{1,2},{2,1},{3,4},{4,3},{5,6},{6,5},{7,8},{8,7},{9,10},{10,... | collective-permute-start | bytes 49160 | tf_op jit(solution)/shard_map/ppermute | solution.py:567
  12.9 3.6 %collective-permute-start.2 = (f32[8,128]{1,0:T(8,128)S(1)}, f32[8,128]{1,0:T(8,128)S(1)}, u32[]{:S(2)}, u32[]{:S(2)}) collective-permute-start(f32[8,128]{1,0:T(8,128)S(1)} %get-tuple-element.54), channel_id=1, source_target_pairs={{0,16},{16,0},{1,17},{17,1},{2,18},{18,2},{3,19},{19,3},{4,20},{20... | collective-permute-start | bytes 12296 | tf_op jit(solution)/shard_map/ppermute | solution.py:572
  14.4 2.1 %collective-permute-start.3 = (f32[8,128]{1,0:T(8,128)S(1)}, f32[8,128]{1,0:T(8,128)S(1)}, u32[]{:S(2)}, u32[]{:S(2)}) collective-permute-start(f32[8,128]{1,0:T(8,128)S(1)} %get-tuple-element.55), channel_id=1, source_target_pairs={{0,1},{1,0},{2,3},{3,2},{4,5},{5,4},{6,7},{7,6},{8,9},{9,8},{10,11... | collective-permute-start | bytes 12296 | tf_op jit(solution)/shard_map/ppermute | solution.py:562
  16.5 6.4 %copy-start = (f32[5]{0:T(128)S(1)}, f32[5]{0:T(128)}, u32[]{:S(2)}) copy-start(f32[5]{0:T(128)} %atom_ref.1) | copy-start | bytes 64
  19.0 7.1 %collective-permute-start.6 = (f32[64,128]{1,0:T(8,128)S(1)}, f32[64,128]{1,0:T(8,128)S(1)}, u32[]{:S(2)}, u32[]{:S(2)}) collective-permute-start(f32[64,128]{1,0:T(8,128)S(1)} %get-tuple-element.70), channel_id=1, source_target_pairs={{0,1},{1,0},{2,3},{3,2},{4,5},{5,4},{6,7},{7,6},{8,9},{9,8},{10,11... | collective-permute-start | bytes 98312 | tf_op jit(solution)/shard_map/ppermute | solution.py:562
  19.1 7.0 %collective-permute-start.7 = (f32[64,128]{1,0:T(8,128)S(1)}, f32[64,128]{1,0:T(8,128)S(1)}, u32[]{:S(2)}, u32[]{:S(2)}) collective-permute-start(f32[64,128]{1,0:T(8,128)S(1)} %get-tuple-element.71), channel_id=1, source_target_pairs={{0,15},{1,2},{2,1},{3,4},{4,3},{5,6},{6,5},{7,8},{8,7},{9,10},{10,... | collective-permute-start | bytes 98312 | tf_op jit(solution)/shard_map/ppermute | solution.py:567
  21.4 4.7 %collective-permute-start.5 = (f32[128,128]{1,0:T(8,128)S(1)}, f32[128,128]{1,0:T(8,128)S(1)}, u32[]{:S(2)}, u32[]{:S(2)}) collective-permute-start(f32[128,128]{1,0:T(8,128)S(1)} %get-tuple-element.69), channel_id=1, source_target_pairs={{0,16},{16,0},{1,17},{17,1},{2,18},{18,2},{3,19},{19,3},{4,20},{20... | collective-permute-start | bytes 196616 | tf_op jit(solution)/shard_map/ppermute | solution.py:572
  28.5 4.9 %collective-permute-start.8 = (f32[64,128]{1,0:T(8,128)S(1)}, f32[64,128]{1,0:T(8,128)S(1)}, u32[]{:S(2)}, u32[]{:S(2)}) collective-permute-start(f32[64,128]{1,0:T(8,128)S(1)} %get-tuple-element.75), channel_id=1, source_target_pairs={{0,8},{1,9},{2,10},{3,11},{4,12},{5,13},{6,14},{7,15},{8,0},{9,1},... | collective-permute-start | bytes 98312 | tf_op jit(solution)/shard_map/ppermute | solution.py:600
  33.4 1.5 %collective-permute-start.9 = (f32[64,128]{1,0:T(8,128)S(1)}, f32[64,128]{1,0:T(8,128)S(1)}, u32[]{:S(2)}, u32[]{:S(2)}) collective-permute-start(f32[64,128]{1,0:T(8,128)S(1)} %add.12), channel_id=1, source_target_pairs={{0,1},{1,0},{2,3},{3,2},{4,5},{5,4},{6,7},{7,6},{8,9},{9,8},{10,11... | collective-permute-start | bytes 98312 | tf_op jit(solution)/shard_map/ppermute | solution.py:600
  33.4 7.3 %collective-permute-start.13 = (f32[128,128]{1,0:T(8,128)S(1)}, f32[128,128]{1,0:T(8,128)S(1)}, u32[]{:S(2)}, u32[]{:S(2)}) collective-permute-start(f32[128,128]{1,0:T(8,128)S(1)} %get-tuple-element.87), channel_id=1, source_target_pairs={{0,16},{16,0},{1,17},{17,1},{2,18},{18,2},{3,19},{19,3},{4,20},{20... | collective-permute-start | bytes 196616 | tf_op jit(solution)/shard_map/ppermute | solution.py:572
  34.5 6.0 %collective-permute-start.11 = (f32[64,128]{1,0:T(8,128)S(1)}, f32[64,128]{1,0:T(8,128)S(1)}, u32[]{:S(2)}, u32[]{:S(2)}) collective-permute-start(f32[64,128]{1,0:T(8,128)S(1)} %get-tuple-element.84), channel_id=1, source_target_pairs={{0,15},{1,2},{2,1},{3,4},{4,3},{5,6},{6,5},{7,8},{8,7},{9,10},{10,... | collective-permute-start | bytes 98312 | tf_op jit(solution)/shard_map/ppermute | solution.py:567
  34.9 5.7 %collective-permute-start.10 = (f32[64,128]{1,0:T(8,128)S(1)}, f32[64,128]{1,0:T(8,128)S(1)}, u32[]{:S(2)}, u32[]{:S(2)}) collective-permute-start(f32[64,128]{1,0:T(8,128)S(1)} %add.13), channel_id=1, source_target_pairs={{0,2},{1,3},{2,0},{3,1},{4,6},{5,7},{6,4},{7,5},{8,10},{9,11},{10,... | collective-permute-start | bytes 98312 | tf_op jit(solution)/shard_map/ppermute | solution.py:600
  36.4 4.3 %collective-permute-start.14 = (f32[64,128]{1,0:T(8,128)S(1)}, f32[64,128]{1,0:T(8,128)S(1)}, u32[]{:S(2)}, u32[]{:S(2)}) collective-permute-start(f32[64,128]{1,0:T(8,128)S(1)} %get-tuple-element.88), channel_id=1, source_target_pairs={{0,1},{1,0},{2,3},{3,2},{4,5},{5,4},{6,7},{7,6},{8,9},{9,8},{10,11... | collective-permute-start | bytes 98312 | tf_op jit(solution)/shard_map/ppermute | solution.py:562
  40.6 4.6 %collective-permute-start.12 = (f32[64,128]{1,0:T(8,128)S(1)}, f32[64,128]{1,0:T(8,128)S(1)}, u32[]{:S(2)}, u32[]{:S(2)}) collective-permute-start(f32[64,128]{1,0:T(8,128)S(1)} %add.14), channel_id=1, source_target_pairs={{0,4},{1,5},{2,6},{3,7},{4,0},{5,1},{6,2},{7,3},{8,12},{9,13},{10,... | collective-permute-start | bytes 98312 | tf_op jit(solution)/shard_map/ppermute | solution.py:600
  42.0 4.3 %collective-permute-start.15 = (f32[8,128]{1,0:T(8,128)S(1)}, f32[8,128]{1,0:T(8,128)S(1)}, u32[]{:S(2)}, u32[]{:S(2)}) collective-permute-start(f32[8,128]{1,0:T(8,128)S(1)} %get-tuple-element.96), channel_id=1, source_target_pairs={{0,16},{16,0},{1,17},{17,1},{2,18},{18,2},{3,19},{19,3},{4,20},{20... | collective-permute-start | bytes 12296 | tf_op jit(solution)/shard_map/ppermute | solution.py:572
  43.0 3.2 %collective-permute-start.16 = (f32[8,128]{1,0:T(8,128)S(1)}, f32[8,128]{1,0:T(8,128)S(1)}, u32[]{:S(2)}, u32[]{:S(2)}) collective-permute-start(f32[8,128]{1,0:T(8,128)S(1)} %get-tuple-element.97), channel_id=1, source_target_pairs={{0,1},{1,0},{2,3},{3,2},{4,5},{5,4},{6,7},{7,6},{8,9},{9,8},{10,11... | collective-permute-start | bytes 12296 | tf_op jit(solution)/shard_map/ppermute | solution.py:562
  43.0 5.9 %collective-permute-start.17 = (f32[32,128]{1,0:T(8,128)S(1)}, f32[32,128]{1,0:T(8,128)S(1)}, u32[]{:S(2)}, u32[]{:S(2)}) collective-permute-start(f32[32,128]{1,0:T(8,128)S(1)} %get-tuple-element.98), channel_id=1, source_target_pairs={{0,15},{1,2},{2,1},{3,4},{4,3},{5,6},{6,5},{7,8},{8,7},{9,10},{10,... | collective-permute-start | bytes 49160 | tf_op jit(solution)/shard_map/ppermute | solution.py:567
  45.2 3.7 %collective-permute-start.18 = (f32[8,128]{1,0:T(8,128)S(1)}, f32[8,128]{1,0:T(8,128)S(1)}, u32[]{:S(2)}, u32[]{:S(2)}) collective-permute-start(f32[8,128]{1,0:T(8,128)S(1)} %slice_add_fusion.rest_0_), channel_id=1, source_target_pairs={{0,16},{16,0},{1,17},{17,1},{2,18},{18,2},{3,19},{19,3},{4,20},{20... | collective-permute-start | bytes 12296 | tf_op jit(solution)/shard_map/ppermute | solution.py:600

commit v4 on v3

--- a/solution.py
+++ b/solution.py
@@ -94,11 +94,6 @@
 def faces_yz(core, chip):
     before, after = previous_and_next(core, chip)
     return jnp.where(left_half(core.shape), before, after)
-
-
-def returned_yz(core, chip):
-    before, after = previous_and_next(core, chip)
-    return jnp.where(left_half(core.shape), after, before)
 
 
 def pack_halves(value):
@@ -372,16 +367,15 @@
     send_chip[...] = jnp.where(even, to_previous, to_next)
 
 
-def factor_kernel(
-    atom_ref, geo, gamma, radials, table, rad_ref, feat_ref, fields_ref,
-    factors, rad_two, slope_two, base,
-    slope_ref,
+def radial_kernel(
+    atom_ref, geo, gamma, radials, table, h_one, onehot, weights,
+    rad_two, slope_one, slope_two, base, found_two,
 ):
     square = geo[SQUARE]
     basis = jnp.exp(-gamma[1] * square)
     rad_two[...] = matmul(radials[1], stacked_rows(basis))
     slope_two[...] = matmul(radials[1], stacked_rows(-gamma[1] * basis))
-    slope_ref[...] = matmul(radials[0], stacked_rows(-gamma[0] * jnp.exp(-gamma[0] * square)))
+    slope_one[...] = matmul(radials[0], stacked_rows(-gamma[0] * jnp.exp(-gamma[0] * square)))
     code = table[3:4, :]
     live = jnp.where(code >= 0.0, 1.0, 0.0)
     energy = jnp.zeros(code.shape, f32)
@@ -391,8 +385,22 @@
     base[...] = jnp.zeros(base.shape, f32)
     base[0:1, :] = fold(energy)
     base[1:2, :] = fold(live)
+    channels, slots = h_one.shape
+    projected = matmul(weights[1], stacked_right(h_one[...]))
+    both = matmul(jnp.concatenate(split2(projected), axis=0), onehot[0:slots, :])
+    found_two[...] = both[0:channels] + both[channels : 2 * channels]
+
+
+def factor_kernel(
+    geo, rad_ref, slope_ref, feat_ref, fields_ref, left, onehot_t, weights, g_own,
+    factors, g_h, g_pos,
+):
     channels, slots = fields_ref.shape[1:]
     entries = feat_ref.shape[1] // slots
+    scattered = matmul(left[...], onehot_t[:, 0:slots])
+    g_proj = scattered[0:channels] + scattered[channels : 2 * channels]
+    g_pos[...] = whole(scattered[2 * channels : 2 * channels + 3 * ROWS])
+    g_h[...] = matmul(weights[4], stacked_right(g_proj)) + g_own[...]
     for lanes, edges in lane_parts(slots, entries):
         units = [[geo[U + d, :, edges[k]] for d in range(3)] for k in range(entries)]
 
@@ -415,18 +423,17 @@
 
 
 def second_layer_kernel(
-    base, table, h_one, got_gx, got_core, got_chip, onehot, y_ref, rad_ref, weights, reads,
+    base, table, h_one, got_gx, got_core, got_chip, onehot, y_ref, rad_ref, weights, reads, found_two,
     feat_ref, fields_ref, g_ref, g_own, tally,
     inv_ref,
 ):
-    slots = table.shape[1]
     h_local = h_one[...]
-    channels = h_local.shape[0]
+    channels, slots = h_local.shape
     before, after = previous_and_next(got_core[...], got_chip[...])
-    h_ext = jnp.concatenate([h_local, got_gx[...], join_halves(before, after)], axis=1)
-    projected = matmul(weights[1], stacked_right(h_ext))
-    both = matmul(jnp.concatenate(split2(projected), axis=0), onehot[...])
-    feat_ref[...] = both[0:channels] + both[channels : 2 * channels]
+    ghosts = jnp.concatenate([got_gx[...], join_halves(before, after)], axis=1)
+    projected = matmul(weights[1], stacked_right(ghosts))
+    both = matmul(jnp.concatenate(split2(projected), axis=0), onehot[slots:, :])
+    feat_ref[...] = found_two[...] + (both[0:channels] + both[channels : 2 * channels])
     gather_sums(y_ref, rad_ref, feat_ref, fields_ref, inv_ref)
     mixed = matmul(weights[2], stacked_right(inv_ref[...]))
     live = jnp.where(table[3:4, :] >= 0.0, 1.0, 0.0)
@@ -440,14 +447,11 @@
 
 
 def second_gradient_kernel(
-    geo, rad_ref, slope_ref, feat_ref, fields_ref, g_ref, g_own, onehot_t, weights,
-    g_h, send_gx, send_core, send_chip, g_pos,
+    geo, rad_ref, slope_ref, feat_ref, fields_ref, g_ref,
     g_feat, g_off,
 ):
     channels, slots = g_ref.shape
-    wide = onehot_t.shape[1]
-    edge_count = feat_ref.shape[1]
-    entries = edge_count // slots
+    entries = feat_ref.shape[1] // slots
     g_off[...] = jnp.zeros(g_off.shape, f32)
     for lanes, edges in lane_parts(slots, entries):
         units = [[geo[U + d, :, edges[k]] for d in range(3)] for k in range(entries)]
@@ -478,26 +482,30 @@
         for k in range(entries):
             for d, item in enumerate(offset_gradients(found[4 * k : 4 * k + 4], geo, edges[k])):
                 g_off[d : d + 1, edges[k]] = item
-    high, low = split2(g_feat[...])
-    left = jnp.concatenate([high, low, pieces(g_off[...])], axis=0)
-    scattered = matmul(left, onehot_t[...])
+
+
+def ghost_gradient_kernel(g_feat, g_off, onehot_t, weights, left, send_gx, send_core, send_chip, g_ghost, g_target):
+    channels, edge_count = g_feat.shape
+    wide = onehot_t.shape[1]
+    slots = g_target.shape[1]
+    entries = edge_count // slots
+    stacked = jnp.concatenate([*split2(g_feat[...]), pieces(g_off[...])], axis=0)
+    left[...] = stacked
+    scattered = matmul(stacked, onehot_t[:, slots:wide])
     g_proj = scattered[0:channels] + scattered[channels : 2 * channels]
-    g_ext = whole(scattered[2 * channels : 2 * channels + 3 * ROWS])
+    g_ghost[...] = whole(scattered[2 * channels : 2 * channels + 3 * ROWS])
     g_all = matmul(weights[4], stacked_right(g_proj))
-    g_h[...] = g_all[:, 0:slots] + g_own[...]
-    send_gx[...] = g_all[:, slots : slots + LANES]
-    to_previous, to_next = pack_halves(g_all[:, slots + LANES : slots + 2 * LANES])
+    send_gx[...] = g_all[:, 0:LANES]
+    to_previous, to_next = pack_halves(g_all[:, LANES : 2 * LANES])
     even = is_even()
     send_core[...] = jnp.where(even, to_next, to_previous)
     send_chip[...] = jnp.where(even, to_previous, to_next)
-    own = sum(g_off[:, k * slots : (k + 1) * slots] for k in range(entries))
-    g_pos[:, 0:slots] = g_ext[:, 0:slots] - own
-    g_pos[:, slots:wide] = g_ext[:, slots:wide]
+    g_target[...] = sum(g_off[:, k * slots : (k + 1) * slots] for k in range(entries))
 
 
 def first_gradient_kernel(
-    g_h, got_gx, got_core, got_chip, slope, factors, geo, g_pos_two, onehot_t, send_t, weights,
-    g_pos, send_gx, send_core, send_chip,
+    g_h, got_gx, got_core, got_chip, slope, factors, geo, g_ghost, onehot_t, send_t, weights,
+    left, g_target, send_gx, send_core, send_chip,
     g_ref, g_off,
 ):
     channels, slots = slope.shape
@@ -522,20 +530,36 @@
         for k in range(entries):
             for d, item in enumerate(offset_gradients(found[4 * k : 4 * k + 4], geo, edges[k])):
                 g_off[d : d + 1, edges[k]] = item
-    g_ext = whole(matmul(pieces(g_off[...]), onehot_t[...])) + g_pos_two[...]
-    own = sum(g_off[:, k * slots : (k + 1) * slots] for k in range(entries))
-    g_pos[...] = g_ext[:, 0:slots] - own
-    send_gx[...] = g_ext[:, slots : slots + LANES]
-    send_core[...] = g_ext[:, slots + LANES : slots + 2 * LANES]
-    send_chip[...] = jnp.zeros(send_chip.shape, f32)
-    send_chip[0:ROWS, :] = g_ext[:, slots + LANES : slots + 2 * LANES]
-
-
-def force_kernel(g_pos, got_gx, got_core, got_chip, send_t, *rest):
+    wide = onehot_t.shape[1]
+    stacked = pieces(g_off[...])
+    left[...] = stacked
+    g_ext = whole(matmul(stacked, onehot_t[:, slots:wide])) + g_ghost[...]
+    for out, piece in ((send_gx, 0), (send_core, 1), (send_chip, 1)):
+        out[...] = jnp.zeros(out.shape, f32)
+        out[0:ROWS, :] = g_ext[:, piece * LANES : (piece + 1) * LANES]
+    g_target[...] = sum(g_off[:, k * slots : (k + 1) * slots] for k in range(entries))
+
+
+def local_kernel(left, onehot_t, g_local_two, g_target_two, g_target_one, g_pos):
+    slots = g_pos.shape[1]
+    g_pos[...] = whole(matmul(left[...], onehot_t[:, 0:slots])) + g_local_two[...] - g_target_two[...] - g_target_one[...]
+
+
+def chip_force_kernel(g_pos, got_chip, send_t, g_sum):
+    half = left_half((ROWS, LANES))
+    wanted = jnp.where(is_even(), 1.0, 0.0)
+    kept = got_chip[0:ROWS, :] * jnp.where(half, 1.0 - wanted, wanted)
+    ghosts = send_t.shape[0]
+    g_sum[...] = g_pos[...] + whole(matmul(pieces(kept), send_t[ghosts - LANES : ghosts, :]))
+
+
+def force_kernel(g_sum, got_gx, got_core, send_t, *rest):
     tallies, (forces, energy) = rest[:-2], rest[-2:]
-    back = jnp.concatenate([got_gx[...], returned_yz(got_core[...], got_chip[0:ROWS, :])], axis=1)
-    total = g_pos[...] + whole(matmul(pieces(back), send_t[...]))
-    forces[...] = -total[0:3]
+    half = left_half((ROWS, LANES))
+    wanted = jnp.where(is_even(), 0.0, 1.0)
+    kept = got_core[0:ROWS, :] * jnp.where(half, 1.0 - wanted, wanted)
+    back = jnp.concatenate([got_gx[0:ROWS, :], kept], axis=1)
+    forces[...] = -(g_sum[...] + whole(matmul(pieces(back), send_t[...])))[0:3]
     sums = jnp.sum(sum(item[0:2, :] for item in tallies), axis=1, keepdims=True)
     energy[...] = sums[0:1, :] / sums[1:2, :]
 
@@ -709,66 +733,95 @@
     got_chip = swap_chip(send_chip)
     got_gx = swap_gx(send_gx)
     got_core = swap_core(send_core)
-    factors, rad_two, slope_two, base = call(
-        factor_kernel,
-        [(4, channels, edges), (rows, edges), (rows, edges), (TALL, LANES)],
+    rad_two, slope_one, slope_two, base, found_two = call(
+        radial_kernel,
+        [(rows, edges), (rows, edges), (rows, edges), (TALL, LANES), (channels, edges)],
         [atom_ref],
-        [geo, gamma, radials, table, rad_one, feat_one, fields_one],
-        [(rows, edges)],
-        name="factors",
-        us=3.5,
+        [geo, gamma, radials, table, h_one, onehot, weights],
+        name="radials",
+        us=2.0,
     )
     feat_two, fields_two, g_two, g_own, tally = call(
         second_layer_kernel,
         [(channels, edges), fields_shape, flat, flat, (TALL, LANES)],
         [],
-        [base, table, h_one, got_gx, got_core, got_chip, onehot, angular, rad_two, weights, reads],
+        [base, table, h_one, got_gx, got_core, got_chip, onehot, angular, rad_two, weights, reads, found_two],
         [flat],
         name="second_layer",
         us=2.5,
     )
     bits = (lax.axis_size("yz") - 1).bit_length()
+    got_sums = partners(tally, "yz", [0])
+    g_feat, g_off = call(
+        second_gradient_kernel,
+        [(channels, edges), (ROWS, edges)],
+        [],
+        [geo, rad_two, slope_two, feat_two, fields_two, g_two],
+        name="second_gradient",
+        us=2.5,
+    )
+    got_sums, g_off = together(got_sums, g_off)
+    tally = sum(got_sums, tally)
     got_sums = partners(tally, "yz", [bits - 1] if bits > 1 else [])
-    g_h, send_gx, send_core, send_chip, g_pos_two = call(
-        second_gradient_kernel,
-        [flat, square, half, half, (ROWS, wide)],
-        [],
-        [geo, rad_two, slope_two, feat_two, fields_two, g_two, g_own, onehot_t, weights],
-        [(channels, edges), (ROWS, edges)],
-        name="second_gradient",
-        us=3.5,
-    )
-    got_sums, g_pos_two = together(got_sums, g_pos_two)
-    tally = sum(got_sums, tally)
-    got_chip = swap_chip(send_chip)
-    got_gx = return_gx(send_gx)
-    got_core = swap_core(send_core)
-    tally = sum(partners(tally, "yz", [0]), tally)
-    got_sums = partners(tally, "yz", [1] if bits > 2 else [])
-    got_sums, got_chip = together(got_sums, got_chip)
-    tally = sum(got_sums, tally)
-    got_sums = partners(tally, "yz", range(2, bits - 1))
-    g_pos, send_gx, send_core, send_chip = call(
-        first_gradient_kernel,
-        [(ROWS, slots), small, small, tall],
-        [],
-        [g_h, got_gx, got_core, got_chip, slope, factors, geo, g_pos_two, onehot_t, send_t, weights],
-        [flat, (ROWS, edges)],
-        name="first_gradient",
-        us=1.2,
-    )
-    got_sums, g_pos = together(got_sums, g_pos)
+    left, send_gx, send_core, send_chip, g_ghost, g_target_two = call(
+        ghost_gradient_kernel,
+        [((2 * channels + 3 * ROWS, edges), bf16), square, half, half, (ROWS, ghosts), (ROWS, slots)],
+        [],
+        [g_feat, g_off, onehot_t, weights],
+        name="ghost_gradient",
+        us=1.5,
+    )
+    got_sums, g_ghost = together(got_sums, g_ghost)
     tally = sum(got_sums, tally)
     got_chip = swap_chip(send_chip)
     got_gx = return_gx(send_gx)
     got_core = swap_core(send_core)
     tally = tally[:ROWS]
+    got_sums = partners(tally, "yz", [1] if bits > 2 else [])
+    factors, g_h, g_local_two = call(
+        factor_kernel,
+        [(4, channels, edges), flat, (ROWS, slots)],
+        [],
+        [geo, rad_one, slope_one, feat_one, fields_one, left, onehot_t, weights, g_own],
+        name="factors",
+        us=3.0,
+    )
+    got_sums, got_chip = together(got_sums, got_chip)
+    tally = sum(got_sums, tally)
+    tally = jnp.pad(tally, ((0, TALL - ROWS), (0, 0)))
+    got_sums = partners(tally, "yz", range(2, bits - 1))
+    left, g_target_one, send_gx, send_core, send_chip = call(
+        first_gradient_kernel,
+        [((3 * ROWS, edges), bf16), (ROWS, slots), (8, LANES), (8, LANES), (8, LANES)],
+        [],
+        [g_h, got_gx, got_core, got_chip, slope, factors, geo, g_ghost, onehot_t, send_t, weights],
+        [flat, (ROWS, edges)],
+        name="first_gradient",
+        us=1.2,
+    )
+    got_sums, left = together(got_sums, left)
+    tally = sum(got_sums, tally)
+    got_chip = swap_chip(send_chip)
+    got_gx = return_gx(send_gx)
+    got_core = swap_core(send_core)
+    (g_pos,) = call(
+        local_kernel,
+        [(ROWS, slots)],
+        [],
+        [left, onehot_t, g_local_two, g_target_two, g_target_one],
+        name="local",
+        us=0.5,
+    )
+    tally = tally[:ROWS]
     tallies = [tally] + partners(tally, "gx", range((lax.axis_size("gx") - 1).bit_length()))
+    (g_sum,) = call(
+        chip_force_kernel, [(ROWS, slots)], [], [g_pos, got_chip, send_t], name="chip_forces", us=0.1
+    )
     forces, energy = call(
         force_kernel,
         [(3, slots), (1, 1)],
         [],
-        [g_pos, got_gx, got_core, got_chip, send_t] + tallies,
+        [g_sum, got_gx, got_core, send_t] + tallies,
         name="forces",
     )
     return (forces, energy.reshape(()))

time: 49.8 us -> 48 us (0.964)
  waiting for transfers between devices: 10.4 us -> 6.86 us
  Pallas kernels: 16.6 us -> 17.5 us
  starting transfers between devices: 21.8 us -> 22.5 us
    ppermute x5, waiting for transfers between devices: 6.79 us -> 2.52 us  [swap_chip(): lax.ppermute(value, 'yz', [(i, (i + 1 if i % 2 else i - 1) % size) for i...]
    pallas_call x9 -> x13, Pallas kernels: 16.6 us -> 17.5 us  [call(): pl.pallas_call(kernel, out_shape=shapes, in_specs=[in_smem] * len(scalars...]
    ppermute x5, starting transfers between devices: 2.73 us -> 3.25 us  [partners(): lax.ppermute(value, axis, [(i, i ^ step) for i in range(size)])]
  transfers between devices with their start and end apart: 19 -> 19, of which waited for: 4 -> 6; matrix products, arithmetic and copies ran while one was open for 0% -> 0% of each run, Pallas kernels for 20% -> 24%
where the time goes in v4:
time: 48 us; the launch traced here: 47.8 us
  starting transfers between devices  22.5 us (47%)
  Pallas kernels  17.5 us (36%)
  waiting for transfers between devices  6.86 us (14%)
  between operations  0.82 us (2%)
    pallas_call x13, Pallas kernels, call(): pl.pallas_call(kernel, out_shape=shapes, in_specs=[in_smem] * len(scalars...  17.5 us
    ppermute x5, starting transfers between devices, swap_chip(): lax.ppermute(value, 'yz', [(i, (i + 1 if i % 2 else i - 1) % size) for i...  13.8 us
    ppermute x4, starting transfers between devices, shift(): lax.ppermute(value, axis, [(i, (i + by) % size) for i in range(size)])  5.04 us
    ppermute x5, starting transfers between devices, partners(): lax.ppermute(value, axis, [(i, i ^ step) for i in range(size)])  3.25 us
    ppermute x4, waiting for transfers between devices, shift(): lax.ppermute(value, axis, [(i, (i + by) % size) for i in range(size)])  2.57 us
    ppermute x5, waiting for transfers between devices, swap_chip(): lax.ppermute(value, 'yz', [(i, (i + 1 if i % 2 else i - 1) % size) for i...  2.52 us
    ppermute x5, waiting for transfers between devices, partners(): lax.ppermute(value, axis, [(i, i ^ step) for i in range(size)])  1.76 us
  transfers between devices with their start and end apart: 19, of which 6 were waited for; matrix products, arithmetic and copies ran while one was open for 0% of the time, Pallas kernels for 24%

profile of v4, /device:TPU:0, one launch (start us, length us, event | category | flops | bytes accessed | tf_op | source)
XLA Modules:
  0.0 47.8 jit_solution(5532145429595871647)
XLA Ops:
  0.6 0.7 %pack.1.own = f32[24,128]{1,0:T(8,128)S(1)} custom-call(s32[1,2]{1,0:T(1,128)} %bitcast.4, s32[2]{0:T(128)} %count_hbm.1, f32[3,256]{1,0:T(4,128)} %pos_hbm.1, s32[2,128]{1,0:T(2,128)} %bitcast.3), custom_call_target="tpu_custom_call" | custom-call | flops 1000000000 | bytes 3000000 | tf_op jit(solution)/shard_map/pack/pallas_call | solution.py:572
  1.4 5.5 %collective-permute-start.1 = (f32[24,128]{1,0:T(8,128)S(1)}, f32[24,128]{1,0:T(8,128)S(1)}, u32[]{:S(2)}, u32[]{:S(2)}) collective-permute-start(f32[24,128]{1,0:T(8,128)S(1)} %pack.1.own), channel_id=1, source_target_pairs={{0,15},{1,2},{2,1},{3,4},{4,3},{5,6},{6,5},{7,8},{8,7},{9,10},{10,... | collective-permute-start | bytes 36872 | tf_op jit(solution)/shard_map/ppermute | solution.py:591
  6.9 0.0 collective-permute-start
  6.9 2.4 %prepare.1 = (bf16[640,1536]{1,0:T(8,128)(2,1)S(1)}, bf16[384,256]{1,0:T(8,128)(2,1)S(1)}, f32[2,8,1536]{2,1,0:T(8,128)S(1)}, bf16[2,384,24]{2,1,0:T(8,128)(2,1)...) custom-call(f32[2,8]{1,0:T(2,128)} %gammas_hbm.1, ...), custom_call_target="tpu_custom_call" | custom-call | flops 3000000000 | bytes 9000000 | tf_op jit(solution)/shard_map/prepare/pallas_call | solution.py:572
  9.3 0.0 collective-permute-done.1.chip
  9.3 0.0 collective-permute-done.core
  9.3 0.1 assemble.1
  9.4 3.5 %collective-permute-start.4 = (f32[32,128]{1,0:T(8,128)S(1)}, f32[32,128]{1,0:T(8,128)S(1)}, u32[]{:S(2)}, u32[]{:S(2)}) collective-permute-start(f32[32,128]{1,0:T(8,128)S(1)} %get-tuple-element.66), channel_id=1, source_target_pairs={{0,15},{1,2},{2,1},{3,4},{4,3},{5,6},{6,5},{7,8},{8,7},{9,10},{10,... | collective-permute-start | bytes 49160 | tf_op jit(solution)/shard_map/ppermute | solution.py:591
  12.9 1.5 %collective-permute-start.2 = (f32[8,128]{1,0:T(8,128)S(1)}, f32[8,128]{1,0:T(8,128)S(1)}, u32[]{:S(2)}, u32[]{:S(2)}) collective-permute-start(f32[8,128]{1,0:T(8,128)S(1)} %get-tuple-element.64), channel_id=1, source_target_pairs={{0,16},{16,0},{1,17},{17,1},{2,18},{18,2},{3,19},{19,3},{4,20},{20... | collective-permute-start | bytes 12296 | tf_op jit(solution)/shard_map/ppermute | solution.py:596
  14.4 0.0 collective-permute-start.3
  14.4 2.1 %collective-permute-done.2.got_gx = f32[8,128]{1,0:T(8,128)S(1)} collective-permute-done((f32[8,128]{1,0:T(8,128)S(1)}, f32[8,128]{1,0:T(8,128)S(1)}, u32[]{:S(2)}, u32[]{:S(2)}) %collective-permute-start.2) | collective-permute-done | bytes 4128 | tf_op jit(solution)/shard_map/ppermute | solution.py:596
  16.5 0.0 collective-permute-done.3.got_core
  16.5 0.0 collective-permute-done.4.got_chip
  16.5 2.5 %first_layer.1 = (f32[128,384]{1,0:T(8,128)S(1)}, f32[128,384]{1,0:T(8,128)S(1)}, f32[128,128]{1,0:T(8,128)S(1)}, f32[64,128]{1,0:T(8,128)S(1)}, f32[64,128]{1,0...) custom-call(f32[8,384]{1,0:T(8,128)S(1)} %get-tuple-element.63.table, ...), custom_call_target="tpu_custom_call" | custom-call | flops 2500000000 | bytes 7500000 | tf_op jit(solution)/shard_map/first_layer/pallas_call | solution.py:572
  19.0 0.1 collective-permute-start.6
  19.1 2.3 %collective-permute-start.7 = (f32[64,128]{1,0:T(8,128)S(1)}, f32[64,128]{1,0:T(8,128)S(1)}, u32[]{:S(2)}, u32[]{:S(2)}) collective-permute-start(f32[64,128]{1,0:T(8,128)S(1)} %get-tuple-element.78), channel_id=1, source_target_pairs={{0,15},{1,2},{2,1},{3,4},{4,3},{5,6},{6,5},{7,8},{8,7},{9,10},{10,... | collective-permute-start | bytes 98312 | tf_op jit(solution)/shard_map/ppermute | solution.py:591
  21.4 1.5 %collective-permute-start.5 = (f32[128,128]{1,0:T(8,128)S(1)}, f32[128,128]{1,0:T(8,128)S(1)}, u32[]{:S(2)}, u32[]{:S(2)}) collective-permute-start(f32[128,128]{1,0:T(8,128)S(1)} %get-tuple-element.76), channel_id=1, source_target_pairs={{0,16},{16,0},{1,17},{17,1},{2,18},{18,2},{3,19},{19,3},{4,20},{20... | collective-permute-start | bytes 196616 | tf_op jit(solution)/shard_map/ppermute | solution.py:596
  22.9 2.2 %radials.1 = (f32[384,1536]{1,0:T(8,128)S(1)}, f32[384,1536]{1,0:T(8,128)S(1)}, f32[384,1536]{1,0:T(8,128)S(1)}, f32[64,128]{1,0:T(8,128)S(1)}, f32[128,1536]{1,0:T(8,128)S(1)}) custom-call(f32[5]{0:T(128)S(1)} %copy-done, f32[8,8,1536]{2,1,0:T(8,128)S(1)} %get-tuple-element.73.geo, f32[2,8,1536]{2,1,0:T(8,128)S(1)} %get-tuple-element.68.gamma, ...), custom_call_target="tpu_custom_call" | custom-call | flops 2000000000 | bytes 6000000 | tf_op jit(solution)/shard_map/radials/pallas_call | solution.py:572
  25.1 0.0 collective-permute-done.6.got_core
  25.1 0.1 collective-permute-done.7.got_chip
  25.2 0.5 %collective-permute-done.5.got_gx = f32[128,128]{1,0:T(8,128)S(1)} collective-permute-done((f32[128,128]{1,0:T(8,128)S(1)}, f32[128,128]{1,0:T(8,128)S(1)}, u32[]{:S(2)}, u32[]{:S(2)}) %collective-permute-start.5) | collective-permute-done | bytes 65568 | tf_op jit(solution)/shard_map/ppermute | solution.py:596
  25.7 2.0 %second_layer.1 = (f32[128,1536]{1,0:T(8,128)S(1)}, f32[9,128,384]{2,1,0:T(8,128)S(1)}, f32[128,384]{1,0:T(8,128)S(1)}, f32[128,384]{1,0:T(8,128)S(1)}, f32[64,128]{1,0:T(8,128)S(1)}) custom-call(f32[64,128]{1,0:T(8,128)S(1)} %get-tuple-element.75.base, f32[8,384]{1,0:T(8,128)S(1)} %get-tuple-element.63.table, f32[128,384]{1,0:T(8,128)S(1)} %get-tuple-element.74.h_one, ...), custom_call_target="tpu_custom_call" | custom-call | flops 2500000000 | bytes 7500000 | tf_op jit(solution)/shard_map/second_layer/pallas_call | solution.py:572
  27.7 0.1 collective-permute-start.8
  27.8 2.1 %second_gradient.1 = (f32[128,1536]{1,0:T(8,128)S(1)}, f32[8,1536]{1,0:T(8,128)S(1)}) custom-call(f32[8,8,1536]{2,1,0:T(8,128)S(1)} %get-tuple-element.73.geo, f32[384,1536]{1,0:T(8,128)S(1)} %get-tuple-element.80.rad_ref, f32[384,1536]{1,0:T(8,128)S(1)} %get-tuple-element.84.slope_ref, f32[128,1536]{1,0:T(8,128)S(1)} %get-tuple-element.85.feat_ref, ...), custom_call_target="tpu_custom_call" | custom-call | flops 2500000000 | bytes 7500000 | tf_op jit(solution)/shard_map/second_gradient/pallas_call | solution.py:572
  29.9 0.0 collective-permute-done.8
  30.0 0.1 collective-permute-start.9
  30.0 0.7 %ghost_gradient.1 = (bf16[280,1536]{1,0:T(8,128)(2,1)S(1)}, f32[128,128]{1,0:T(8,128)S(1)}, f32[64,128]{1,0:T(8,128)S(1)}, f32[64,128]{1,0:T(8,128)S(1)}, f32[8,256]{1,0:T(8,128)S(1)}, /*index=5*/f32[8,384]{1,0:T(8,128)S(1)}) custom-call(f32[128,1536]{1,0:T(8,128)S(1)} %get-tuple-element.90.g_feat, f32[8,1536]{1,0:T(8,128)S(1)} %get-tuple-element.91.g_off, ...), custom_call_target="tpu_custom_call" | custom-call | flops 1500000000 | bytes 4500000 | tf_op jit(solution)/shard_map/ghost_gradient/pallas_call | solution.py:572
  30.8 1.8 %collective-permute-start.11 = (f32[64,128]{1,0:T(8,128)S(1)}, f32[64,128]{1,0:T(8,128)S(1)}, u32[]{:S(2)}, u32[]{:S(2)}) collective-permute-start(f32[64,128]{1,0:T(8,128)S(1)} %get-tuple-element.95), channel_id=1, source_target_pairs={{0,15},{1,2},{2,1},{3,4},{4,3},{5,6},{6,5},{7,8},{8,7},{9,10},{10,... | collective-permute-start | bytes 98312 | tf_op jit(solution)/shard_map/ppermute | solution.py:591
  32.6 0.0 collective-permute-start.14
  32.6 1.5 %collective-permute-start.13 = (f32[128,128]{1,0:T(8,128)S(1)}, f32[128,128]{1,0:T(8,128)S(1)}, u32[]{:S(2)}, u32[]{:S(2)}) collective-permute-start(f32[128,128]{1,0:T(8,128)S(1)} %get-tuple-element.104), channel_id=1, source_target_pairs={{0,16},{16,0},{1,17},{17,1},{2,18},{18,2},{3,19},{19,3},{4,20},{20... | collective-permute-start | bytes 196616 | tf_op jit(solution)/shard_map/ppermute | solution.py:596
  34.1 0.7 %collective-permute-done.9 = f32[64,128]{1,0:T(8,128)S(1)} collective-permute-done((f32[64,128]{1,0:T(8,128)S(1)}, f32[64,128]{1,0:T(8,128)S(1)}, u32[]{:S(2)}, u32[]{:S(2)}) %collective-permute-start.9) | collective-permute-done | bytes 32800 | tf_op jit(solution)/shard_map/ppermute | solution.py:624
  34.8 0.2 collective-permute-start.10
  35.0 2.4 %factors.1 = (f32[4,128,1536]{2,1,0:T(8,128)S(1)}, f32[128,384]{1,0:T(8,128)S(1)}, f32[8,384]{1,0:T(8,128)S(1)}) custom-call(f32[8,8,1536]{2,1,0:T(8,128)S(1)} %get-tuple-element.73.geo, f32[384,1536]{1,0:T(8,128)S(1)} %get-tuple-element.97.rad_ref, f32[384,1536]{1,0:T(8,128)S(1)} %get-tuple-element.98.slope_ref, ...), custom_call_target="tpu_custom_call" | custom-call | flops 3000000000 | bytes 9000000 | tf_op jit(solution)/shard_map/factors/pallas_call | solution.py:572
  37.4 0.0 collective-permute-done.11.got_chip
  37.4 1.0 %collective-permute-done.10 = f32[8,128]{1,0:T(8,128)S(1)} collective-permute-done((f32[8,128]{1,0:T(8,128)S(1)}, f32[8,128]{1,0:T(8,128)S(1)}, u32[]{:S(2)}, u32[]{:S(2)}) %collective-permute-start.10) | collective-permute-done | bytes 4128 | tf_op jit(solution)/shard_map/ppermute | solution.py:624
  38.5 1.4 %collective-permute-start.12 = (f32[64,128]{1,0:T(8,128)S(1)}, f32[64,128]{1,0:T(8,128)S(1)}, u32[]{:S(2)}, u32[]{:S(2)}) collective-permute-start(f32[64,128]{1,0:T(8,128)S(1)} %pad.4), channel_id=1, source_target_pairs={{0,4},{1,5},{2,6},{3,7},{4,0},{5,1},{6,2},{7,3},{8,12},{9,13},{10,... | collective-permute-start | bytes 98312 | tf_op jit(solution)/shard_map/ppermute | solution.py:624
  39.9 1.2 %first_gradient.1 = (bf16[24,1536]{1,0:T(8,128)(2,1)S(1)}, f32[8,384]{1,0:T(8,128)S(1)}, f32[8,128]{1,0:T(8,128)S(1)}, f32[8,128]{1,0:T(8,128)S(1)}, f32[8,128]{1,0:T(8,128)S(1)}) custom-call(f32[128,384]{1,0:T(8,128)S(1)} %get-tuple-element.103.g_h, f32[128,128]{1,0:T(8,128)S(1)} %collective-permute-done.13.got_gx, ...), custom_call_target="tpu_custom_call" | custom-call | flops 1200000000 | bytes 3600000 | tf_op jit(solution)/shard_map/first_gradient/pallas_call | solution.py:572
  41.0 0.7 %collective-permute-start.15 = (f32[8,128]{1,0:T(8,128)S(1)}, f32[8,128]{1,0:T(8,128)S(1)}, u32[]{:S(2)}, u32[]{:S(2)}) collective-permute-start(f32[8,128]{1,0:T(8,128)S(1)} %get-tuple-element.116), channel_id=1, source_target_pairs={{0,15},{1,2},{2,1},{3,4},{4,3},{5,6},{6,5},{7,8},{8,7},{9,10},{10,... | collective-permute-start | bytes 12296 | tf_op jit(solution)/shard_map/ppermute | solution.py:591
  41.8 0.5 %collective-permute-start.16 = (f32[8,128]{1,0:T(8,128)S(1)}, f32[8,128]{1,0:T(8,128)S(1)}, u32[]{:S(2)}, u32[]{:S(2)}) collective-permute-start(f32[8,128]{1,0:T(8,128)S(1)} %get-tuple-element.117), channel_id=1, source_target_pairs={{0,16},{16,0},{1,17},{17,1},{2,18},{18,2},{3,19},{19,3},{4,20},{20... | collective-permute-start | bytes 12296 | tf_op jit(solution)/shard_map/ppermute | solution.py:596
  42.3 0.3 collective-permute-start.17
  42.6 0.0 collective-permute-done.12
  42.6 1.5 %collective-permute-start.18 = (f32[8,128]{1,0:T(8,128)S(1)}, f32[8,128]{1,0:T(8,128)S(1)}, u32[]{:S(2)}, u32[]{:S(2)}) collective-permute-start(f32[8,128]{1,0:T(8,128)S(1)} %slice_add_fusion.rest_0_), channel_id=1, source_target_pairs={{0,16},{16,0},{1,17},{17,1},{2,18},{18,2},{3,19},{19,3},{4,20},{20... | collective-permute-start | bytes 12296 | tf_op jit(solution)/shard_map/ppermute | solution.py:624
  44.1 0.3 local.1.g_pos
  44.4 2.4 %collective-permute-done.15.got_chip = f32[8,128]{1,0:T(8,128)S(1)} collective-permute-done((f32[8,128]{1,0:T(8,128)S(1)}, f32[8,128]{1,0:T(8,128)S(1)}, u32[]{:S(2)}, u32[]{:S(2)}) %collective-permute-start.15) | collective-permute-done | bytes 4128 | tf_op jit(solution)/shard_map/ppermute | solution.py:591
  46.8 0.1 chip_forces.1.g_sum
  47.0 0.0 collective-permute-done.16.got_gx
  47.0 0.0 collective-permute-done.17.got_core
  47.0 0.8 %forces.1 = (f32[3,384]{1,0:T(4,128)}, f32[1,1]{1,0:T(1,128)}) custom-call(f32[8,384]{1,0:T(8,128)S(1)} %chip_forces.1.g_sum, f32[8,128]{1,0:T(8,128)S(1)} %collective-permute-done.16.got_gx, f32[8,128]{1,0:T(8,128)S(1)} %collective-permute-done.17.got_core, bf16[256,384]{1,0:T(8,128)(2,1)S(1)} %get-tuple-element.110.send_t, ...), custom_call_target="tpu_custom_call" | custom-call | flops 1000000000 | bytes 3000000 | tf_op jit(solution)/shard_map/forces/pallas_call | solution.py:572
  (10 shorter events, 0.0 us)
Async XLA Ops:
  1.4 7.9 %collective-permute-start.1 = (f32[24,128]{1,0:T(8,128)S(1)}, f32[24,128]{1,0:T(8,128)S(1)}, u32[]{:S(2)}, u32[]{:S(2)}) collective-permute-start(f32[24,128]{1,0:T(8,128)S(1)} %pack.1.own), channel_id=1, source_target_pairs={{0,15},{1,2},{2,1},{3,4},{4,3},{5,6},{6,5},{7,8},{8,7},{9,10},{10,... | collective-permute-start | bytes 36872 | tf_op jit(solution)/shard_map/ppermute | solution.py:591
  6.9 2.4 %collective-permute-start = (f32[24,128]{1,0:T(8,128)S(1)}, f32[24,128]{1,0:T(8,128)S(1)}, u32[]{:S(2)}, u32[]{:S(2)}) collective-permute-start(f32[24,128]{1,0:T(8,128)S(1)} %pack.1.own), channel_id=1, source_target_pairs={{0,1},{1,0},{2,3},{3,2},{4,5},{5,4},{6,7},{7,6},{8,9},{9,8},{10,11... | collective-permute-start | bytes 36872 | tf_op jit(solution)/shard_map/ppermute | solution.py:586
  9.4 7.1 %collective-permute-start.4 = (f32[32,128]{1,0:T(8,128)S(1)}, f32[32,128]{1,0:T(8,128)S(1)}, u32[]{:S(2)}, u32[]{:S(2)}) collective-permute-start(f32[32,128]{1,0:T(8,128)S(1)} %get-tuple-element.66), channel_id=1, source_target_pairs={{0,15},{1,2},{2,1},{3,4},{4,3},{5,6},{6,5},{7,8},{8,7},{9,10},{10,... | collective-permute-start | bytes 49160 | tf_op jit(solution)/shard_map/ppermute | solution.py:591
  12.9 3.6 %collective-permute-start.2 = (f32[8,128]{1,0:T(8,128)S(1)}, f32[8,128]{1,0:T(8,128)S(1)}, u32[]{:S(2)}, u32[]{:S(2)}) collective-permute-start(f32[8,128]{1,0:T(8,128)S(1)} %get-tuple-element.64), channel_id=1, source_target_pairs={{0,16},{16,0},{1,17},{17,1},{2,18},{18,2},{3,19},{19,3},{4,20},{20... | collective-permute-start | bytes 12296 | tf_op jit(solution)/shard_map/ppermute | solution.py:596
  14.4 2.1 %collective-permute-start.3 = (f32[8,128]{1,0:T(8,128)S(1)}, f32[8,128]{1,0:T(8,128)S(1)}, u32[]{:S(2)}, u32[]{:S(2)}) collective-permute-start(f32[8,128]{1,0:T(8,128)S(1)} %get-tuple-element.65), channel_id=1, source_target_pairs={{0,1},{1,0},{2,3},{3,2},{4,5},{5,4},{6,7},{7,6},{8,9},{9,8},{10,11... | collective-permute-start | bytes 12296 | tf_op jit(solution)/shard_map/ppermute | solution.py:586
  16.5 6.4 %copy-start = (f32[5]{0:T(128)S(1)}, f32[5]{0:T(128)}, u32[]{:S(2)}) copy-start(f32[5]{0:T(128)} %atom_ref.1) | copy-start | bytes 64
  19.0 6.1 %collective-permute-start.6 = (f32[64,128]{1,0:T(8,128)S(1)}, f32[64,128]{1,0:T(8,128)S(1)}, u32[]{:S(2)}, u32[]{:S(2)}) collective-permute-start(f32[64,128]{1,0:T(8,128)S(1)} %get-tuple-element.77), channel_id=1, source_target_pairs={{0,1},{1,0},{2,3},{3,2},{4,5},{5,4},{6,7},{7,6},{8,9},{9,8},{10,11... | collective-permute-start | bytes 98312 | tf_op jit(solution)/shard_map/ppermute | solution.py:586
  19.1 6.1 %collective-permute-start.7 = (f32[64,128]{1,0:T(8,128)S(1)}, f32[64,128]{1,0:T(8,128)S(1)}, u32[]{:S(2)}, u32[]{:S(2)}) collective-permute-start(f32[64,128]{1,0:T(8,128)S(1)} %get-tuple-element.78), channel_id=1, source_target_pairs={{0,15},{1,2},{2,1},{3,4},{4,3},{5,6},{6,5},{7,8},{8,7},{9,10},{10,... | collective-permute-start | bytes 98312 | tf_op jit(solution)/shard_map/ppermute | solution.py:591
  21.4 4.3 %collective-permute-start.5 = (f32[128,128]{1,0:T(8,128)S(1)}, f32[128,128]{1,0:T(8,128)S(1)}, u32[]{:S(2)}, u32[]{:S(2)}) collective-permute-start(f32[128,128]{1,0:T(8,128)S(1)} %get-tuple-element.76), channel_id=1, source_target_pairs={{0,16},{16,0},{1,17},{17,1},{2,18},{18,2},{3,19},{19,3},{4,20},{20... | collective-permute-start | bytes 196616 | tf_op jit(solution)/shard_map/ppermute | solution.py:596
  27.7 2.2 %collective-permute-start.8 = (f32[64,128]{1,0:T(8,128)S(1)}, f32[64,128]{1,0:T(8,128)S(1)}, u32[]{:S(2)}, u32[]{:S(2)}) collective-permute-start(f32[64,128]{1,0:T(8,128)S(1)} %get-tuple-element.83), channel_id=1, source_target_pairs={{0,1},{1,0},{2,3},{3,2},{4,5},{5,4},{6,7},{7,6},{8,9},{9,8},{10,11... | collective-permute-start | bytes 98312 | tf_op jit(solution)/shard_map/ppermute | solution.py:624
  30.0 4.9 %collective-permute-start.9 = (f32[64,128]{1,0:T(8,128)S(1)}, f32[64,128]{1,0:T(8,128)S(1)}, u32[]{:S(2)}, u32[]{:S(2)}) collective-permute-start(f32[64,128]{1,0:T(8,128)S(1)} %add.14), channel_id=1, source_target_pairs={{0,8},{1,9},{2,10},{3,11},{4,12},{5,13},{6,14},{7,15},{8,0},{9,1},... | collective-permute-start | bytes 98312 | tf_op jit(solution)/shard_map/ppermute | solution.py:624
  30.8 6.6 %collective-permute-start.11 = (f32[64,128]{1,0:T(8,128)S(1)}, f32[64,128]{1,0:T(8,128)S(1)}, u32[]{:S(2)}, u32[]{:S(2)}) collective-permute-start(f32[64,128]{1,0:T(8,128)S(1)} %get-tuple-element.95), channel_id=1, source_target_pairs={{0,15},{1,2},{2,1},{3,4},{4,3},{5,6},{6,5},{7,8},{8,7},{9,10},{10,... | collective-permute-start | bytes 98312 | tf_op jit(solution)/shard_map/ppermute | solution.py:591
  32.6 7.3 %collective-permute-start.14 = (f32[64,128]{1,0:T(8,128)S(1)}, f32[64,128]{1,0:T(8,128)S(1)}, u32[]{:S(2)}, u32[]{:S(2)}) collective-permute-start(f32[64,128]{1,0:T(8,128)S(1)} %get-tuple-element.105), channel_id=1, source_target_pairs={{0,1},{1,0},{2,3},{3,2},{4,5},{5,4},{6,7},{7,6},{8,9},{9,8},{10,11... | collective-permute-start | bytes 98312 | tf_op jit(solution)/shard_map/ppermute | solution.py:586
  32.6 7.3 %collective-permute-start.13 = (f32[128,128]{1,0:T(8,128)S(1)}, f32[128,128]{1,0:T(8,128)S(1)}, u32[]{:S(2)}, u32[]{:S(2)}) collective-permute-start(f32[128,128]{1,0:T(8,128)S(1)} %get-tuple-element.104), channel_id=1, source_target_pairs={{0,16},{16,0},{1,17},{17,1},{2,18},{18,2},{3,19},{19,3},{4,20},{20... | collective-permute-start | bytes 196616 | tf_op jit(solution)/shard_map/ppermute | solution.py:596
  34.8 3.6 %collective-permute-start.10 = (f32[8,128]{1,0:T(8,128)S(1)}, f32[8,128]{1,0:T(8,128)S(1)}, u32[]{:S(2)}, u32[]{:S(2)}) collective-permute-start(f32[8,128]{1,0:T(8,128)S(1)} %slice_add_fusion.1), channel_id=1, source_target_pairs={{0,2},{1,3},{2,0},{3,1},{4,6},{5,7},{6,4},{7,5},{8,10},{9,11},{10,... | collective-permute-start | bytes 12296 | tf_op jit(solution)/shard_map/ppermute | solution.py:624
  38.5 4.2 %collective-permute-start.12 = (f32[64,128]{1,0:T(8,128)S(1)}, f32[64,128]{1,0:T(8,128)S(1)}, u32[]{:S(2)}, u32[]{:S(2)}) collective-permute-start(f32[64,128]{1,0:T(8,128)S(1)} %pad.4), channel_id=1, source_target_pairs={{0,4},{1,5},{2,6},{3,7},{4,0},{5,1},{6,2},{7,3},{8,12},{9,13},{10,... | collective-permute-start | bytes 98312 | tf_op jit(solution)/shard_map/ppermute | solution.py:624
  41.0 5.8 %collective-permute-start.15 = (f32[8,128]{1,0:T(8,128)S(1)}, f32[8,128]{1,0:T(8,128)S(1)}, u32[]{:S(2)}, u32[]{:S(2)}) collective-permute-start(f32[8,128]{1,0:T(8,128)S(1)} %get-tuple-element.116), channel_id=1, source_target_pairs={{0,15},{1,2},{2,1},{3,4},{4,3},{5,6},{6,5},{7,8},{8,7},{9,10},{10,... | collective-permute-start | bytes 12296 | tf_op jit(solution)/shard_map/ppermute | solution.py:591
  41.8 5.2 %collective-permute-start.16 = (f32[8,128]{1,0:T(8,128)S(1)}, f32[8,128]{1,0:T(8,128)S(1)}, u32[]{:S(2)}, u32[]{:S(2)}) collective-permute-start(f32[8,128]{1,0:T(8,128)S(1)} %get-tuple-element.117), channel_id=1, source_target_pairs={{0,16},{16,0},{1,17},{17,1},{2,18},{18,2},{3,19},{19,3},{4,20},{20... | collective-permute-start | bytes 12296 | tf_op jit(solution)/shard_map/ppermute | solution.py:596
  42.3 4.7 %collective-permute-start.17 = (f32[8,128]{1,0:T(8,128)S(1)}, f32[8,128]{1,0:T(8,128)S(1)}, u32[]{:S(2)}, u32[]{:S(2)}) collective-permute-start(f32[8,128]{1,0:T(8,128)S(1)} %get-tuple-element.118), channel_id=1, source_target_pairs={{0,1},{1,0},{2,3},{3,2},{4,5},{5,4},{6,7},{7,6},{8,9},{9,8},{10,11... | collective-permute-start | bytes 12296 | tf_op jit(solution)/shard_map/ppermute | solution.py:586
  42.6 4.4 %collective-permute-start.18 = (f32[8,128]{1,0:T(8,128)S(1)}, f32[8,128]{1,0:T(8,128)S(1)}, u32[]{:S(2)}, u32[]{:S(2)}) collective-permute-start(f32[8,128]{1,0:T(8,128)S(1)} %slice_add_fusion.rest_0_), channel_id=1, source_target_pairs={{0,16},{16,0},{1,17},{17,1},{2,18},{18,2},{3,19},{19,3},{4,20},{20... | collective-permute-start | bytes 12296 | tf_op jit(solution)/shard_map/ppermute | solution.py:624

commit v5 on v4

--- a/solution.py
+++ b/solution.py
@@ -16,7 +16,10 @@
 ROWS = 8
 LANES = 128
 TALL = 64
-CHIP_ROWS = 32
+CHIP_ROWS = 16
+SUMS_UNROLL = 16
+EDGE_UNROLL = 16
+FORCE_UNROLL = 16
 VMEM_BYTES = 16 * 1024 * 1024
 
 
@@ -161,11 +164,12 @@
 U, R, SCALE, SQUARE = 0, 3, 6, 7
 
 
-def gather_sums(y_ref, rad_ref, feat_ref, fields_ref, invariant_ref):
+def gather_sums(geo, y_ref, rad_ref, feat_ref, fields_ref, invariant_ref):
     channels, slots = invariant_ref.shape
     entries = feat_ref.shape[1] // slots
     for lanes, edges in lane_parts(slots, entries):
-        angular = [[y_ref[m, :, edges[k]] for m in range(8)] for k in range(entries)]
+        first = [[geo[U + d, :, edges[k]] for d in range(3)] for k in range(entries)]
+        second = [[y_ref[m, :, edges[k]] for m in range(5)] for k in range(entries)]
 
         def body(index, carry):
             rows = tile(index)
@@ -173,32 +177,29 @@
             sums = None
             for k in range(entries):
                 feat = feat_ref[rows, edges[k]]
-                weighted = [rad_ref[degree, edges[k]] * feat for degree in degrees]
-                terms = [weighted[0]] + [angular[k][m] * weighted[1 if m < 3 else 2] for m in range(8)]
+                zero, one, two = [rad_ref[degree, edges[k]] * feat for degree in degrees]
+                terms = [zero] + [item * one for item in first[k]] + [item * two for item in second[k]]
                 sums = terms if k == 0 else [old + new for old, new in zip(sums, terms)]
             total = sums[0]
             for item in sums[1:]:
                 total = total + item * item
             invariant_ref[rows, lanes] = total
             a1, a2, a3, a4, a5, a6, a7, a8 = sums[1:]
-            c6, c8 = (2.0 * root_five) * a6, (2.0 * root_fifteen) * a8
-            fields = [(2.0 * root_three) * a for a in (a1, a2, a3)]
-            fields += [(2.0 * root_fifteen) * a for a in (a4, a5, a7)]
-            fields += [c8 - c6, c8 + c6, c6 + c6]
-            for number, field in enumerate(fields):
+            c6 = (1.0 / root_three) * a6
+            for number, field in enumerate((a1, a2, a3, a4, a5, a7, a8 - c6, a8 + c6, c6 + c6)):
                 fields_ref[number, rows, lanes] = field
             return carry
 
-        lax.fori_loop(0, channels // ROWS, body, 0, unroll=2)
+        lax.fori_loop(0, channels // ROWS, body, 0, unroll=SUMS_UNROLL)
 
 
 def direction_terms(fields, unit):
-    b1, b2, b3, c4, c5, c7, minus, plus, twice = fields
+    a1, a2, a3, a4, a5, a7, minus, plus, twice = fields
     ux, uy, uz = unit
-    h_x = uy * c4 + uz * c7 + ux * minus
-    h_y = ux * c4 + uz * c5 - uy * plus
-    h_z = uy * c5 + ux * c7 + uz * twice
-    one = ux * b1 + uy * b2 + uz * b3
+    h_x = uy * a4 + uz * a7 + ux * minus
+    h_y = ux * a4 + uz * a5 - uy * plus
+    h_z = uy * a5 + ux * a7 + uz * twice
+    one = ux * a1 + uy * a2 + uz * a3
     two = 0.5 * (ux * h_x + uy * h_y + uz * h_z)
     return h_x, h_y, h_z, one, two
 
@@ -272,12 +273,15 @@
         send[:, face * ghosts : (face + 1) * ghosts] = onehot_rows(slots, lists[face : face + 1, :])
     count = w_rad.shape[1]
     which = lax.broadcasted_iota(jnp.int32, gamma.shape[1:], 0)
+    channels = w_up.shape[1]
+    place = lax.broadcasted_iota(jnp.int32, w_rad.shape[1:], 1)
+    scales = jnp.where(place < channels, 1.0, jnp.where(place < 2 * channels, root_three, root_fifteen)) * (1.0 / entries)
     for layer in range(2):
         value = jnp.zeros(which.shape, f32)
         for q in range(count):
             value = jnp.where(which == q, gammas[layer, q], value)
         gamma[layer] = value
-        radials[layer] = stacked_rows_left(w_rad[layer] * (1.0 / entries)).T.astype(bf16)
+        radials[layer] = stacked_rows_left(w_rad[layer] * scales).T.astype(bf16)
     padded[...] = jnp.zeros(padded.shape, f32)
     padded[0 : embed.shape[0], :] = embed[...]
     species = padded[...]
@@ -317,20 +321,24 @@
     pick_chip[0:ROWS, :] = picked[:, LANES : 2 * LANES]
 
 
+def own_positions_kernel(table, onehot, found):
+    found[...] = whole(matmul(pieces(table[...]), onehot[0 : table.shape[1], :]))
+
+
 def first_layer_kernel(
-    table, got_gx, got_core, got_chip, onehot, send, gamma, radials, species_up, species_in, weights,
+    found_own, table, got_gx, got_core, got_chip, onehot, send, gamma, radials, species_up, species_in, weights,
     h_out, slope_out, send_gx, send_core, send_chip, geo, y_ref, rad_ref, feat_ref, fields_ref,
     inv_ref,
 ):
     slots = table.shape[1]
     edges = onehot.shape[1]
     entries = edges // slots
-    ext = jnp.concatenate([table[...], got_gx[...], faces_yz(got_core[...], got_chip[0:ROWS, :])], axis=1)
-    found = whole(matmul(pieces(ext), onehot[...]))
+    ghosts = jnp.concatenate([got_gx[...], faces_yz(got_core[...], got_chip[0:ROWS, :])], axis=1)
+    found = found_own[...] + whole(matmul(pieces(ghosts), onehot[slots:, :]))
     feat_ref[...] = matmul(species_up[...], species_onehot(found[3:4], ROWS))
     spread = lambda row: jnp.broadcast_to(row, (ROWS, edges))
     rx, ry, rz = [
-        spread(found[d : d + 1] - repeat(ext[d : d + 1, 0:slots], entries)) for d in range(3)
+        spread(found[d : d + 1] - repeat(table[d : d + 1, :], entries)) for d in range(3)
     ]
     square = rx * rx + ry * ry + rz * rz
     basis = jnp.exp(-gamma[0] * square)
@@ -339,18 +347,14 @@
     ux, uy, uz = rx * scale, ry * scale, rz * scale
     for number, item in enumerate((ux, uy, uz, rx, ry, rz, scale, square)):
         geo[number] = item
-    unit_square = ux * ux + uy * uy + uz * uz
-    y_ref[0] = root_three * ux
-    y_ref[1] = root_three * uy
-    y_ref[2] = root_three * uz
-    y_ref[3] = root_fifteen * ux * uy
-    y_ref[4] = root_fifteen * uy * uz
-    y_ref[5] = 0.5 * root_five * (3.0 * uz * uz - unit_square)
-    y_ref[6] = root_fifteen * ux * uz
-    y_ref[7] = 0.5 * root_fifteen * (ux * ux - uy * uy)
-    gather_sums(y_ref, rad_ref, feat_ref, fields_ref, inv_ref)
+    xx, yy, zz = ux * ux, uy * uy, uz * uz
+    for number, item in enumerate(
+        (ux * uy, uy * uz, (0.5 / root_three) * (2.0 * zz - xx - yy), ux * uz, 0.5 * (xx - yy))
+    ):
+        y_ref[number] = item
+    gather_sums(geo, y_ref, rad_ref, feat_ref, fields_ref, inv_ref)
     mixed = matmul(weights[0], stacked_right(inv_ref[...]))
-    code = ext[3:4, 0:slots]
+    code = table[3:4, :]
     live = jnp.where(code >= 0.0, 1.0, 0.0)
     h_zero = matmul(species_in[...], species_onehot(code, ROWS))
     value, slope = silu_and_slope(mixed)
@@ -413,17 +417,17 @@
                 feat = feat_ref[rows, edges[k]]
                 r1, r2 = [rad_ref[d, edges[k]] * feat for d in degrees[1:]]
                 d0, d1, d2 = [slope_ref[d, edges[k]] for d in degrees]
-                factors[0, rows, edges[k]] = feat * (d0 + d1 * one + d2 * two)
+                factors[0, rows, edges[k]] = feat * (0.5 * d0 + d1 * one + d2 * two)
                 factors[1, rows, edges[k]] = r1 * fields[0] + r2 * h_x
                 factors[2, rows, edges[k]] = r1 * fields[1] + r2 * h_y
                 factors[3, rows, edges[k]] = r1 * fields[2] + r2 * h_z
             return carry
 
-        lax.fori_loop(0, channels // ROWS, body, 0)
+        lax.fori_loop(0, channels // ROWS, body, 0, unroll=2)
 
 
 def second_layer_kernel(
-    base, table, h_one, got_gx, got_core, got_chip, onehot, y_ref, rad_ref, weights, reads, found_two,
+    base, table, h_one, got_gx, got_core, got_chip, onehot, geo, y_ref, rad_ref, weights, reads, found_two,
     feat_ref, fields_ref, g_ref, g_own, tally,
     inv_ref,
 ):
@@ -434,7 +438,7 @@
     projected = matmul(weights[1], stacked_right(ghosts))
     both = matmul(jnp.concatenate(split2(projected), axis=0), onehot[slots:, :])
     feat_ref[...] = found_two[...] + (both[0:channels] + both[channels : 2 * channels])
-    gather_sums(y_ref, rad_ref, feat_ref, fields_ref, inv_ref)
+    gather_sums(geo, y_ref, rad_ref, feat_ref, fields_ref, inv_ref)
     mixed = matmul(weights[2], stacked_right(inv_ref[...]))
     live = jnp.where(table[3:4, :] >= 0.0, 1.0, 0.0)
     value, slope = silu_and_slope(mixed)
@@ -460,7 +464,7 @@
             rows = tile(index)
             degrees = degree_tiles(index, channels)
             g = g_ref[rows, lanes]
-            fields = [g * fields_ref[m, rows, lanes] for m in range(9)]
+            fields = [(g + g) * fields_ref[m, rows, lanes] for m in range(9)]
             found = []
             for k in range(entries):
                 h_x, h_y, h_z, one, two = direction_terms(fields, units[k])
@@ -478,7 +482,7 @@
             return tuple(found)
 
         zero = jnp.zeros((ROWS, LANES), f32)
-        found = lax.fori_loop(0, channels // ROWS, body, (zero,) * (4 * entries))
+        found = lax.fori_loop(0, channels // ROWS, body, (zero,) * (4 * entries), unroll=EDGE_UNROLL)
         for k in range(entries):
             for d, item in enumerate(offset_gradients(found[4 * k : 4 * k + 4], geo, edges[k])):
                 g_off[d : d + 1, edges[k]] = item
@@ -514,7 +518,7 @@
     back = jnp.concatenate([got_gx[...], join_halves(after, before)], axis=1)
     returned = matmul(jnp.concatenate(split2(back), axis=0), send_t[...])
     g_total = g_h[...] + (returned[0:channels] + returned[channels : 2 * channels])
-    g_ref[...] = matmul(weights[5], stacked_right(g_total * slope[...]))
+    g_ref[...] = matmul(weights[5], stacked_right(g_total * (2.0 * slope[...])))
     g_off[...] = jnp.zeros(g_off.shape, f32)
     for lanes, edges in lane_parts(slots, entries):
 
@@ -526,7 +530,7 @@
             )
 
         zero = jnp.zeros((ROWS, LANES), f32)
-        found = lax.fori_loop(0, channels // ROWS, body, (zero,) * (4 * entries), unroll=4)
+        found = lax.fori_loop(0, channels // ROWS, body, (zero,) * (4 * entries), unroll=FORCE_UNROLL)
         for k in range(entries):
             for d, item in enumerate(offset_gradients(found[4 * k : 4 * k + 4], geo, edges[k])):
                 g_off[d : d + 1, edges[k]] = item
@@ -717,15 +721,18 @@
     got_chip = swap_chip(pick_chip)
     got_gx = swap_gx(pick_gx)
     got_core = swap_core(pick_core)
+    (found_own,) = call(
+        own_positions_kernel, [(ROWS, edges)], [], [table, onehot], name="own_positions", us=0.02
+    )
     flat = (channels, slots)
     square = (channels, LANES)
     half = (channels // 2, LANES)
     fields_shape = (9, channels, slots)
     h_one, slope, send_gx, send_core, send_chip, geo, angular, rad_one, feat_one, fields_one = call(
         first_layer_kernel,
-        [flat, flat, square, half, half, (8, ROWS, edges), (8, ROWS, edges), (rows, edges), (channels, edges), fields_shape],
-        [],
-        [table, got_gx, got_core, got_chip, onehot, send, gamma, radials, species_up, species_in, weights],
+        [flat, flat, square, half, half, (8, ROWS, edges), (5, ROWS, edges), (rows, edges), (channels, edges), fields_shape],
+        [],
+        [found_own, table, got_gx, got_core, got_chip, onehot, send, gamma, radials, species_up, species_in, weights],
         [flat],
         name="first_layer",
         us=2.5,
@@ -745,7 +752,7 @@
         second_layer_kernel,
         [(channels, edges), fields_shape, flat, flat, (TALL, LANES)],
         [],
-        [base, table, h_one, got_gx, got_core, got_chip, onehot, angular, rad_two, weights, reads, found_two],
+        [base, table, h_one, got_gx, got_core, got_chip, onehot, geo, angular, rad_two, weights, reads, found_two],
         [flat],
         name="second_layer",
         us=2.5,

time: 48 us -> 46.1 us (0.960)
  Pallas kernels: 17.5 us -> 16 us
    pallas_call x13 -> x14, Pallas kernels: 17.5 us -> 16 us  [call(): pl.pallas_call(kernel, out_shape=shapes, in_specs=[in_smem] * len(scalars...]
  transfers between devices with their start and end apart: 19 -> 19, of which waited for: 6 -> 6; matrix products, arithmetic and copies ran while one was open for 0% -> 0% of each run, Pallas kernels for 24% -> 23%
where the time goes in v5:
time: 46.1 us; the launch traced here: 45.8 us
  starting transfers between devices  22.4 us (49%)
  Pallas kernels  16 us (35%)
  waiting for transfers between devices  6.57 us (14%)
  between operations  0.81 us (2%)
    pallas_call x14, Pallas kernels, call(): pl.pallas_call(kernel, out_shape=shapes, in_specs=[in_smem] * len(scalars...  16 us
    ppermute x5, starting transfers between devices, swap_chip(): lax.ppermute(value, 'yz', [(i, (i + 1 if i % 2 else i - 1) % size) for i...  13.7 us
    ppermute x4, starting transfers between devices, shift(): lax.ppermute(value, axis, [(i, (i + by) % size) for i in range(size)])  5.07 us
    ppermute x5, starting transfers between devices, partners(): lax.ppermute(value, axis, [(i, i ^ step) for i in range(size)])  3.1 us
    ppermute x5, waiting for transfers between devices, swap_chip(): lax.ppermute(value, 'yz', [(i, (i + 1 if i % 2 else i - 1) % size) for i...  2.44 us
    ppermute x4, waiting for transfers between devices, shift(): lax.ppermute(value, axis, [(i, (i + by) % size) for i in range(size)])  2.21 us
    ppermute x5, waiting for transfers between devices, partners(): lax.ppermute(value, axis, [(i, i ^ step) for i in range(size)])  1.91 us
  transfers between devices with their start and end apart: 19, of which 6 were waited for; matrix products, arithmetic and copies ran while one was open for 0% of the time, Pallas kernels for 23%

profile of v5, /device:TPU:0, one launch (start us, length us, event | category | flops | bytes accessed | tf_op | source)
XLA Modules:
  0.0 45.8 jit_solution(10523204744274652591)
XLA Ops:
  0.6 0.7 %pack.1.own = f32[24,128]{1,0:T(8,128)S(1)} custom-call(s32[1,2]{1,0:T(1,128)} %bitcast.4, s32[2]{0:T(128)} %count_hbm.1, f32[3,256]{1,0:T(4,128)} %pos_hbm.1, s32[2,128]{1,0:T(2,128)} %bitcast.3), custom_call_target="tpu_custom_call" | custom-call | flops 1000000000 | bytes 3000000 | tf_op jit(solution)/shard_map/pack/pallas_call | solution.py:576
  1.4 5.5 %collective-permute-start.1 = (f32[24,128]{1,0:T(8,128)S(1)}, f32[24,128]{1,0:T(8,128)S(1)}, u32[]{:S(2)}, u32[]{:S(2)}) collective-permute-start(f32[24,128]{1,0:T(8,128)S(1)} %pack.1.own), channel_id=1, source_target_pairs={{0,15},{1,2},{2,1},{3,4},{4,3},{5,6},{6,5},{7,8},{8,7},{9,10},{10,... | collective-permute-start | bytes 36872 | tf_op jit(solution)/shard_map/ppermute | solution.py:595
  6.9 0.0 collective-permute-start
  6.9 2.4 %prepare.1 = (bf16[640,1536]{1,0:T(8,128)(2,1)S(1)}, bf16[384,256]{1,0:T(8,128)(2,1)S(1)}, f32[2,8,1536]{2,1,0:T(8,128)S(1)}, bf16[2,384,24]{2,1,0:T(8,128)(2,1)...) custom-call(f32[2,8]{1,0:T(2,128)} %gammas_hbm.1, ...), custom_call_target="tpu_custom_call" | custom-call | flops 3000000000 | bytes 9000000 | tf_op jit(solution)/shard_map/prepare/pallas_call | solution.py:576
  9.3 0.0 collective-permute-done.1.chip
  9.3 0.0 collective-permute-done.core
  9.3 0.1 assemble.1
  9.4 3.5 %collective-permute-start.4 = (f32[16,128]{1,0:T(8,128)S(1)}, f32[16,128]{1,0:T(8,128)S(1)}, u32[]{:S(2)}, u32[]{:S(2)}) collective-permute-start(f32[16,128]{1,0:T(8,128)S(1)} %get-tuple-element.67), channel_id=1, source_target_pairs={{0,15},{1,2},{2,1},{3,4},{4,3},{5,6},{6,5},{7,8},{8,7},{9,10},{10,... | collective-permute-start | bytes 24584 | tf_op jit(solution)/shard_map/ppermute | solution.py:595
  12.9 1.5 %collective-permute-start.2 = (f32[8,128]{1,0:T(8,128)S(1)}, f32[8,128]{1,0:T(8,128)S(1)}, u32[]{:S(2)}, u32[]{:S(2)}) collective-permute-start(f32[8,128]{1,0:T(8,128)S(1)} %get-tuple-element.65), channel_id=1, source_target_pairs={{0,16},{16,0},{1,17},{17,1},{2,18},{18,2},{3,19},{19,3},{4,20},{20... | collective-permute-start | bytes 12296 | tf_op jit(solution)/shard_map/ppermute | solution.py:600
  14.4 0.0 collective-permute-start.3
  14.4 0.3 own_positions.1.found_own
  14.7 1.8 %collective-permute-done.2.got_gx = f32[8,128]{1,0:T(8,128)S(1)} collective-permute-done((f32[8,128]{1,0:T(8,128)S(1)}, f32[8,128]{1,0:T(8,128)S(1)}, u32[]{:S(2)}, u32[]{:S(2)}) %collective-permute-start.2) | collective-permute-done | bytes 4128 | tf_op jit(solution)/shard_map/ppermute | solution.py:600
  16.5 0.0 collective-permute-done.3.got_core
  16.5 0.0 collective-permute-done.4.got_chip
  16.5 1.9 %first_layer.1 = (f32[128,384]{1,0:T(8,128)S(1)}, f32[128,384]{1,0:T(8,128)S(1)}, f32[128,128]{1,0:T(8,128)S(1)}, f32[64,128]{1,0:T(8,128)S(1)}, f32[64,128]{1,0...) custom-call(f32[8,1536]{1,0:T(8,128)S(1)} %own_positions.1.found_own, ...), custom_call_target="tpu_custom_call" | custom-call | flops 2500000000 | bytes 7500000 | tf_op jit(solution)/shard_map/first_layer/pallas_call | solution.py:576
  18.4 0.1 collective-permute-start.6
  18.5 2.2 %collective-permute-start.7 = (f32[64,128]{1,0:T(8,128)S(1)}, f32[64,128]{1,0:T(8,128)S(1)}, u32[]{:S(2)}, u32[]{:S(2)}) collective-permute-start(f32[64,128]{1,0:T(8,128)S(1)} %get-tuple-element.78), channel_id=1, source_target_pairs={{0,15},{1,2},{2,1},{3,4},{4,3},{5,6},{6,5},{7,8},{8,7},{9,10},{10,... | collective-permute-start | bytes 98312 | tf_op jit(solution)/shard_map/ppermute | solution.py:595
  20.7 1.5 %collective-permute-start.5 = (f32[128,128]{1,0:T(8,128)S(1)}, f32[128,128]{1,0:T(8,128)S(1)}, u32[]{:S(2)}, u32[]{:S(2)}) collective-permute-start(f32[128,128]{1,0:T(8,128)S(1)} %get-tuple-element.76), channel_id=1, source_target_pairs={{0,16},{16,0},{1,17},{17,1},{2,18},{18,2},{3,19},{19,3},{4,20},{20... | collective-permute-start | bytes 196616 | tf_op jit(solution)/shard_map/ppermute | solution.py:600
  22.2 2.2 %radials.1 = (f32[384,1536]{1,0:T(8,128)S(1)}, f32[384,1536]{1,0:T(8,128)S(1)}, f32[384,1536]{1,0:T(8,128)S(1)}, f32[64,128]{1,0:T(8,128)S(1)}, f32[128,1536]{1,0:T(8,128)S(1)}) custom-call(f32[5]{0:T(128)S(1)} %copy-done, f32[8,8,1536]{2,1,0:T(8,128)S(1)} %get-tuple-element.73.geo, f32[2,8,1536]{2,1,0:T(8,128)S(1)} %get-tuple-element.68.gamma, ...), custom_call_target="tpu_custom_call" | custom-call | flops 2000000000 | bytes 6000000 | tf_op jit(solution)/shard_map/radials/pallas_call | solution.py:576
  24.4 0.0 collective-permute-done.6.got_core
  24.4 0.2 collective-permute-done.7.got_chip
  24.6 0.4 collective-permute-done.5.got_gx
  25.0 1.8 %second_layer.1 = (f32[128,1536]{1,0:T(8,128)S(1)}, f32[9,128,384]{2,1,0:T(8,128)S(1)}, f32[128,384]{1,0:T(8,128)S(1)}, f32[128,384]{1,0:T(8,128)S(1)}, f32[64,128]{1,0:T(8,128)S(1)}) custom-call(f32[64,128]{1,0:T(8,128)S(1)} %get-tuple-element.75.base, f32[8,384]{1,0:T(8,128)S(1)} %get-tuple-element.63.table, f32[128,384]{1,0:T(8,128)S(1)} %get-tuple-element.74.h_one, ...), custom_call_target="tpu_custom_call" | custom-call | flops 2500000000 | bytes 7500000 | tf_op jit(solution)/shard_map/second_layer/pallas_call | solution.py:576
  26.7 0.1 collective-permute-start.8
  26.8 1.5 %second_gradient.1 = (f32[128,1536]{1,0:T(8,128)S(1)}, f32[8,1536]{1,0:T(8,128)S(1)}) custom-call(f32[8,8,1536]{2,1,0:T(8,128)S(1)} %get-tuple-element.73.geo, f32[384,1536]{1,0:T(8,128)S(1)} %get-tuple-element.80.rad_ref, f32[384,1536]{1,0:T(8,128)S(1)} %get-tuple-element.84.slope_ref, f32[128,1536]{1,0:T(8,128)S(1)} %get-tuple-element.85.feat_ref, ...), custom_call_target="tpu_custom_call" | custom-call | flops 2500000000 | bytes 7500000 | tf_op jit(solution)/shard_map/second_gradient/pallas_call | solution.py:576
  28.3 0.0 collective-permute-done.8
  28.3 0.1 collective-permute-start.9
  28.4 0.7 %ghost_gradient.1 = (bf16[280,1536]{1,0:T(8,128)(2,1)S(1)}, f32[128,128]{1,0:T(8,128)S(1)}, f32[64,128]{1,0:T(8,128)S(1)}, f32[64,128]{1,0:T(8,128)S(1)}, f32[8,256]{1,0:T(8,128)S(1)}, /*index=5*/f32[8,384]{1,0:T(8,128)S(1)}) custom-call(f32[128,1536]{1,0:T(8,128)S(1)} %get-tuple-element.90.g_feat, f32[8,1536]{1,0:T(8,128)S(1)} %get-tuple-element.91.g_off, ...), custom_call_target="tpu_custom_call" | custom-call | flops 1500000000 | bytes 4500000 | tf_op jit(solution)/shard_map/ghost_gradient/pallas_call | solution.py:576
  29.2 1.8 %collective-permute-start.11 = (f32[64,128]{1,0:T(8,128)S(1)}, f32[64,128]{1,0:T(8,128)S(1)}, u32[]{:S(2)}, u32[]{:S(2)}) collective-permute-start(f32[64,128]{1,0:T(8,128)S(1)} %get-tuple-element.95), channel_id=1, source_target_pairs={{0,15},{1,2},{2,1},{3,4},{4,3},{5,6},{6,5},{7,8},{8,7},{9,10},{10,... | collective-permute-start | bytes 98312 | tf_op jit(solution)/shard_map/ppermute | solution.py:595
  31.0 0.0 collective-permute-start.14
  31.0 1.5 %collective-permute-start.13 = (f32[128,128]{1,0:T(8,128)S(1)}, f32[128,128]{1,0:T(8,128)S(1)}, u32[]{:S(2)}, u32[]{:S(2)}) collective-permute-start(f32[128,128]{1,0:T(8,128)S(1)} %get-tuple-element.104), channel_id=1, source_target_pairs={{0,16},{16,0},{1,17},{17,1},{2,18},{18,2},{3,19},{19,3},{4,20},{20... | collective-permute-start | bytes 196616 | tf_op jit(solution)/shard_map/ppermute | solution.py:600
  32.5 0.7 %collective-permute-done.9 = f32[64,128]{1,0:T(8,128)S(1)} collective-permute-done((f32[64,128]{1,0:T(8,128)S(1)}, f32[64,128]{1,0:T(8,128)S(1)}, u32[]{:S(2)}, u32[]{:S(2)}) %collective-permute-start.9) | collective-permute-done | bytes 32800 | tf_op jit(solution)/shard_map/ppermute | solution.py:628
  33.2 0.2 collective-permute-start.10
  33.4 2.2 %factors.1 = (f32[4,128,1536]{2,1,0:T(8,128)S(1)}, f32[128,384]{1,0:T(8,128)S(1)}, f32[8,384]{1,0:T(8,128)S(1)}) custom-call(f32[8,8,1536]{2,1,0:T(8,128)S(1)} %get-tuple-element.73.geo, f32[384,1536]{1,0:T(8,128)S(1)} %get-tuple-element.97.rad_ref, f32[384,1536]{1,0:T(8,128)S(1)} %get-tuple-element.98.slope_ref, ...), custom_call_target="tpu_custom_call" | custom-call | flops 3000000000 | bytes 9000000 | tf_op jit(solution)/shard_map/factors/pallas_call | solution.py:576
  35.6 0.0 collective-permute-done.11.got_chip
  35.6 1.2 %collective-permute-done.10 = f32[8,128]{1,0:T(8,128)S(1)} collective-permute-done((f32[8,128]{1,0:T(8,128)S(1)}, f32[8,128]{1,0:T(8,128)S(1)}, u32[]{:S(2)}, u32[]{:S(2)}) %collective-permute-start.10) | collective-permute-done | bytes 4128 | tf_op jit(solution)/shard_map/ppermute | solution.py:628
  36.8 1.3 %collective-permute-start.12 = (f32[64,128]{1,0:T(8,128)S(1)}, f32[64,128]{1,0:T(8,128)S(1)}, u32[]{:S(2)}, u32[]{:S(2)}) collective-permute-start(f32[64,128]{1,0:T(8,128)S(1)} %pad.4), channel_id=1, source_target_pairs={{0,4},{1,5},{2,6},{3,7},{4,0},{5,1},{6,2},{7,3},{8,12},{9,13},{10,... | collective-permute-start | bytes 98312 | tf_op jit(solution)/shard_map/ppermute | solution.py:628
  38.1 0.0 collective-permute-done.13.got_gx
  38.1 1.0 %first_gradient.1 = (bf16[24,1536]{1,0:T(8,128)(2,1)S(1)}, f32[8,384]{1,0:T(8,128)S(1)}, f32[8,128]{1,0:T(8,128)S(1)}, f32[8,128]{1,0:T(8,128)S(1)}, f32[8,128]{1,0:T(8,128)S(1)}) custom-call(f32[128,384]{1,0:T(8,128)S(1)} %get-tuple-element.103.g_h, f32[128,128]{1,0:T(8,128)S(1)} %collective-permute-done.13.got_gx, ...), custom_call_target="tpu_custom_call" | custom-call | flops 1200000000 | bytes 3600000 | tf_op jit(solution)/shard_map/first_gradient/pallas_call | solution.py:576
  39.1 0.7 %collective-permute-start.15 = (f32[8,128]{1,0:T(8,128)S(1)}, f32[8,128]{1,0:T(8,128)S(1)}, u32[]{:S(2)}, u32[]{:S(2)}) collective-permute-start(f32[8,128]{1,0:T(8,128)S(1)} %get-tuple-element.116), channel_id=1, source_target_pairs={{0,15},{1,2},{2,1},{3,4},{4,3},{5,6},{6,5},{7,8},{8,7},{9,10},{10,... | collective-permute-start | bytes 12296 | tf_op jit(solution)/shard_map/ppermute | solution.py:595
  39.9 0.5 %collective-permute-start.16 = (f32[8,128]{1,0:T(8,128)S(1)}, f32[8,128]{1,0:T(8,128)S(1)}, u32[]{:S(2)}, u32[]{:S(2)}) collective-permute-start(f32[8,128]{1,0:T(8,128)S(1)} %get-tuple-element.117), channel_id=1, source_target_pairs={{0,16},{16,0},{1,17},{17,1},{2,18},{18,2},{3,19},{19,3},{4,20},{20... | collective-permute-start | bytes 12296 | tf_op jit(solution)/shard_map/ppermute | solution.py:600
  40.4 0.5 %collective-permute-start.17 = (f32[8,128]{1,0:T(8,128)S(1)}, f32[8,128]{1,0:T(8,128)S(1)}, u32[]{:S(2)}, u32[]{:S(2)}) collective-permute-start(f32[8,128]{1,0:T(8,128)S(1)} %get-tuple-element.118), channel_id=1, source_target_pairs={{0,1},{1,0},{2,3},{3,2},{4,5},{5,4},{6,7},{7,6},{8,9},{9,8},{10,11... | collective-permute-start | bytes 12296 | tf_op jit(solution)/shard_map/ppermute | solution.py:590
  40.8 0.0 collective-permute-done.12
  40.8 1.5 %collective-permute-start.18 = (f32[8,128]{1,0:T(8,128)S(1)}, f32[8,128]{1,0:T(8,128)S(1)}, u32[]{:S(2)}, u32[]{:S(2)}) collective-permute-start(f32[8,128]{1,0:T(8,128)S(1)} %slice_add_fusion.rest_0_), channel_id=1, source_target_pairs={{0,16},{16,0},{1,17},{17,1},{2,18},{18,2},{3,19},{19,3},{4,20},{20... | collective-permute-start | bytes 12296 | tf_op jit(solution)/shard_map/ppermute | solution.py:628
  42.3 0.3 local.1.g_pos
  42.7 2.3 %collective-permute-done.15.got_chip = f32[8,128]{1,0:T(8,128)S(1)} collective-permute-done((f32[8,128]{1,0:T(8,128)S(1)}, f32[8,128]{1,0:T(8,128)S(1)}, u32[]{:S(2)}, u32[]{:S(2)}) %collective-permute-start.15) | collective-permute-done | bytes 4128 | tf_op jit(solution)/shard_map/ppermute | solution.py:595
  44.9 0.1 chip_forces.1.g_sum
  45.1 0.8 %forces.1 = (f32[3,384]{1,0:T(4,128)}, f32[1,1]{1,0:T(1,128)}) custom-call(f32[8,384]{1,0:T(8,128)S(1)} %chip_forces.1.g_sum, f32[8,128]{1,0:T(8,128)S(1)} %collective-permute-done.16.got_gx, f32[8,128]{1,0:T(8,128)S(1)} %collective-permute-done.17.got_core, bf16[256,384]{1,0:T(8,128)(2,1)S(1)} %get-tuple-element.110.send_t, ...), custom_call_target="tpu_custom_call" | custom-call | flops 1000000000 | bytes 3000000 | tf_op jit(solution)/shard_map/forces/pallas_call | solution.py:576
  (11 shorter events, 0.0 us)
Async XLA Ops:
  1.4 7.9 %collective-permute-start.1 = (f32[24,128]{1,0:T(8,128)S(1)}, f32[24,128]{1,0:T(8,128)S(1)}, u32[]{:S(2)}, u32[]{:S(2)}) collective-permute-start(f32[24,128]{1,0:T(8,128)S(1)} %pack.1.own), channel_id=1, source_target_pairs={{0,15},{1,2},{2,1},{3,4},{4,3},{5,6},{6,5},{7,8},{8,7},{9,10},{10,... | collective-permute-start | bytes 36872 | tf_op jit(solution)/shard_map/ppermute | solution.py:595
  6.9 2.4 %collective-permute-start = (f32[24,128]{1,0:T(8,128)S(1)}, f32[24,128]{1,0:T(8,128)S(1)}, u32[]{:S(2)}, u32[]{:S(2)}) collective-permute-start(f32[24,128]{1,0:T(8,128)S(1)} %pack.1.own), channel_id=1, source_target_pairs={{0,1},{1,0},{2,3},{3,2},{4,5},{5,4},{6,7},{7,6},{8,9},{9,8},{10,11... | collective-permute-start | bytes 36872 | tf_op jit(solution)/shard_map/ppermute | solution.py:590
  9.4 7.1 %collective-permute-start.4 = (f32[16,128]{1,0:T(8,128)S(1)}, f32[16,128]{1,0:T(8,128)S(1)}, u32[]{:S(2)}, u32[]{:S(2)}) collective-permute-start(f32[16,128]{1,0:T(8,128)S(1)} %get-tuple-element.67), channel_id=1, source_target_pairs={{0,15},{1,2},{2,1},{3,4},{4,3},{5,6},{6,5},{7,8},{8,7},{9,10},{10,... | collective-permute-start | bytes 24584 | tf_op jit(solution)/shard_map/ppermute | solution.py:595
  12.9 3.6 %collective-permute-start.2 = (f32[8,128]{1,0:T(8,128)S(1)}, f32[8,128]{1,0:T(8,128)S(1)}, u32[]{:S(2)}, u32[]{:S(2)}) collective-permute-start(f32[8,128]{1,0:T(8,128)S(1)} %get-tuple-element.65), channel_id=1, source_target_pairs={{0,16},{16,0},{1,17},{17,1},{2,18},{18,2},{3,19},{19,3},{4,20},{20... | collective-permute-start | bytes 12296 | tf_op jit(solution)/shard_map/ppermute | solution.py:600
  14.4 2.1 %collective-permute-start.3 = (f32[8,128]{1,0:T(8,128)S(1)}, f32[8,128]{1,0:T(8,128)S(1)}, u32[]{:S(2)}, u32[]{:S(2)}) collective-permute-start(f32[8,128]{1,0:T(8,128)S(1)} %get-tuple-element.66), channel_id=1, source_target_pairs={{0,1},{1,0},{2,3},{3,2},{4,5},{5,4},{6,7},{7,6},{8,9},{9,8},{10,11... | collective-permute-start | bytes 12296 | tf_op jit(solution)/shard_map/ppermute | solution.py:590
  16.5 5.7 %copy-start = (f32[5]{0:T(128)S(1)}, f32[5]{0:T(128)}, u32[]{:S(2)}) copy-start(f32[5]{0:T(128)} %atom_ref.1) | copy-start | bytes 64
  18.4 6.0 %collective-permute-start.6 = (f32[64,128]{1,0:T(8,128)S(1)}, f32[64,128]{1,0:T(8,128)S(1)}, u32[]{:S(2)}, u32[]{:S(2)}) collective-permute-start(f32[64,128]{1,0:T(8,128)S(1)} %get-tuple-element.77), channel_id=1, source_target_pairs={{0,1},{1,0},{2,3},{3,2},{4,5},{5,4},{6,7},{7,6},{8,9},{9,8},{10,11... | collective-permute-start | bytes 98312 | tf_op jit(solution)/shard_map/ppermute | solution.py:590
  18.5 6.1 %collective-permute-start.7 = (f32[64,128]{1,0:T(8,128)S(1)}, f32[64,128]{1,0:T(8,128)S(1)}, u32[]{:S(2)}, u32[]{:S(2)}) collective-permute-start(f32[64,128]{1,0:T(8,128)S(1)} %get-tuple-element.78), channel_id=1, source_target_pairs={{0,15},{1,2},{2,1},{3,4},{4,3},{5,6},{6,5},{7,8},{8,7},{9,10},{10,... | collective-permute-start | bytes 98312 | tf_op jit(solution)/shard_map/ppermute | solution.py:595
  20.7 4.3 %collective-permute-start.5 = (f32[128,128]{1,0:T(8,128)S(1)}, f32[128,128]{1,0:T(8,128)S(1)}, u32[]{:S(2)}, u32[]{:S(2)}) collective-permute-start(f32[128,128]{1,0:T(8,128)S(1)} %get-tuple-element.76), channel_id=1, source_target_pairs={{0,16},{16,0},{1,17},{17,1},{2,18},{18,2},{3,19},{19,3},{4,20},{20... | collective-permute-start | bytes 196616 | tf_op jit(solution)/shard_map/ppermute | solution.py:600
  26.7 1.6 %collective-permute-start.8 = (f32[64,128]{1,0:T(8,128)S(1)}, f32[64,128]{1,0:T(8,128)S(1)}, u32[]{:S(2)}, u32[]{:S(2)}) collective-permute-start(f32[64,128]{1,0:T(8,128)S(1)} %get-tuple-element.83), channel_id=1, source_target_pairs={{0,1},{1,0},{2,3},{3,2},{4,5},{5,4},{6,7},{7,6},{8,9},{9,8},{10,11... | collective-permute-start | bytes 98312 | tf_op jit(solution)/shard_map/ppermute | solution.py:628
  28.3 4.9 %collective-permute-start.9 = (f32[64,128]{1,0:T(8,128)S(1)}, f32[64,128]{1,0:T(8,128)S(1)}, u32[]{:S(2)}, u32[]{:S(2)}) collective-permute-start(f32[64,128]{1,0:T(8,128)S(1)} %add.14), channel_id=1, source_target_pairs={{0,8},{1,9},{2,10},{3,11},{4,12},{5,13},{6,14},{7,15},{8,0},{9,1},... | collective-permute-start | bytes 98312 | tf_op jit(solution)/shard_map/ppermute | solution.py:628
  29.2 6.4 %collective-permute-start.11 = (f32[64,128]{1,0:T(8,128)S(1)}, f32[64,128]{1,0:T(8,128)S(1)}, u32[]{:S(2)}, u32[]{:S(2)}) collective-permute-start(f32[64,128]{1,0:T(8,128)S(1)} %get-tuple-element.95), channel_id=1, source_target_pairs={{0,15},{1,2},{2,1},{3,4},{4,3},{5,6},{6,5},{7,8},{8,7},{9,10},{10,... | collective-permute-start | bytes 98312 | tf_op jit(solution)/shard_map/ppermute | solution.py:595
  31.0 7.1 %collective-permute-start.14 = (f32[64,128]{1,0:T(8,128)S(1)}, f32[64,128]{1,0:T(8,128)S(1)}, u32[]{:S(2)}, u32[]{:S(2)}) collective-permute-start(f32[64,128]{1,0:T(8,128)S(1)} %get-tuple-element.105), channel_id=1, source_target_pairs={{0,1},{1,0},{2,3},{3,2},{4,5},{5,4},{6,7},{7,6},{8,9},{9,8},{10,11... | collective-permute-start | bytes 98312 | tf_op jit(solution)/shard_map/ppermute | solution.py:590
  31.0 7.1 %collective-permute-start.13 = (f32[128,128]{1,0:T(8,128)S(1)}, f32[128,128]{1,0:T(8,128)S(1)}, u32[]{:S(2)}, u32[]{:S(2)}) collective-permute-start(f32[128,128]{1,0:T(8,128)S(1)} %get-tuple-element.104), channel_id=1, source_target_pairs={{0,16},{16,0},{1,17},{17,1},{2,18},{18,2},{3,19},{19,3},{4,20},{20... | collective-permute-start | bytes 196616 | tf_op jit(solution)/shard_map/ppermute | solution.py:600
  33.2 3.6 %collective-permute-start.10 = (f32[8,128]{1,0:T(8,128)S(1)}, f32[8,128]{1,0:T(8,128)S(1)}, u32[]{:S(2)}, u32[]{:S(2)}) collective-permute-start(f32[8,128]{1,0:T(8,128)S(1)} %slice_add_fusion.1), channel_id=1, source_target_pairs={{0,2},{1,3},{2,0},{3,1},{4,6},{5,7},{6,4},{7,5},{8,10},{9,11},{10,... | collective-permute-start | bytes 12296 | tf_op jit(solution)/shard_map/ppermute | solution.py:628
  36.8 4.0 %collective-permute-start.12 = (f32[64,128]{1,0:T(8,128)S(1)}, f32[64,128]{1,0:T(8,128)S(1)}, u32[]{:S(2)}, u32[]{:S(2)}) collective-permute-start(f32[64,128]{1,0:T(8,128)S(1)} %pad.4), channel_id=1, source_target_pairs={{0,4},{1,5},{2,6},{3,7},{4,0},{5,1},{6,2},{7,3},{8,12},{9,13},{10,... | collective-permute-start | bytes 98312 | tf_op jit(solution)/shard_map/ppermute | solution.py:628
  39.1 5.8 %collective-permute-start.15 = (f32[8,128]{1,0:T(8,128)S(1)}, f32[8,128]{1,0:T(8,128)S(1)}, u32[]{:S(2)}, u32[]{:S(2)}) collective-permute-start(f32[8,128]{1,0:T(8,128)S(1)} %get-tuple-element.116), channel_id=1, source_target_pairs={{0,15},{1,2},{2,1},{3,4},{4,3},{5,6},{6,5},{7,8},{8,7},{9,10},{10,... | collective-permute-start | bytes 12296 | tf_op jit(solution)/shard_map/ppermute | solution.py:595
  39.9 5.2 %collective-permute-start.16 = (f32[8,128]{1,0:T(8,128)S(1)}, f32[8,128]{1,0:T(8,128)S(1)}, u32[]{:S(2)}, u32[]{:S(2)}) collective-permute-start(f32[8,128]{1,0:T(8,128)S(1)} %get-tuple-element.117), channel_id=1, source_target_pairs={{0,16},{16,0},{1,17},{17,1},{2,18},{18,2},{3,19},{19,3},{4,20},{20... | collective-permute-start | bytes 12296 | tf_op jit(solution)/shard_map/ppermute | solution.py:600
  40.4 4.7 %collective-permute-start.17 = (f32[8,128]{1,0:T(8,128)S(1)}, f32[8,128]{1,0:T(8,128)S(1)}, u32[]{:S(2)}, u32[]{:S(2)}) collective-permute-start(f32[8,128]{1,0:T(8,128)S(1)} %get-tuple-element.118), channel_id=1, source_target_pairs={{0,1},{1,0},{2,3},{3,2},{4,5},{5,4},{6,7},{7,6},{8,9},{9,8},{10,11... | collective-permute-start | bytes 12296 | tf_op jit(solution)/shard_map/ppermute | solution.py:590
  40.8 4.2 %collective-permute-start.18 = (f32[8,128]{1,0:T(8,128)S(1)}, f32[8,128]{1,0:T(8,128)S(1)}, u32[]{:S(2)}, u32[]{:S(2)}) collective-permute-start(f32[8,128]{1,0:T(8,128)S(1)} %slice_add_fusion.rest_0_), channel_id=1, source_target_pairs={{0,16},{16,0},{1,17},{17,1},{2,18},{18,2},{3,19},{19,3},{4,20},{20... | collective-permute-start | bytes 12296 | tf_op jit(solution)/shard_map/ppermute | solution.py:628

commit v6 on v5

--- a/solution.py
+++ b/solution.py
@@ -15,7 +15,7 @@
 bf16 = jnp.bfloat16
 ROWS = 8
 LANES = 128
-TALL = 64
+TALL = 8
 CHIP_ROWS = 16
 SUMS_UNROLL = 16
 EDGE_UNROLL = 16
@@ -620,12 +620,13 @@
     )
 
 
-def partners(value, axis, bits):
-    size = lax.axis_size(axis)
+def partners(value, bits):
+    axes = ("gx", "yz")
+    size = lax.axis_size(axes)
     steps = [0]
     for bit in bits:
         steps += [step ^ (1 << bit) for step in steps]
-    return [lax.ppermute(value, axis, [(i, i ^ step) for i in range(size)]) for step in steps[1:]]
+    return [lax.ppermute(value, axes, [(i, i ^ step) for i in range(size)]) for step in steps[1:]]
 
 
 def together(values, other):
@@ -758,7 +759,8 @@
         us=2.5,
     )
     bits = (lax.axis_size("yz") - 1).bit_length()
-    got_sums = partners(tally, "yz", [0])
+    all_bits = (lax.axis_size(("gx", "yz")) - 1).bit_length()
+    got_sums = partners(tally, [0])
     g_feat, g_off = call(
         second_gradient_kernel,
         [(channels, edges), (ROWS, edges)],
@@ -769,7 +771,7 @@
     )
     got_sums, g_off = together(got_sums, g_off)
     tally = sum(got_sums, tally)
-    got_sums = partners(tally, "yz", [bits - 1] if bits > 1 else [])
+    got_sums = partners(tally, [bits - 1] if bits > 1 else [])
     left, send_gx, send_core, send_chip, g_ghost, g_target_two = call(
         ghost_gradient_kernel,
         [((2 * channels + 3 * ROWS, edges), bf16), square, half, half, (ROWS, ghosts), (ROWS, slots)],
@@ -783,8 +785,8 @@
     got_chip = swap_chip(send_chip)
     got_gx = return_gx(send_gx)
     got_core = swap_core(send_core)
-    tally = tally[:ROWS]
-    got_sums = partners(tally, "yz", [1] if bits > 2 else [])
+    (slope_one,), tally = together([slope_one], tally)
+    got_sums = partners(tally, [bit for bit in range(1, bits - 1) if bit != 2])
     factors, g_h, g_local_two = call(
         factor_kernel,
         [(4, channels, edges), flat, (ROWS, slots)],
@@ -793,10 +795,6 @@
         name="factors",
         us=3.0,
     )
-    got_sums, got_chip = together(got_sums, got_chip)
-    tally = sum(got_sums, tally)
-    tally = jnp.pad(tally, ((0, TALL - ROWS), (0, 0)))
-    got_sums = partners(tally, "yz", range(2, bits - 1))
     left, g_target_one, send_gx, send_core, send_chip = call(
         first_gradient_kernel,
         [((3 * ROWS, edges), bf16), (ROWS, slots), (8, LANES), (8, LANES), (8, LANES)],
@@ -808,6 +806,7 @@
     )
     got_sums, left = together(got_sums, left)
     tally = sum(got_sums, tally)
+    got_sums = partners(tally, [2] if bits > 3 else [])
     got_chip = swap_chip(send_chip)
     got_gx = return_gx(send_gx)
     got_core = swap_core(send_core)
@@ -819,8 +818,8 @@
         name="local",
         us=0.5,
     )
-    tally = tally[:ROWS]
-    tallies = [tally] + partners(tally, "gx", range((lax.axis_size("gx") - 1).bit_length()))
+    tally = sum(got_sums, tally)[:ROWS]
+    tallies = [tally] + partners(tally, range(bits, all_bits))
     (g_sum,) = call(
         chip_force_kernel, [(ROWS, slots)], [], [g_pos, got_chip, send_t], name="chip_forces", us=0.1
     )

time: 46.1 us -> 45.1 us (0.978)
  waiting for transfers between devices: 6.57 us -> 5.01 us
  starting transfers between devices: 22.4 us -> 23.1 us
    ppermute x5, waiting for transfers between devices: 1.91 us -> 0.83 us  [partners(): lax.ppermute(value, axes, [(i, i ^ step) for i in range(size)])]
    ppermute x5, starting transfers between devices: 13.7 us -> 14.6 us  [swap_chip(): lax.ppermute(value, 'yz', [(i, (i + 1 if i % 2 else i - 1) % size) for i...]
    ppermute x5, starting transfers between devices: 3.1 us -> 2.3 us  [partners(): lax.ppermute(value, axes, [(i, i ^ step) for i in range(size)])]
    ppermute x4, starting transfers between devices: 5.07 us -> 5.56 us  [shift(): lax.ppermute(value, axis, [(i, (i + by) % size) for i in range(size)])]
    ppermute x5, waiting for transfers between devices: 2.44 us -> 1.96 us  [swap_chip(): lax.ppermute(value, 'yz', [(i, (i + 1 if i % 2 else i - 1) % size) for i...]
  transfers between devices with their start and end apart: 19 -> 19, of which waited for: 6 -> 6; matrix products, arithmetic and copies ran while one was open for 0% -> 0% of each run, Pallas kernels for 23% -> 24%
where the time goes in v6:
time: 45.1 us; the launch traced here: 44.9 us
  starting transfers between devices  23.1 us (51%)
  Pallas kernels  15.9 us (35%)
  waiting for transfers between devices  5.01 us (11%)
  between operations  0.84 us (2%)
    pallas_call x14, Pallas kernels, call(): pl.pallas_call(kernel, out_shape=shapes, in_specs=[in_smem] * len(scalars...  15.9 us
    ppermute x5, starting transfers between devices, swap_chip(): lax.ppermute(value, 'yz', [(i, (i + 1 if i % 2 else i - 1) % size) for i...  14.6 us
    ppermute x4, starting transfers between devices, shift(): lax.ppermute(value, axis, [(i, (i + by) % size) for i in range(size)])  5.56 us
    ppermute x5, starting transfers between devices, partners(): lax.ppermute(value, axes, [(i, i ^ step) for i in range(size)])  2.3 us
    ppermute x4, waiting for transfers between devices, shift(): lax.ppermute(value, axis, [(i, (i + by) % size) for i in range(size)])  2.21 us
    ppermute x5, waiting for transfers between devices, swap_chip(): lax.ppermute(value, 'yz', [(i, (i + 1 if i % 2 else i - 1) % size) for i...  1.96 us
  transfers between devices with their start and end apart: 19, of which 6 were waited for; matrix products, arithmetic and copies ran while one was open for 0% of the time, Pallas kernels for 24%

profile of v6, /device:TPU:0, one launch (start us, length us, event | category | flops | bytes accessed | tf_op | source)
XLA Modules:
  0.0 44.9 jit_solution(11806336762736377119)
XLA Ops:
  0.6 0.7 %pack.1.own = f32[24,128]{1,0:T(8,128)S(1)} custom-call(s32[1,2]{1,0:T(1,128)} %bitcast.4, s32[2]{0:T(128)} %count_hbm.1, f32[3,256]{1,0:T(4,128)} %pos_hbm.1, s32[2,128]{1,0:T(2,128)} %bitcast.3), custom_call_target="tpu_custom_call" | custom-call | flops 1000000000 | bytes 3000000 | tf_op jit(solution)/shard_map/pack/pallas_call | solution.py:576
  1.4 5.5 %collective-permute-start.1 = (f32[24,128]{1,0:T(8,128)S(1)}, f32[24,128]{1,0:T(8,128)S(1)}, u32[]{:S(2)}, u32[]{:S(2)}) collective-permute-start(f32[24,128]{1,0:T(8,128)S(1)} %pack.1.own), channel_id=1, source_target_pairs={{0,15},{1,2},{2,1},{3,4},{4,3},{5,6},{6,5},{7,8},{8,7},{9,10},{10,... | collective-permute-start | bytes 36872 | tf_op jit(solution)/shard_map/ppermute | solution.py:595
  6.9 0.0 collective-permute-start
  6.9 2.4 %prepare.1 = (bf16[640,1536]{1,0:T(8,128)(2,1)S(1)}, bf16[384,256]{1,0:T(8,128)(2,1)S(1)}, f32[2,8,1536]{2,1,0:T(8,128)S(1)}, bf16[2,384,24]{2,1,0:T(8,128)(2,1)...) custom-call(f32[2,8]{1,0:T(2,128)} %gammas_hbm.1, ...), custom_call_target="tpu_custom_call" | custom-call | flops 3000000000 | bytes 9000000 | tf_op jit(solution)/shard_map/prepare/pallas_call | solution.py:576
  9.3 0.0 collective-permute-done.1.chip
  9.3 0.0 collective-permute-done.core
  9.3 0.1 assemble.1
  9.4 3.5 %collective-permute-start.4 = (f32[16,128]{1,0:T(8,128)S(1)}, f32[16,128]{1,0:T(8,128)S(1)}, u32[]{:S(2)}, u32[]{:S(2)}) collective-permute-start(f32[16,128]{1,0:T(8,128)S(1)} %get-tuple-element.67), channel_id=1, source_target_pairs={{0,15},{1,2},{2,1},{3,4},{4,3},{5,6},{6,5},{7,8},{8,7},{9,10},{10,... | collective-permute-start | bytes 24584 | tf_op jit(solution)/shard_map/ppermute | solution.py:595
  12.9 1.5 %collective-permute-start.2 = (f32[8,128]{1,0:T(8,128)S(1)}, f32[8,128]{1,0:T(8,128)S(1)}, u32[]{:S(2)}, u32[]{:S(2)}) collective-permute-start(f32[8,128]{1,0:T(8,128)S(1)} %get-tuple-element.65), channel_id=1, source_target_pairs={{0,16},{16,0},{1,17},{17,1},{2,18},{18,2},{3,19},{19,3},{4,20},{20... | collective-permute-start | bytes 12296 | tf_op jit(solution)/shard_map/ppermute | solution.py:600
  14.4 0.3 own_positions.1.found_own
  14.7 1.8 %collective-permute-done.2.got_gx = f32[8,128]{1,0:T(8,128)S(1)} collective-permute-done((f32[8,128]{1,0:T(8,128)S(1)}, f32[8,128]{1,0:T(8,128)S(1)}, u32[]{:S(2)}, u32[]{:S(2)}) %collective-permute-start.2) | collective-permute-done | bytes 4128 | tf_op jit(solution)/shard_map/ppermute | solution.py:600
  16.5 0.0 collective-permute-done.3.got_core
  16.5 0.0 collective-permute-done.4.got_chip
  16.5 1.9 %first_layer.1 = (f32[128,384]{1,0:T(8,128)S(1)}, f32[128,384]{1,0:T(8,128)S(1)}, f32[128,128]{1,0:T(8,128)S(1)}, f32[64,128]{1,0:T(8,128)S(1)}, f32[64,128]{1,0...) custom-call(f32[8,1536]{1,0:T(8,128)S(1)} %own_positions.1.found_own, ...), custom_call_target="tpu_custom_call" | custom-call | flops 2500000000 | bytes 7500000 | tf_op jit(solution)/shard_map/first_layer/pallas_call | solution.py:576
  18.4 0.1 collective-permute-start.6
  18.5 2.2 %collective-permute-start.7 = (f32[64,128]{1,0:T(8,128)S(1)}, f32[64,128]{1,0:T(8,128)S(1)}, u32[]{:S(2)}, u32[]{:S(2)}) collective-permute-start(f32[64,128]{1,0:T(8,128)S(1)} %get-tuple-element.79), channel_id=1, source_target_pairs={{0,15},{1,2},{2,1},{3,4},{4,3},{5,6},{6,5},{7,8},{8,7},{9,10},{10,... | collective-permute-start | bytes 98312 | tf_op jit(solution)/shard_map/ppermute | solution.py:595
  20.7 1.5 %collective-permute-start.5 = (f32[128,128]{1,0:T(8,128)S(1)}, f32[128,128]{1,0:T(8,128)S(1)}, u32[]{:S(2)}, u32[]{:S(2)}) collective-permute-start(f32[128,128]{1,0:T(8,128)S(1)} %get-tuple-element.77), channel_id=1, source_target_pairs={{0,16},{16,0},{1,17},{17,1},{2,18},{18,2},{3,19},{19,3},{4,20},{20... | collective-permute-start | bytes 196616 | tf_op jit(solution)/shard_map/ppermute | solution.py:600
  22.2 2.2 %radials.1 = (f32[384,1536]{1,0:T(8,128)S(1)}, f32[384,1536]{1,0:T(8,128)S(1)}, f32[384,1536]{1,0:T(8,128)S(1)}, f32[8,128]{1,0:T(8,128)S(1)}, f32[128,1536]{1,0:T(8,128)S(1)}) custom-call(f32[5]{0:T(128)S(1)} %copy-done, f32[8,8,1536]{2,1,0:T(8,128)S(1)} %get-tuple-element.73.geo, f32[2,8,1536]{2,1,0:T(8,128)S(1)} %get-tuple-element.68.gamma, ...), custom_call_target="tpu_custom_call" | custom-call | flops 2000000000 | bytes 6000000 | tf_op jit(solution)/shard_map/radials/pallas_call | solution.py:576
  24.4 0.0 collective-permute-done.6.got_core
  24.4 0.2 collective-permute-done.7.got_chip
  24.6 0.4 collective-permute-done.5.got_gx
  24.9 1.7 %second_layer.1 = (f32[128,1536]{1,0:T(8,128)S(1)}, f32[9,128,384]{2,1,0:T(8,128)S(1)}, f32[128,384]{1,0:T(8,128)S(1)}, f32[128,384]{1,0:T(8,128)S(1)}, f32[8,128]{1,0:T(8,128)S(1)}) custom-call(f32[8,128]{1,0:T(8,128)S(1)} %get-tuple-element.76.base, f32[8,384]{1,0:T(8,128)S(1)} %get-tuple-element.63.table, f32[128,384]{1,0:T(8,128)S(1)} %get-tuple-element.74.h_one, ...), custom_call_target="tpu_custom_call" | custom-call | flops 2500000000 | bytes 7500000 | tf_op jit(solution)/shard_map/second_layer/pallas_call | solution.py:576
  26.6 0.1 collective-permute-start.8
  26.7 1.5 %second_gradient.1 = (f32[128,1536]{1,0:T(8,128)S(1)}, f32[8,1536]{1,0:T(8,128)S(1)}) custom-call(f32[8,8,1536]{2,1,0:T(8,128)S(1)} %get-tuple-element.73.geo, f32[384,1536]{1,0:T(8,128)S(1)} %get-tuple-element.81.rad_ref, f32[384,1536]{1,0:T(8,128)S(1)} %get-tuple-element.85.slope_ref, f32[128,1536]{1,0:T(8,128)S(1)} %get-tuple-element.86.feat_ref, ...), custom_call_target="tpu_custom_call" | custom-call | flops 2500000000 | bytes 7500000 | tf_op jit(solution)/shard_map/second_gradient/pallas_call | solution.py:576
  28.2 0.0 collective-permute-done.8
  28.2 0.1 collective-permute-start.9
  28.3 0.7 %ghost_gradient.1 = (bf16[280,1536]{1,0:T(8,128)(2,1)S(1)}, f32[128,128]{1,0:T(8,128)S(1)}, f32[64,128]{1,0:T(8,128)S(1)}, f32[64,128]{1,0:T(8,128)S(1)}, f32[8,256]{1,0:T(8,128)S(1)}, /*index=5*/f32[8,384]{1,0:T(8,128)S(1)}) custom-call(f32[128,1536]{1,0:T(8,128)S(1)} %get-tuple-element.91.g_feat, f32[8,1536]{1,0:T(8,128)S(1)} %get-tuple-element.92.g_off, ...), custom_call_target="tpu_custom_call" | custom-call | flops 1500000000 | bytes 4500000 | tf_op jit(solution)/shard_map/ghost_gradient/pallas_call | solution.py:576
  29.1 0.6 %collective-permute-start.12 = (f32[64,128]{1,0:T(8,128)S(1)}, f32[64,128]{1,0:T(8,128)S(1)}, u32[]{:S(2)}, u32[]{:S(2)}) collective-permute-start(f32[64,128]{1,0:T(8,128)S(1)} %get-tuple-element.105), channel_id=1, source_target_pairs={{0,1},{1,0},{2,3},{3,2},{4,5},{5,4},{6,7},{7,6},{8,9},{9,8},{10,11... | collective-permute-start | bytes 98312 | tf_op jit(solution)/shard_map/ppermute | solution.py:590
  29.6 1.8 %collective-permute-start.13 = (f32[64,128]{1,0:T(8,128)S(1)}, f32[64,128]{1,0:T(8,128)S(1)}, u32[]{:S(2)}, u32[]{:S(2)}) collective-permute-start(f32[64,128]{1,0:T(8,128)S(1)} %get-tuple-element.106), channel_id=1, source_target_pairs={{0,15},{1,2},{2,1},{3,4},{4,3},{5,6},{6,5},{7,8},{8,7},{9,10},{10,... | collective-permute-start | bytes 98312 | tf_op jit(solution)/shard_map/ppermute | solution.py:595
  31.4 1.5 %collective-permute-start.11 = (f32[128,128]{1,0:T(8,128)S(1)}, f32[128,128]{1,0:T(8,128)S(1)}, u32[]{:S(2)}, u32[]{:S(2)}) collective-permute-start(f32[128,128]{1,0:T(8,128)S(1)} %get-tuple-element.104), channel_id=1, source_target_pairs={{0,16},{16,0},{1,17},{17,1},{2,18},{18,2},{3,19},{19,3},{4,20},{20... | collective-permute-start | bytes 196616 | tf_op jit(solution)/shard_map/ppermute | solution.py:600
  32.9 0.0 collective-permute-start.10
  32.9 2.2 %factors.1 = (f32[4,128,1536]{2,1,0:T(8,128)S(1)}, f32[128,384]{1,0:T(8,128)S(1)}, f32[8,384]{1,0:T(8,128)S(1)}) custom-call(f32[8,8,1536]{2,1,0:T(8,128)S(1)} %get-tuple-element.73.geo, f32[384,1536]{1,0:T(8,128)S(1)} %get-tuple-element.97.rad_ref, f32[384,1536]{1,0:T(8,128)S(1)} %get-tuple-element.98.slope_ref, ...), custom_call_target="tpu_custom_call" | custom-call | flops 3000000000 | bytes 9000000 | tf_op jit(solution)/shard_map/factors/pallas_call | solution.py:576
  35.2 0.0 collective-permute-done.12.got_core
  35.2 0.5 %collective-permute-done.13.got_chip = f32[64,128]{1,0:T(8,128)S(1)} collective-permute-done((f32[64,128]{1,0:T(8,128)S(1)}, f32[64,128]{1,0:T(8,128)S(1)}, u32[]{:S(2)}, u32[]{:S(2)}) %collective-permute-start.13) | collective-permute-done | bytes 32800 | tf_op jit(solution)/shard_map/ppermute | solution.py:595
  35.7 0.0 collective-permute-done.11.got_gx
  35.7 1.0 %first_gradient.1 = (bf16[24,1536]{1,0:T(8,128)(2,1)S(1)}, f32[8,384]{1,0:T(8,128)S(1)}, f32[8,128]{1,0:T(8,128)S(1)}, f32[8,128]{1,0:T(8,128)S(1)}, f32[8,128]{1,0:T(8,128)S(1)}) custom-call(f32[128,384]{1,0:T(8,128)S(1)} %get-tuple-element.103.g_h, f32[128,128]{1,0:T(8,128)S(1)} %collective-permute-done.11.got_gx, ...), custom_call_target="tpu_custom_call" | custom-call | flops 1200000000 | bytes 3600000 | tf_op jit(solution)/shard_map/first_gradient/pallas_call | solution.py:576
  36.7 0.0 collective-permute-done.10
  36.7 0.7 %collective-permute-start.17 = (f32[8,128]{1,0:T(8,128)S(1)}, f32[8,128]{1,0:T(8,128)S(1)}, u32[]{:S(2)}, u32[]{:S(2)}) collective-permute-start(f32[8,128]{1,0:T(8,128)S(1)} %add.14), channel_id=1, source_target_pairs={{0,4},{1,5},{2,6},{3,7},{4,0},{5,1},{6,2},{7,3},{8,12},{9,13},{10,... | collective-permute-start | bytes 12296 | tf_op jit(solution)/shard_map/ppermute | solution.py:629
  37.4 1.7 %collective-permute-start.14 = (f32[8,128]{1,0:T(8,128)S(1)}, f32[8,128]{1,0:T(8,128)S(1)}, u32[]{:S(2)}, u32[]{:S(2)}) collective-permute-start(f32[8,128]{1,0:T(8,128)S(1)} %get-tuple-element.116), channel_id=1, source_target_pairs={{0,15},{1,2},{2,1},{3,4},{4,3},{5,6},{6,5},{7,8},{8,7},{9,10},{10,... | collective-permute-start | bytes 12296 | tf_op jit(solution)/shard_map/ppermute | solution.py:595
  39.1 1.0 %collective-permute-start.15 = (f32[8,128]{1,0:T(8,128)S(1)}, f32[8,128]{1,0:T(8,128)S(1)}, u32[]{:S(2)}, u32[]{:S(2)}) collective-permute-start(f32[8,128]{1,0:T(8,128)S(1)} %get-tuple-element.117), channel_id=1, source_target_pairs={{0,16},{16,0},{1,17},{17,1},{2,18},{18,2},{3,19},{19,3},{4,20},{20... | collective-permute-start | bytes 12296 | tf_op jit(solution)/shard_map/ppermute | solution.py:600
  40.1 0.0 collective-permute-start.16
  40.1 0.3 local.1.g_pos
  40.5 1.4 %collective-permute-start.18 = (f32[8,128]{1,0:T(8,128)S(1)}, f32[8,128]{1,0:T(8,128)S(1)}, u32[]{:S(2)}, u32[]{:S(2)}) collective-permute-start(f32[8,128]{1,0:T(8,128)S(1)} %add.15.rest_0_), channel_id=1, source_target_pairs={{0,16},{1,17},{2,18},{3,19},{4,20},{5,21},{6,22},{7,23},{8,24},{9,... | collective-permute-start | bytes 12296 | tf_op jit(solution)/shard_map/ppermute | solution.py:629
  41.9 1.3 %collective-permute-done.14.got_chip = f32[8,128]{1,0:T(8,128)S(1)} collective-permute-done((f32[8,128]{1,0:T(8,128)S(1)}, f32[8,128]{1,0:T(8,128)S(1)}, u32[]{:S(2)}, u32[]{:S(2)}) %collective-permute-start.14) | collective-permute-done | bytes 4128 | tf_op jit(solution)/shard_map/ppermute | solution.py:595
  43.2 0.1 chip_forces.1.g_sum
  43.3 0.0 collective-permute-done.15.got_gx
  43.3 0.8 %collective-permute-done.18.rest_1_ = f32[8,128]{1,0:T(8,128)S(1)} collective-permute-done((f32[8,128]{1,0:T(8,128)S(1)}, f32[8,128]{1,0:T(8,128)S(1)}, u32[]{:S(2)}, u32[]{:S(2)}) %collective-permute-start.18) | collective-permute-done | bytes 4128 | tf_op jit(solution)/shard_map/ppermute | solution.py:629
  44.1 0.8 %forces.1 = (f32[3,384]{1,0:T(4,128)}, f32[1,1]{1,0:T(1,128)}) custom-call(f32[8,384]{1,0:T(8,128)S(1)} %chip_forces.1.g_sum, f32[8,128]{1,0:T(8,128)S(1)} %collective-permute-done.15.got_gx, f32[8,128]{1,0:T(8,128)S(1)} %collective-permute-done.16.got_core, bf16[256,384]{1,0:T(8,128)(2,1)S(1)} %get-tuple-element.110.send_t, f32[8,128]{1,0:T(8,128)S(1)} %add.15.rest_0_, ...), custom_call_target="tpu_custom_call" | custom-call | flops 1000000000 | bytes 3000000 | tf_op jit(solution)/shard_map/forces/pallas_call | solution.py:576
  (10 shorter events, 0.0 us)
Async XLA Ops:
  1.4 7.9 %collective-permute-start.1 = (f32[24,128]{1,0:T(8,128)S(1)}, f32[24,128]{1,0:T(8,128)S(1)}, u32[]{:S(2)}, u32[]{:S(2)}) collective-permute-start(f32[24,128]{1,0:T(8,128)S(1)} %pack.1.own), channel_id=1, source_target_pairs={{0,15},{1,2},{2,1},{3,4},{4,3},{5,6},{6,5},{7,8},{8,7},{9,10},{10,... | collective-permute-start | bytes 36872 | tf_op jit(solution)/shard_map/ppermute | solution.py:595
  6.9 2.4 %collective-permute-start = (f32[24,128]{1,0:T(8,128)S(1)}, f32[24,128]{1,0:T(8,128)S(1)}, u32[]{:S(2)}, u32[]{:S(2)}) collective-permute-start(f32[24,128]{1,0:T(8,128)S(1)} %pack.1.own), channel_id=1, source_target_pairs={{0,1},{1,0},{2,3},{3,2},{4,5},{5,4},{6,7},{7,6},{8,9},{9,8},{10,11... | collective-permute-start | bytes 36872 | tf_op jit(solution)/shard_map/ppermute | solution.py:590
  9.4 7.1 %collective-permute-start.4 = (f32[16,128]{1,0:T(8,128)S(1)}, f32[16,128]{1,0:T(8,128)S(1)}, u32[]{:S(2)}, u32[]{:S(2)}) collective-permute-start(f32[16,128]{1,0:T(8,128)S(1)} %get-tuple-element.67), channel_id=1, source_target_pairs={{0,15},{1,2},{2,1},{3,4},{4,3},{5,6},{6,5},{7,8},{8,7},{9,10},{10,... | collective-permute-start | bytes 24584 | tf_op jit(solution)/shard_map/ppermute | solution.py:595
  12.9 3.6 %collective-permute-start.2 = (f32[8,128]{1,0:T(8,128)S(1)}, f32[8,128]{1,0:T(8,128)S(1)}, u32[]{:S(2)}, u32[]{:S(2)}) collective-permute-start(f32[8,128]{1,0:T(8,128)S(1)} %get-tuple-element.65), channel_id=1, source_target_pairs={{0,16},{16,0},{1,17},{17,1},{2,18},{18,2},{3,19},{19,3},{4,20},{20... | collective-permute-start | bytes 12296 | tf_op jit(solution)/shard_map/ppermute | solution.py:600
  14.4 2.1 %collective-permute-start.3 = (f32[8,128]{1,0:T(8,128)S(1)}, f32[8,128]{1,0:T(8,128)S(1)}, u32[]{:S(2)}, u32[]{:S(2)}) collective-permute-start(f32[8,128]{1,0:T(8,128)S(1)} %get-tuple-element.66), channel_id=1, source_target_pairs={{0,1},{1,0},{2,3},{3,2},{4,5},{5,4},{6,7},{7,6},{8,9},{9,8},{10,11... | collective-permute-start | bytes 12296 | tf_op jit(solution)/shard_map/ppermute | solution.py:590
  16.5 5.7 %copy-start = (f32[5]{0:T(128)S(1)}, f32[5]{0:T(128)}, u32[]{:S(2)}) copy-start(f32[5]{0:T(128)} %atom_ref.1) | copy-start | bytes 64
  18.4 6.0 %collective-permute-start.6 = (f32[64,128]{1,0:T(8,128)S(1)}, f32[64,128]{1,0:T(8,128)S(1)}, u32[]{:S(2)}, u32[]{:S(2)}) collective-permute-start(f32[64,128]{1,0:T(8,128)S(1)} %get-tuple-element.78), channel_id=1, source_target_pairs={{0,1},{1,0},{2,3},{3,2},{4,5},{5,4},{6,7},{7,6},{8,9},{9,8},{10,11... | collective-permute-start | bytes 98312 | tf_op jit(solution)/shard_map/ppermute | solution.py:590
  18.5 6.1 %collective-permute-start.7 = (f32[64,128]{1,0:T(8,128)S(1)}, f32[64,128]{1,0:T(8,128)S(1)}, u32[]{:S(2)}, u32[]{:S(2)}) collective-permute-start(f32[64,128]{1,0:T(8,128)S(1)} %get-tuple-element.79), channel_id=1, source_target_pairs={{0,15},{1,2},{2,1},{3,4},{4,3},{5,6},{6,5},{7,8},{8,7},{9,10},{10,... | collective-permute-start | bytes 98312 | tf_op jit(solution)/shard_map/ppermute | solution.py:595
  20.7 4.3 %collective-permute-start.5 = (f32[128,128]{1,0:T(8,128)S(1)}, f32[128,128]{1,0:T(8,128)S(1)}, u32[]{:S(2)}, u32[]{:S(2)}) collective-permute-start(f32[128,128]{1,0:T(8,128)S(1)} %get-tuple-element.77), channel_id=1, source_target_pairs={{0,16},{16,0},{1,17},{17,1},{2,18},{18,2},{3,19},{19,3},{4,20},{20... | collective-permute-start | bytes 196616 | tf_op jit(solution)/shard_map/ppermute | solution.py:600
  26.6 1.6 %collective-permute-start.8 = (f32[8,128]{1,0:T(8,128)S(1)}, f32[8,128]{1,0:T(8,128)S(1)}, u32[]{:S(2)}, u32[]{:S(2)}) collective-permute-start(f32[8,128]{1,0:T(8,128)S(1)} %get-tuple-element.84), channel_id=1, source_target_pairs={{0,1},{1,0},{2,3},{3,2},{4,5},{5,4},{6,7},{7,6},{8,9},{9,8},{10,11... | collective-permute-start | bytes 12296 | tf_op jit(solution)/shard_map/ppermute | solution.py:629
  28.2 4.7 %collective-permute-start.9 = (f32[8,128]{1,0:T(8,128)S(1)}, f32[8,128]{1,0:T(8,128)S(1)}, u32[]{:S(2)}, u32[]{:S(2)}) collective-permute-start(f32[8,128]{1,0:T(8,128)S(1)} %add.12), channel_id=1, source_target_pairs={{0,8},{1,9},{2,10},{3,11},{4,12},{5,13},{6,14},{7,15},{8,0},{9,1},... | collective-permute-start | bytes 12296 | tf_op jit(solution)/shard_map/ppermute | solution.py:629
  29.1 6.1 %collective-permute-start.12 = (f32[64,128]{1,0:T(8,128)S(1)}, f32[64,128]{1,0:T(8,128)S(1)}, u32[]{:S(2)}, u32[]{:S(2)}) collective-permute-start(f32[64,128]{1,0:T(8,128)S(1)} %get-tuple-element.105), channel_id=1, source_target_pairs={{0,1},{1,0},{2,3},{3,2},{4,5},{5,4},{6,7},{7,6},{8,9},{9,8},{10,11... | collective-permute-start | bytes 98312 | tf_op jit(solution)/shard_map/ppermute | solution.py:590
  29.6 6.0 %collective-permute-start.13 = (f32[64,128]{1,0:T(8,128)S(1)}, f32[64,128]{1,0:T(8,128)S(1)}, u32[]{:S(2)}, u32[]{:S(2)}) collective-permute-start(f32[64,128]{1,0:T(8,128)S(1)} %get-tuple-element.106), channel_id=1, source_target_pairs={{0,15},{1,2},{2,1},{3,4},{4,3},{5,6},{6,5},{7,8},{8,7},{9,10},{10,... | collective-permute-start | bytes 98312 | tf_op jit(solution)/shard_map/ppermute | solution.py:595
  31.4 4.3 %collective-permute-start.11 = (f32[128,128]{1,0:T(8,128)S(1)}, f32[128,128]{1,0:T(8,128)S(1)}, u32[]{:S(2)}, u32[]{:S(2)}) collective-permute-start(f32[128,128]{1,0:T(8,128)S(1)} %get-tuple-element.104), channel_id=1, source_target_pairs={{0,16},{16,0},{1,17},{17,1},{2,18},{18,2},{3,19},{19,3},{4,20},{20... | collective-permute-start | bytes 196616 | tf_op jit(solution)/shard_map/ppermute | solution.py:600
  32.9 3.8 %collective-permute-start.10 = (f32[8,128]{1,0:T(8,128)S(1)}, f32[8,128]{1,0:T(8,128)S(1)}, u32[]{:S(2)}, u32[]{:S(2)}) collective-permute-start(f32[8,128]{1,0:T(8,128)S(1)} %add.13), channel_id=1, source_target_pairs={{0,2},{1,3},{2,0},{3,1},{4,6},{5,7},{6,4},{7,5},{8,10},{9,11},{10,... | collective-permute-start | bytes 12296 | tf_op jit(solution)/shard_map/ppermute | solution.py:629
  36.7 3.7 %collective-permute-start.17 = (f32[8,128]{1,0:T(8,128)S(1)}, f32[8,128]{1,0:T(8,128)S(1)}, u32[]{:S(2)}, u32[]{:S(2)}) collective-permute-start(f32[8,128]{1,0:T(8,128)S(1)} %add.14), channel_id=1, source_target_pairs={{0,4},{1,5},{2,6},{3,7},{4,0},{5,1},{6,2},{7,3},{8,12},{9,13},{10,... | collective-permute-start | bytes 12296 | tf_op jit(solution)/shard_map/ppermute | solution.py:629
  37.4 5.7 %collective-permute-start.14 = (f32[8,128]{1,0:T(8,128)S(1)}, f32[8,128]{1,0:T(8,128)S(1)}, u32[]{:S(2)}, u32[]{:S(2)}) collective-permute-start(f32[8,128]{1,0:T(8,128)S(1)} %get-tuple-element.116), channel_id=1, source_target_pairs={{0,15},{1,2},{2,1},{3,4},{4,3},{5,6},{6,5},{7,8},{8,7},{9,10},{10,... | collective-permute-start | bytes 12296 | tf_op jit(solution)/shard_map/ppermute | solution.py:595
  39.1 4.2 %collective-permute-start.15 = (f32[8,128]{1,0:T(8,128)S(1)}, f32[8,128]{1,0:T(8,128)S(1)}, u32[]{:S(2)}, u32[]{:S(2)}) collective-permute-start(f32[8,128]{1,0:T(8,128)S(1)} %get-tuple-element.117), channel_id=1, source_target_pairs={{0,16},{16,0},{1,17},{17,1},{2,18},{18,2},{3,19},{19,3},{4,20},{20... | collective-permute-start | bytes 12296 | tf_op jit(solution)/shard_map/ppermute | solution.py:600
  40.1 3.2 %collective-permute-start.16 = (f32[8,128]{1,0:T(8,128)S(1)}, f32[8,128]{1,0:T(8,128)S(1)}, u32[]{:S(2)}, u32[]{:S(2)}) collective-permute-start(f32[8,128]{1,0:T(8,128)S(1)} %get-tuple-element.118), channel_id=1, source_target_pairs={{0,1},{1,0},{2,3},{3,2},{4,5},{5,4},{6,7},{7,6},{8,9},{9,8},{10,11... | collective-permute-start | bytes 12296 | tf_op jit(solution)/shard_map/ppermute | solution.py:590
  40.5 3.7 %collective-permute-start.18 = (f32[8,128]{1,0:T(8,128)S(1)}, f32[8,128]{1,0:T(8,128)S(1)}, u32[]{:S(2)}, u32[]{:S(2)}) collective-permute-start(f32[8,128]{1,0:T(8,128)S(1)} %add.15.rest_0_), channel_id=1, source_target_pairs={{0,16},{1,17},{2,18},{3,19},{4,20},{5,21},{6,22},{7,23},{8,24},{9,... | collective-permute-start | bytes 12296 | tf_op jit(solution)/shard_map/ppermute | solution.py:629

commit v7 on v6

--- a/solution.py
+++ b/solution.py
@@ -20,6 +20,7 @@
 SUMS_UNROLL = 16
 EDGE_UNROLL = 16
 FORCE_UNROLL = 16
+FACTOR_UNROLL = 16
 VMEM_BYTES = 16 * 1024 * 1024
 
 
@@ -52,10 +53,8 @@
 
 
 def pieces(table):
-    high = table.astype(bf16).astype(f32)
-    rest = table - high
-    mid = rest.astype(bf16).astype(f32)
-    return jnp.concatenate([high, mid, rest - mid], axis=0).astype(bf16)
+    parts = pieces_f32(table)
+    return jnp.concatenate([parts, jnp.zeros(table.shape, f32)], axis=0).astype(bf16)
 
 
 def pieces_f32(table):
@@ -403,7 +402,7 @@
     entries = feat_ref.shape[1] // slots
     scattered = matmul(left[...], onehot_t[:, 0:slots])
     g_proj = scattered[0:channels] + scattered[channels : 2 * channels]
-    g_pos[...] = whole(scattered[2 * channels : 2 * channels + 3 * ROWS])
+    g_pos[...] = whole(scattered[2 * channels : 2 * channels + 4 * ROWS])
     g_h[...] = matmul(weights[4], stacked_right(g_proj)) + g_own[...]
     for lanes, edges in lane_parts(slots, entries):
         units = [[geo[U + d, :, edges[k]] for d in range(3)] for k in range(entries)]
@@ -423,7 +422,7 @@
                 factors[3, rows, edges[k]] = r1 * fields[2] + r2 * h_z
             return carry
 
-        lax.fori_loop(0, channels // ROWS, body, 0, unroll=2)
+        lax.fori_loop(0, channels // ROWS, body, 0, unroll=FACTOR_UNROLL)
 
 
 def second_layer_kernel(
@@ -497,7 +496,7 @@
     left[...] = stacked
     scattered = matmul(stacked, onehot_t[:, slots:wide])
     g_proj = scattered[0:channels] + scattered[channels : 2 * channels]
-    g_ghost[...] = whole(scattered[2 * channels : 2 * channels + 3 * ROWS])
+    g_ghost[...] = whole(scattered[2 * channels : 2 * channels + 4 * ROWS])
     g_all = matmul(weights[4], stacked_right(g_proj))
     send_gx[...] = g_all[:, 0:LANES]
     to_previous, to_next = pack_halves(g_all[:, LANES : 2 * LANES])
@@ -774,7 +773,7 @@
     got_sums = partners(tally, [bits - 1] if bits > 1 else [])
     left, send_gx, send_core, send_chip, g_ghost, g_target_two = call(
         ghost_gradient_kernel,
-        [((2 * channels + 3 * ROWS, edges), bf16), square, half, half, (ROWS, ghosts), (ROWS, slots)],
+        [((2 * channels + 4 * ROWS, edges), bf16), square, half, half, (ROWS, ghosts), (ROWS, slots)],
         [],
         [g_feat, g_off, onehot_t, weights],
         name="ghost_gradient",
@@ -797,7 +796,7 @@
     )
     left, g_target_one, send_gx, send_core, send_chip = call(
         first_gradient_kernel,
-        [((3 * ROWS, edges), bf16), (ROWS, slots), (8, LANES), (8, LANES), (8, LANES)],
+        [((4 * ROWS, edges), bf16), (ROWS, slots), (8, LANES), (8, LANES), (8, LANES)],
         [],
         [g_h, got_gx, got_core, got_chip, slope, factors, geo, g_ghost, onehot_t, send_t, weights],
         [flat, (ROWS, edges)],

time: 45.1 us -> 45.1 us (level)
  transfers between devices with their start and end apart: 19 -> 19, of which waited for: 6 -> 6; matrix products, arithmetic and copies ran while one was open for 0% -> 0% of each run, Pallas kernels for 24% -> 23%
where the time goes in v7:
time: 45.1 us; the launch traced here: 44.9 us
  starting transfers between devices  23.2 us (51%)
  Pallas kernels  15.6 us (35%)
  waiting for transfers between devices  5.33 us (12%)
  between operations  0.84 us (2%)
    pallas_call x14, Pallas kernels, call(): pl.pallas_call(kernel, out_shape=shapes, in_specs=[in_smem] * len(scalars...  15.6 us
    ppermute x5, starting transfers between devices, swap_chip(): lax.ppermute(value, 'yz', [(i, (i + 1 if i % 2 else i - 1) % size) for i...  14.6 us
    ppermute x4, starting transfers between devices, shift(): lax.ppermute(value, axis, [(i, (i + by) % size) for i in range(size)])  5.93 us
    ppermute x4, waiting for transfers between devices, shift(): lax.ppermute(value, axis, [(i, (i + by) % size) for i in range(size)])  2.2 us
    ppermute x5, starting transfers between devices, partners(): lax.ppermute(value, axes, [(i, i ^ step) for i in range(size)])  1.95 us
    ppermute x5, waiting for transfers between devices, swap_chip(): lax.ppermute(value, 'yz', [(i, (i + 1 if i % 2 else i - 1) % size) for i...  1.93 us
    ppermute x5, waiting for transfers between devices, partners(): lax.ppermute(value, axes, [(i, i ^ step) for i in range(size)])  1.19 us
  transfers between devices with their start and end apart: 19, of which 6 were waited for; matrix products, arithmetic and copies ran while one was open for 0% of the time, Pallas kernels for 23%

profile of v7, /device:TPU:0, one launch (start us, length us, event | category | flops | bytes accessed | tf_op | source)
XLA Modules:
  0.0 44.9 jit_solution(1115479449193306169)
XLA Ops:
  0.6 0.7 %pack.1.own = f32[24,128]{1,0:T(8,128)S(1)} custom-call(s32[1,2]{1,0:T(1,128)} %bitcast.4, s32[2]{0:T(128)} %count_hbm.1, f32[3,256]{1,0:T(4,128)} %pos_hbm.1, s32[2,128]{1,0:T(2,128)} %bitcast.3), custom_call_target="tpu_custom_call" | custom-call | flops 1000000000 | bytes 3000000 | tf_op jit(solution)/shard_map/pack/pallas_call | solution.py:575
  1.4 5.5 %collective-permute-start.1 = (f32[24,128]{1,0:T(8,128)S(1)}, f32[24,128]{1,0:T(8,128)S(1)}, u32[]{:S(2)}, u32[]{:S(2)}) collective-permute-start(f32[24,128]{1,0:T(8,128)S(1)} %pack.1.own), channel_id=1, source_target_pairs={{0,15},{1,2},{2,1},{3,4},{4,3},{5,6},{6,5},{7,8},{8,7},{9,10},{10,... | collective-permute-start | bytes 36872 | tf_op jit(solution)/shard_map/ppermute | solution.py:594
  6.9 0.0 collective-permute-start
  6.9 2.4 %prepare.1 = (bf16[640,1536]{1,0:T(8,128)(2,1)S(1)}, bf16[384,256]{1,0:T(8,128)(2,1)S(1)}, f32[2,8,1536]{2,1,0:T(8,128)S(1)}, bf16[2,384,24]{2,1,0:T(8,128)(2,1)...) custom-call(f32[2,8]{1,0:T(2,128)} %gammas_hbm.1, ...), custom_call_target="tpu_custom_call" | custom-call | flops 3000000000 | bytes 9000000 | tf_op jit(solution)/shard_map/prepare/pallas_call | solution.py:575
  9.3 0.0 collective-permute-done.1.chip
  9.3 0.0 collective-permute-done.core
  9.3 0.1 assemble.1
  9.4 3.5 %collective-permute-start.4 = (f32[16,128]{1,0:T(8,128)S(1)}, f32[16,128]{1,0:T(8,128)S(1)}, u32[]{:S(2)}, u32[]{:S(2)}) collective-permute-start(f32[16,128]{1,0:T(8,128)S(1)} %get-tuple-element.67), channel_id=1, source_target_pairs={{0,15},{1,2},{2,1},{3,4},{4,3},{5,6},{6,5},{7,8},{8,7},{9,10},{10,... | collective-permute-start | bytes 24584 | tf_op jit(solution)/shard_map/ppermute | solution.py:594
  12.9 1.5 %collective-permute-start.2 = (f32[8,128]{1,0:T(8,128)S(1)}, f32[8,128]{1,0:T(8,128)S(1)}, u32[]{:S(2)}, u32[]{:S(2)}) collective-permute-start(f32[8,128]{1,0:T(8,128)S(1)} %get-tuple-element.65), channel_id=1, source_target_pairs={{0,16},{16,0},{1,17},{17,1},{2,18},{18,2},{3,19},{19,3},{4,20},{20... | collective-permute-start | bytes 12296 | tf_op jit(solution)/shard_map/ppermute | solution.py:599
  14.4 0.0 collective-permute-start.3
  14.4 0.3 own_positions.1.found_own
  14.7 1.8 %collective-permute-done.2.got_gx = f32[8,128]{1,0:T(8,128)S(1)} collective-permute-done((f32[8,128]{1,0:T(8,128)S(1)}, f32[8,128]{1,0:T(8,128)S(1)}, u32[]{:S(2)}, u32[]{:S(2)}) %collective-permute-start.2) | collective-permute-done | bytes 4128 | tf_op jit(solution)/shard_map/ppermute | solution.py:599
  16.5 0.0 collective-permute-done.3.got_core
  16.5 1.9 %first_layer.1 = (f32[128,384]{1,0:T(8,128)S(1)}, f32[128,384]{1,0:T(8,128)S(1)}, f32[128,128]{1,0:T(8,128)S(1)}, f32[64,128]{1,0:T(8,128)S(1)}, f32[64,128]{1,0...) custom-call(f32[8,1536]{1,0:T(8,128)S(1)} %own_positions.1.found_own, ...), custom_call_target="tpu_custom_call" | custom-call | flops 2500000000 | bytes 7500000 | tf_op jit(solution)/shard_map/first_layer/pallas_call | solution.py:575
  18.4 0.1 collective-permute-start.6
  18.5 2.2 %collective-permute-start.7 = (f32[64,128]{1,0:T(8,128)S(1)}, f32[64,128]{1,0:T(8,128)S(1)}, u32[]{:S(2)}, u32[]{:S(2)}) collective-permute-start(f32[64,128]{1,0:T(8,128)S(1)} %get-tuple-element.79), channel_id=1, source_target_pairs={{0,15},{1,2},{2,1},{3,4},{4,3},{5,6},{6,5},{7,8},{8,7},{9,10},{10,... | collective-permute-start | bytes 98312 | tf_op jit(solution)/shard_map/ppermute | solution.py:594
  20.7 1.5 %collective-permute-start.5 = (f32[128,128]{1,0:T(8,128)S(1)}, f32[128,128]{1,0:T(8,128)S(1)}, u32[]{:S(2)}, u32[]{:S(2)}) collective-permute-start(f32[128,128]{1,0:T(8,128)S(1)} %get-tuple-element.77), channel_id=1, source_target_pairs={{0,16},{16,0},{1,17},{17,1},{2,18},{18,2},{3,19},{19,3},{4,20},{20... | collective-permute-start | bytes 196616 | tf_op jit(solution)/shard_map/ppermute | solution.py:599
  22.2 2.2 %radials.1 = (f32[384,1536]{1,0:T(8,128)S(1)}, f32[384,1536]{1,0:T(8,128)S(1)}, f32[384,1536]{1,0:T(8,128)S(1)}, f32[8,128]{1,0:T(8,128)S(1)}, f32[128,1536]{1,0:T(8,128)S(1)}) custom-call(f32[5]{0:T(128)S(1)} %copy-done, f32[8,8,1536]{2,1,0:T(8,128)S(1)} %get-tuple-element.73.geo, f32[2,8,1536]{2,1,0:T(8,128)S(1)} %get-tuple-element.68.gamma, ...), custom_call_target="tpu_custom_call" | custom-call | flops 2000000000 | bytes 6000000 | tf_op jit(solution)/shard_map/radials/pallas_call | solution.py:575
  24.4 0.0 collective-permute-done.6.got_core
  24.4 0.2 collective-permute-done.7.got_chip
  24.6 0.4 collective-permute-done.5.got_gx
  25.0 1.7 %second_layer.1 = (f32[128,1536]{1,0:T(8,128)S(1)}, f32[9,128,384]{2,1,0:T(8,128)S(1)}, f32[128,384]{1,0:T(8,128)S(1)}, f32[128,384]{1,0:T(8,128)S(1)}, f32[8,128]{1,0:T(8,128)S(1)}) custom-call(f32[8,128]{1,0:T(8,128)S(1)} %get-tuple-element.76.base, f32[8,384]{1,0:T(8,128)S(1)} %get-tuple-element.63.table, f32[128,384]{1,0:T(8,128)S(1)} %get-tuple-element.74.h_one, ...), custom_call_target="tpu_custom_call" | custom-call | flops 2500000000 | bytes 7500000 | tf_op jit(solution)/shard_map/second_layer/pallas_call | solution.py:575
  26.7 0.1 collective-permute-start.8
  26.8 1.5 %second_gradient.1 = (f32[128,1536]{1,0:T(8,128)S(1)}, f32[8,1536]{1,0:T(8,128)S(1)}) custom-call(f32[8,8,1536]{2,1,0:T(8,128)S(1)} %get-tuple-element.73.geo, f32[384,1536]{1,0:T(8,128)S(1)} %get-tuple-element.81.rad_ref, f32[384,1536]{1,0:T(8,128)S(1)} %get-tuple-element.85.slope_ref, f32[128,1536]{1,0:T(8,128)S(1)} %get-tuple-element.86.feat_ref, ...), custom_call_target="tpu_custom_call" | custom-call | flops 2500000000 | bytes 7500000 | tf_op jit(solution)/shard_map/second_gradient/pallas_call | solution.py:575
  28.3 0.0 collective-permute-done.8
  28.3 0.1 collective-permute-start.9
  28.4 0.7 %ghost_gradient.1 = (bf16[288,1536]{1,0:T(8,128)(2,1)S(1)}, f32[128,128]{1,0:T(8,128)S(1)}, f32[64,128]{1,0:T(8,128)S(1)}, f32[64,128]{1,0:T(8,128)S(1)}, f32[8,256]{1,0:T(8,128)S(1)}, /*index=5*/f32[8,384]{1,0:T(8,128)S(1)}) custom-call(f32[128,1536]{1,0:T(8,128)S(1)} %get-tuple-element.91.g_feat, f32[8,1536]{1,0:T(8,128)S(1)} %get-tuple-element.92.g_off, ...), custom_call_target="tpu_custom_call" | custom-call | flops 1500000000 | bytes 4500000 | tf_op jit(solution)/shard_map/ghost_gradient/pallas_call | solution.py:575
  29.1 0.6 %collective-permute-start.12 = (f32[64,128]{1,0:T(8,128)S(1)}, f32[64,128]{1,0:T(8,128)S(1)}, u32[]{:S(2)}, u32[]{:S(2)}) collective-permute-start(f32[64,128]{1,0:T(8,128)S(1)} %get-tuple-element.105), channel_id=1, source_target_pairs={{0,1},{1,0},{2,3},{3,2},{4,5},{5,4},{6,7},{7,6},{8,9},{9,8},{10,11... | collective-permute-start | bytes 98312 | tf_op jit(solution)/shard_map/ppermute | solution.py:589
  29.7 1.8 %collective-permute-start.13 = (f32[64,128]{1,0:T(8,128)S(1)}, f32[64,128]{1,0:T(8,128)S(1)}, u32[]{:S(2)}, u32[]{:S(2)}) collective-permute-start(f32[64,128]{1,0:T(8,128)S(1)} %get-tuple-element.106), channel_id=1, source_target_pairs={{0,15},{1,2},{2,1},{3,4},{4,3},{5,6},{6,5},{7,8},{8,7},{9,10},{10,... | collective-permute-start | bytes 98312 | tf_op jit(solution)/shard_map/ppermute | solution.py:594
  31.4 1.5 %collective-permute-start.11 = (f32[128,128]{1,0:T(8,128)S(1)}, f32[128,128]{1,0:T(8,128)S(1)}, u32[]{:S(2)}, u32[]{:S(2)}) collective-permute-start(f32[128,128]{1,0:T(8,128)S(1)} %get-tuple-element.104), channel_id=1, source_target_pairs={{0,16},{16,0},{1,17},{17,1},{2,18},{18,2},{3,19},{19,3},{4,20},{20... | collective-permute-start | bytes 196616 | tf_op jit(solution)/shard_map/ppermute | solution.py:599
  33.0 0.0 collective-permute-start.10
  33.0 1.9 %factors.1 = (f32[4,128,1536]{2,1,0:T(8,128)S(1)}, f32[128,384]{1,0:T(8,128)S(1)}, f32[8,384]{1,0:T(8,128)S(1)}) custom-call(f32[8,8,1536]{2,1,0:T(8,128)S(1)} %get-tuple-element.73.geo, f32[384,1536]{1,0:T(8,128)S(1)} %get-tuple-element.97.rad_ref, f32[384,1536]{1,0:T(8,128)S(1)} %get-tuple-element.98.slope_ref, ...), custom_call_target="tpu_custom_call" | custom-call | flops 3000000000 | bytes 9000000 | tf_op jit(solution)/shard_map/factors/pallas_call | solution.py:575
  34.9 0.8 %collective-permute-done.13.got_chip = f32[64,128]{1,0:T(8,128)S(1)} collective-permute-done((f32[64,128]{1,0:T(8,128)S(1)}, f32[64,128]{1,0:T(8,128)S(1)}, u32[]{:S(2)}, u32[]{:S(2)}) %collective-permute-start.13) | collective-permute-done | bytes 32800 | tf_op jit(solution)/shard_map/ppermute | solution.py:594
  35.7 0.0 collective-permute-done.11.got_gx
  35.7 1.0 %first_gradient.1 = (bf16[32,1536]{1,0:T(8,128)(2,1)S(1)}, f32[8,384]{1,0:T(8,128)S(1)}, f32[8,128]{1,0:T(8,128)S(1)}, f32[8,128]{1,0:T(8,128)S(1)}, f32[8,128]{1,0:T(8,128)S(1)}) custom-call(f32[128,384]{1,0:T(8,128)S(1)} %get-tuple-element.103.g_h, f32[128,128]{1,0:T(8,128)S(1)} %collective-permute-done.11.got_gx, ...), custom_call_target="tpu_custom_call" | custom-call | flops 1200000000 | bytes 3600000 | tf_op jit(solution)/shard_map/first_gradient/pallas_call | solution.py:575
  36.7 0.0 collective-permute-done.10
  36.7 0.4 collective-permute-start.17
  37.1 1.7 %collective-permute-start.14 = (f32[8,128]{1,0:T(8,128)S(1)}, f32[8,128]{1,0:T(8,128)S(1)}, u32[]{:S(2)}, u32[]{:S(2)}) collective-permute-start(f32[8,128]{1,0:T(8,128)S(1)} %get-tuple-element.116), channel_id=1, source_target_pairs={{0,15},{1,2},{2,1},{3,4},{4,3},{5,6},{6,5},{7,8},{8,7},{9,10},{10,... | collective-permute-start | bytes 12296 | tf_op jit(solution)/shard_map/ppermute | solution.py:594
  38.8 1.4 %collective-permute-start.15 = (f32[8,128]{1,0:T(8,128)S(1)}, f32[8,128]{1,0:T(8,128)S(1)}, u32[]{:S(2)}, u32[]{:S(2)}) collective-permute-start(f32[8,128]{1,0:T(8,128)S(1)} %get-tuple-element.117), channel_id=1, source_target_pairs={{0,16},{16,0},{1,17},{17,1},{2,18},{18,2},{3,19},{19,3},{4,20},{20... | collective-permute-start | bytes 12296 | tf_op jit(solution)/shard_map/ppermute | solution.py:599
  40.2 0.0 collective-permute-start.16
  40.2 0.3 local.1.g_pos
  40.5 1.4 %collective-permute-start.18 = (f32[8,128]{1,0:T(8,128)S(1)}, f32[8,128]{1,0:T(8,128)S(1)}, u32[]{:S(2)}, u32[]{:S(2)}) collective-permute-start(f32[8,128]{1,0:T(8,128)S(1)} %add.15.rest_0_), channel_id=1, source_target_pairs={{0,16},{1,17},{2,18},{3,19},{4,20},{5,21},{6,22},{7,23},{8,24},{9,... | collective-permute-start | bytes 12296 | tf_op jit(solution)/shard_map/ppermute | solution.py:628
  41.9 0.9 %collective-permute-done.14.got_chip = f32[8,128]{1,0:T(8,128)S(1)} collective-permute-done((f32[8,128]{1,0:T(8,128)S(1)}, f32[8,128]{1,0:T(8,128)S(1)}, u32[]{:S(2)}, u32[]{:S(2)}) %collective-permute-start.14) | collective-permute-done | bytes 4128 | tf_op jit(solution)/shard_map/ppermute | solution.py:594
  42.8 0.1 chip_forces.1.g_sum
  43.0 0.0 collective-permute-done.15.got_gx
  43.0 0.0 collective-permute-done.16.got_core
  43.0 1.2 %collective-permute-done.18.rest_1_ = f32[8,128]{1,0:T(8,128)S(1)} collective-permute-done((f32[8,128]{1,0:T(8,128)S(1)}, f32[8,128]{1,0:T(8,128)S(1)}, u32[]{:S(2)}, u32[]{:S(2)}) %collective-permute-start.18) | collective-permute-done | bytes 4128 | tf_op jit(solution)/shard_map/ppermute | solution.py:628
  44.2 0.8 %forces.1 = (f32[3,384]{1,0:T(4,128)}, f32[1,1]{1,0:T(1,128)}) custom-call(f32[8,384]{1,0:T(8,128)S(1)} %chip_forces.1.g_sum, f32[8,128]{1,0:T(8,128)S(1)} %collective-permute-done.15.got_gx, f32[8,128]{1,0:T(8,128)S(1)} %collective-permute-done.16.got_core, bf16[256,384]{1,0:T(8,128)(2,1)S(1)} %get-tuple-element.110.send_t, f32[8,128]{1,0:T(8,128)S(1)} %add.15.rest_0_, ...), custom_call_target="tpu_custom_call" | custom-call | flops 1000000000 | bytes 3000000 | tf_op jit(solution)/shard_map/forces/pallas_call | solution.py:575
  (10 shorter events, 0.0 us)
Async XLA Ops:
  1.4 7.9 %collective-permute-start.1 = (f32[24,128]{1,0:T(8,128)S(1)}, f32[24,128]{1,0:T(8,128)S(1)}, u32[]{:S(2)}, u32[]{:S(2)}) collective-permute-start(f32[24,128]{1,0:T(8,128)S(1)} %pack.1.own), channel_id=1, source_target_pairs={{0,15},{1,2},{2,1},{3,4},{4,3},{5,6},{6,5},{7,8},{8,7},{9,10},{10,... | collective-permute-start | bytes 36872 | tf_op jit(solution)/shard_map/ppermute | solution.py:594
  6.9 2.4 %collective-permute-start = (f32[24,128]{1,0:T(8,128)S(1)}, f32[24,128]{1,0:T(8,128)S(1)}, u32[]{:S(2)}, u32[]{:S(2)}) collective-permute-start(f32[24,128]{1,0:T(8,128)S(1)} %pack.1.own), channel_id=1, source_target_pairs={{0,1},{1,0},{2,3},{3,2},{4,5},{5,4},{6,7},{7,6},{8,9},{9,8},{10,11... | collective-permute-start | bytes 36872 | tf_op jit(solution)/shard_map/ppermute | solution.py:589
  9.4 7.1 %collective-permute-start.4 = (f32[16,128]{1,0:T(8,128)S(1)}, f32[16,128]{1,0:T(8,128)S(1)}, u32[]{:S(2)}, u32[]{:S(2)}) collective-permute-start(f32[16,128]{1,0:T(8,128)S(1)} %get-tuple-element.67), channel_id=1, source_target_pairs={{0,15},{1,2},{2,1},{3,4},{4,3},{5,6},{6,5},{7,8},{8,7},{9,10},{10,... | collective-permute-start | bytes 24584 | tf_op jit(solution)/shard_map/ppermute | solution.py:594
  12.9 3.6 %collective-permute-start.2 = (f32[8,128]{1,0:T(8,128)S(1)}, f32[8,128]{1,0:T(8,128)S(1)}, u32[]{:S(2)}, u32[]{:S(2)}) collective-permute-start(f32[8,128]{1,0:T(8,128)S(1)} %get-tuple-element.65), channel_id=1, source_target_pairs={{0,16},{16,0},{1,17},{17,1},{2,18},{18,2},{3,19},{19,3},{4,20},{20... | collective-permute-start | bytes 12296 | tf_op jit(solution)/shard_map/ppermute | solution.py:599
  14.4 2.1 %collective-permute-start.3 = (f32[8,128]{1,0:T(8,128)S(1)}, f32[8,128]{1,0:T(8,128)S(1)}, u32[]{:S(2)}, u32[]{:S(2)}) collective-permute-start(f32[8,128]{1,0:T(8,128)S(1)} %get-tuple-element.66), channel_id=1, source_target_pairs={{0,1},{1,0},{2,3},{3,2},{4,5},{5,4},{6,7},{7,6},{8,9},{9,8},{10,11... | collective-permute-start | bytes 12296 | tf_op jit(solution)/shard_map/ppermute | solution.py:589
  16.5 5.7 %copy-start = (f32[5]{0:T(128)S(1)}, f32[5]{0:T(128)}, u32[]{:S(2)}) copy-start(f32[5]{0:T(128)} %atom_ref.1) | copy-start | bytes 64
  18.4 6.0 %collective-permute-start.6 = (f32[64,128]{1,0:T(8,128)S(1)}, f32[64,128]{1,0:T(8,128)S(1)}, u32[]{:S(2)}, u32[]{:S(2)}) collective-permute-start(f32[64,128]{1,0:T(8,128)S(1)} %get-tuple-element.78), channel_id=1, source_target_pairs={{0,1},{1,0},{2,3},{3,2},{4,5},{5,4},{6,7},{7,6},{8,9},{9,8},{10,11... | collective-permute-start | bytes 98312 | tf_op jit(solution)/shard_map/ppermute | solution.py:589
  18.5 6.1 %collective-permute-start.7 = (f32[64,128]{1,0:T(8,128)S(1)}, f32[64,128]{1,0:T(8,128)S(1)}, u32[]{:S(2)}, u32[]{:S(2)}) collective-permute-start(f32[64,128]{1,0:T(8,128)S(1)} %get-tuple-element.79), channel_id=1, source_target_pairs={{0,15},{1,2},{2,1},{3,4},{4,3},{5,6},{6,5},{7,8},{8,7},{9,10},{10,... | collective-permute-start | bytes 98312 | tf_op jit(solution)/shard_map/ppermute | solution.py:594
  20.7 4.3 %collective-permute-start.5 = (f32[128,128]{1,0:T(8,128)S(1)}, f32[128,128]{1,0:T(8,128)S(1)}, u32[]{:S(2)}, u32[]{:S(2)}) collective-permute-start(f32[128,128]{1,0:T(8,128)S(1)} %get-tuple-element.77), channel_id=1, source_target_pairs={{0,16},{16,0},{1,17},{17,1},{2,18},{18,2},{3,19},{19,3},{4,20},{20... | collective-permute-start | bytes 196616 | tf_op jit(solution)/shard_map/ppermute | solution.py:599
  26.7 1.6 %collective-permute-start.8 = (f32[8,128]{1,0:T(8,128)S(1)}, f32[8,128]{1,0:T(8,128)S(1)}, u32[]{:S(2)}, u32[]{:S(2)}) collective-permute-start(f32[8,128]{1,0:T(8,128)S(1)} %get-tuple-element.84), channel_id=1, source_target_pairs={{0,1},{1,0},{2,3},{3,2},{4,5},{5,4},{6,7},{7,6},{8,9},{9,8},{10,11... | collective-permute-start | bytes 12296 | tf_op jit(solution)/shard_map/ppermute | solution.py:628
  28.3 4.7 %collective-permute-start.9 = (f32[8,128]{1,0:T(8,128)S(1)}, f32[8,128]{1,0:T(8,128)S(1)}, u32[]{:S(2)}, u32[]{:S(2)}) collective-permute-start(f32[8,128]{1,0:T(8,128)S(1)} %add.12), channel_id=1, source_target_pairs={{0,8},{1,9},{2,10},{3,11},{4,12},{5,13},{6,14},{7,15},{8,0},{9,1},... | collective-permute-start | bytes 12296 | tf_op jit(solution)/shard_map/ppermute | solution.py:628
  29.1 5.7 %collective-permute-start.12 = (f32[64,128]{1,0:T(8,128)S(1)}, f32[64,128]{1,0:T(8,128)S(1)}, u32[]{:S(2)}, u32[]{:S(2)}) collective-permute-start(f32[64,128]{1,0:T(8,128)S(1)} %get-tuple-element.105), channel_id=1, source_target_pairs={{0,1},{1,0},{2,3},{3,2},{4,5},{5,4},{6,7},{7,6},{8,9},{9,8},{10,11... | collective-permute-start | bytes 98312 | tf_op jit(solution)/shard_map/ppermute | solution.py:589
  29.7 6.0 %collective-permute-start.13 = (f32[64,128]{1,0:T(8,128)S(1)}, f32[64,128]{1,0:T(8,128)S(1)}, u32[]{:S(2)}, u32[]{:S(2)}) collective-permute-start(f32[64,128]{1,0:T(8,128)S(1)} %get-tuple-element.106), channel_id=1, source_target_pairs={{0,15},{1,2},{2,1},{3,4},{4,3},{5,6},{6,5},{7,8},{8,7},{9,10},{10,... | collective-permute-start | bytes 98312 | tf_op jit(solution)/shard_map/ppermute | solution.py:594
  31.4 4.3 %collective-permute-start.11 = (f32[128,128]{1,0:T(8,128)S(1)}, f32[128,128]{1,0:T(8,128)S(1)}, u32[]{:S(2)}, u32[]{:S(2)}) collective-permute-start(f32[128,128]{1,0:T(8,128)S(1)} %get-tuple-element.104), channel_id=1, source_target_pairs={{0,16},{16,0},{1,17},{17,1},{2,18},{18,2},{3,19},{19,3},{4,20},{20... | collective-permute-start | bytes 196616 | tf_op jit(solution)/shard_map/ppermute | solution.py:599
  33.0 3.7 %collective-permute-start.10 = (f32[8,128]{1,0:T(8,128)S(1)}, f32[8,128]{1,0:T(8,128)S(1)}, u32[]{:S(2)}, u32[]{:S(2)}) collective-permute-start(f32[8,128]{1,0:T(8,128)S(1)} %add.13), channel_id=1, source_target_pairs={{0,2},{1,3},{2,0},{3,1},{4,6},{5,7},{6,4},{7,5},{8,10},{9,11},{10,... | collective-permute-start | bytes 12296 | tf_op jit(solution)/shard_map/ppermute | solution.py:628
  36.7 3.8 %collective-permute-start.17 = (f32[8,128]{1,0:T(8,128)S(1)}, f32[8,128]{1,0:T(8,128)S(1)}, u32[]{:S(2)}, u32[]{:S(2)}) collective-permute-start(f32[8,128]{1,0:T(8,128)S(1)} %add.14), channel_id=1, source_target_pairs={{0,4},{1,5},{2,6},{3,7},{4,0},{5,1},{6,2},{7,3},{8,12},{9,13},{10,... | collective-permute-start | bytes 12296 | tf_op jit(solution)/shard_map/ppermute | solution.py:628
  37.1 5.7 %collective-permute-start.14 = (f32[8,128]{1,0:T(8,128)S(1)}, f32[8,128]{1,0:T(8,128)S(1)}, u32[]{:S(2)}, u32[]{:S(2)}) collective-permute-start(f32[8,128]{1,0:T(8,128)S(1)} %get-tuple-element.116), channel_id=1, source_target_pairs={{0,15},{1,2},{2,1},{3,4},{4,3},{5,6},{6,5},{7,8},{8,7},{9,10},{10,... | collective-permute-start | bytes 12296 | tf_op jit(solution)/shard_map/ppermute | solution.py:594
  38.8 4.2 %collective-permute-start.15 = (f32[8,128]{1,0:T(8,128)S(1)}, f32[8,128]{1,0:T(8,128)S(1)}, u32[]{:S(2)}, u32[]{:S(2)}) collective-permute-start(f32[8,128]{1,0:T(8,128)S(1)} %get-tuple-element.117), channel_id=1, source_target_pairs={{0,16},{16,0},{1,17},{17,1},{2,18},{18,2},{3,19},{19,3},{4,20},{20... | collective-permute-start | bytes 12296 | tf_op jit(solution)/shard_map/ppermute | solution.py:599
  40.2 2.8 %collective-permute-start.16 = (f32[8,128]{1,0:T(8,128)S(1)}, f32[8,128]{1,0:T(8,128)S(1)}, u32[]{:S(2)}, u32[]{:S(2)}) collective-permute-start(f32[8,128]{1,0:T(8,128)S(1)} %get-tuple-element.118), channel_id=1, source_target_pairs={{0,1},{1,0},{2,3},{3,2},{4,5},{5,4},{6,7},{7,6},{8,9},{9,8},{10,11... | collective-permute-start | bytes 12296 | tf_op jit(solution)/shard_map/ppermute | solution.py:589
  40.5 3.7 %collective-permute-start.18 = (f32[8,128]{1,0:T(8,128)S(1)}, f32[8,128]{1,0:T(8,128)S(1)}, u32[]{:S(2)}, u32[]{:S(2)}) collective-permute-start(f32[8,128]{1,0:T(8,128)S(1)} %add.15.rest_0_), channel_id=1, source_target_pairs={{0,16},{1,17},{2,18},{3,19},{4,20},{5,21},{6,22},{7,23},{8,24},{9,... | collective-permute-start | bytes 12296 | tf_op jit(solution)/shard_map/ppermute | solution.py:628
